TPU v7x, 32 devices: a whole 2x2x4 slice. The times are simulated.
32 devices in a mesh: groups: 2 (over y), seq: 4 (over z), res: 2 (over x), sub: 2 (over core).
Axes of the slice: x: 2, y: 2, z: 4, core: 2. Of those that a mesh axis runs over, the one named last changes fastest.
Arguments:
- alignment_input: bfloat16 [64, 512, 64], P(('groups', 'seq'), ('res', 'sub')), parts along dimension 0
- pair_features: bfloat16 [1024, 512, 128], P(('groups', 'seq'), ('res', 'sub')), parts along dimension 0
- update_cotangent: bfloat16 [64, 512, 64], P(('groups', 'seq'), ('res', 'sub')), parts along dimension 0, may hold values from -6 to 6
- alignment_norm_gain: bfloat16 [64], replicated, may hold values from 0.099609375 to 1.8984375
- pair_norm_gain: bfloat16 [128], replicated, may hold values from 0.099609375 to 1.8984375
- value_matrix: bfloat16 [64, 256], replicated, may hold values from -0.75 to 0.75
- gate_matrix: bfloat16 [64, 256], replicated, may hold values from -0.75 to 0.75
- output_matrix: bfloat16 [256, 64], replicated, may hold values from -0.375 to 0.375
- head_bias_matrix: bfloat16 [128, 8], replicated
- sequence_mask: int32 [64], P(('groups', 'seq')), parts along dimension 0, may hold values from 0 to 1, as said below
- token_padding_mask: int32 [1024], P(('groups', 'res', 'sub')), parts along dimension 0, may hold values from 0 to 1, as said below
Outputs:
- alignment_update: bfloat16 [64, 512, 64], P(('groups', 'seq'), ('res', 'sub')), parts along dimension 0
- alignment_gradient: bfloat16 [64, 512, 64], P(('groups', 'seq'), ('res', 'sub')), parts along dimension 0
- pair_gradient: bfloat16 [1024, 512, 128], P(('groups', 'seq'), ('res', 'sub')), parts along dimension 0
There are 2 independent parts, one for each index of `groups`. A program takes and returns all parts, laid end to end along the dimension named above; an argument that names none is the same for every part. Nothing has to cross between parts.
Inputs may be any that keep to these rules, and one draw needn't show every extreme that they name: `sequence_mask`: the first sequence is 1 and the last sequence is 0. `token_padding_mask`: 1 for the first tokens and 0 for all after them; at least the first half is 1 and the last token is 0.
All inputs are finite; a program needn't handle non-finite values.
Results may differ from a plain program's by a relative error of at most 0.014.
Values may be sent and summed in bfloat16 or wider, within the bound.
No kernel may reach another device: no remote copies, remote signals or barrier semaphores. Data moves between devices by JAX's collectives and lax.ppermute only.
A program may use at most 128 MiB of HBM per device.

v0:
```python
import jax
import jax.numpy as jnp
from jax import lax
from jax.sharding import PartitionSpec as P


def joined(value, axis, join):
    pieces = jax.tree.map(lambda part: lax.all_gather(part, axis), value)
    head = jax.tree.map(lambda part: part[0], pieces)
    tail = jax.tree.map(lambda part: part[1:], pieces)
    so_far, _ = lax.scan(lambda so_far, share: (join(so_far, share), None), head, tail)
    return so_far


def layer_normalize(inputs, gain):
    center = inputs - jnp.mean(inputs, axis=-1, keepdims=True)
    inverse = lax.rsqrt(jnp.mean(center * center, axis=-1, keepdims=True) + 1e-05)
    scaled = center * inverse
    return (scaled * gain, scaled, inverse)


def recover_normalized(scaled, inverse, gain, incoming):
    grads = incoming * gain
    mean_grad = jnp.mean(grads, axis=-1, keepdims=True)
    mean_cross = jnp.mean(grads * scaled, axis=-1, keepdims=True)
    return inverse * (grads - mean_grad - scaled * mean_cross)


def matrix_multiply(left_side, right_side):
    flat = left_side.reshape(-1, left_side.shape[-1])
    product = jnp.dot(flat, right_side, preferred_element_type=jnp.float32)
    return product.reshape(left_side.shape[:-1] + (right_side.shape[-1],))


def combine_stats(former, latter):
    highest = jnp.maximum(former[0], latter[0])
    return (
        highest,
        former[1] * jnp.exp(former[0] - highest) + latter[1] * jnp.exp(latter[0] - highest),
    )


def shards(
    alignment_input,
    pair_features,
    update_cotangent,
    alignment_norm_gain,
    pair_norm_gain,
    value_matrix,
    gate_matrix,
    output_matrix,
    head_bias_matrix,
    sequence_mask,
    token_padding_mask,
):
    sequence_count, column_count, alignment_width = alignment_input.shape
    head_count = head_bias_matrix.shape[1]
    hidden_width = value_matrix.shape[1]
    head_depth = hidden_width // head_count
    inner_width = sequence_count * head_depth
    normed_complete, alignment_scaled, alignment_inverse_deviation = layer_normalize(
        alignment_input.astype(jnp.float32), alignment_norm_gain.astype(jnp.float32)
    )
    normed_alignment = normed_complete.astype(jnp.bfloat16)
    value_rows = matrix_multiply(normed_alignment, value_matrix).astype(jnp.bfloat16)
    gate_activation = jax.nn.sigmoid(matrix_multiply(normed_alignment, gate_matrix))
    normed_pair, pair_scaled, pair_inverse = layer_normalize(
        pair_features.astype(jnp.float32), pair_norm_gain.astype(jnp.float32)
    )
    padding = 1000000000.0 * (token_padding_mask.astype(jnp.float32) - 1.0)
    logits = (
        jnp.einsum(
            "ijk,kh->hij",
            normed_pair,
            head_bias_matrix.astype(jnp.float32),
            precision=lax.Precision.HIGHEST,
        )
        + padding[None, None, :]
    )
    local_peak = jnp.max(logits, axis=-1)
    local_total = jnp.sum(jnp.exp(logits - local_peak[:, :, None]), axis=-1)
    row_peak, row_total = joined((local_peak, local_total), ("res", "sub"), combine_stats)
    probs = jnp.exp(logits - row_peak[:, :, None]) / row_total[:, :, None]
    weights = probs.astype(jnp.bfloat16)
    whole_weights = lax.all_gather(weights, "seq", axis=1, tiled=True)
    value_heads = (
        value_rows.reshape(sequence_count, column_count, head_count, head_depth)
        .transpose(2, 1, 0, 3)
        .reshape(head_count, column_count, inner_width)
    )
    own_rows = lax.all_to_all(
        whole_weights, ("res", "sub"), split_axis=1, concat_axis=2, tiled=True
    )
    mixed_heads = jnp.einsum(
        "hij,hjk->hik",
        own_rows,
        lax.all_gather(value_heads, ("res", "sub"), axis=1, tiled=True),
        preferred_element_type=jnp.float32,
    )
    mixed = (
        mixed_heads.reshape(head_count, column_count, sequence_count, head_depth)
        .transpose(2, 1, 0, 3)
        .reshape(sequence_count, column_count, hidden_width)
    )
    gated_output = (mixed * gate_activation).astype(jnp.bfloat16)
    active_entries = (sequence_mask[:, None] * token_padding_mask[None, :]).astype(jnp.float32)[
        :, :, None
    ]
    alignment_update = (matrix_multiply(gated_output, output_matrix) * active_entries).astype(
        jnp.bfloat16
    )
    upstream = (update_cotangent.astype(jnp.float32) * active_entries).astype(jnp.bfloat16)
    d_gated = matrix_multiply(upstream, output_matrix.T)
    d_mixed = (d_gated * gate_activation).astype(jnp.bfloat16)
    gating_gradient = (d_gated * mixed * gate_activation * (1.0 - gate_activation)).astype(
        jnp.bfloat16
    )
    grad_heads = (
        d_mixed.reshape(sequence_count, column_count, head_count, head_depth)
        .transpose(2, 1, 0, 3)
        .reshape(head_count, column_count, inner_width)
    )
    grad_piece = lax.all_gather(grad_heads, ("res", "sub"), axis=1, tiled=True)
    value_grads = jnp.einsum(
        "hij,hik->hjk", whole_weights, grad_piece, preferred_element_type=jnp.float32
    )
    score_rows = jnp.einsum(
        "hik,hjk->hij", grad_piece, value_heads, preferred_element_type=jnp.float32
    )
    score_grads = score_rows
    value_grads, score_grads = (value_grads, score_grads)
    score_sums = lax.psum_scatter(
        score_grads.astype(jnp.bfloat16), "seq", scatter_dimension=1, tiled=True
    ).astype(jnp.float32)
    row_weight = lax.psum(jnp.sum(probs * score_sums, axis=-1), ("res", "sub"))
    d_logits = probs * (score_sums - row_weight[:, :, None])
    d_normed_pair = jnp.einsum(
        "hij,kh->ijk",
        d_logits,
        head_bias_matrix.astype(jnp.float32),
        precision=lax.Precision.HIGHEST,
    )
    pair_gradient = recover_normalized(
        pair_scaled, pair_inverse, pair_norm_gain.astype(jnp.float32), d_normed_pair
    ).astype(jnp.bfloat16)
    value_gradient = (
        value_grads.reshape(head_count, column_count, sequence_count, head_depth)
        .transpose(2, 1, 0, 3)
        .reshape(sequence_count, column_count, hidden_width)
        .astype(jnp.bfloat16)
    )
    normed_alignment_gradient = matrix_multiply(value_gradient, value_matrix.T) + matrix_multiply(
        gating_gradient, gate_matrix.T
    )
    alignment_gradient = recover_normalized(
        alignment_scaled,
        alignment_inverse_deviation,
        alignment_norm_gain.astype(jnp.float32),
        normed_alignment_gradient,
    ).astype(jnp.bfloat16)
    return (alignment_update, alignment_gradient, pair_gradient)


def solution(mesh):
    placed = (
        P(("groups", "seq"), ("res", "sub"), None),
        P(("groups", "seq"), ("res", "sub"), None),
        P(("groups", "seq"), ("res", "sub"), None),
        P(),
        P(),
        P(),
        P(),
        P(),
        P(),
        P(("groups", "seq")),
        P(("groups", "res", "sub")),
    )
    return jax.shard_map(
        shards,
        mesh=mesh,
        in_specs=placed,
        out_specs=(
            P(("groups", "seq"), ("res", "sub"), None),
            P(("groups", "seq"), ("res", "sub"), None),
            P(("groups", "seq"), ("res", "sub"), None),
        ),
        check_vma=False,
    )
```

profile of v0, /device:TPU:0, one launch (start us, length us, event | category | flops | bytes accessed | tf_op | source)
XLA Modules:
  0.0 147.8 jit_solution(5288960442522409305)
XLA Ops:
  7.2 0.0 copy-start
  7.2 0.0 copy-start.3
  7.2 0.0 copy-start.8
  7.2 0.0 copy-start.4
  7.2 0.0 all-gather.10.cloned.1.call-start
  7.3 0.7 convert_element_type.84
  7.9 0.9 convert_reduce_fusion.1
  8.9 1.0 fusion.44
  9.9 0.7 multiply_convert_fusion.7
  10.6 1.4 fusion.19
  12.1 0.0 copy-done
  12.1 2.2 %multiply_convert_fusion.1 = (bf16[8,128,256]{2,1,0:T(8,128)(2,1)S(1)}, f32[8,128,256]{2,1,0:T(8,128)}) fusion(f32[8,128,256]{2,1,0:T(8,128)S(1)} %fusion.19, bf16[256,64]{0,1:T(8,128)(2,1)S(1)} %copy-done, bf16[8,128,64]{1,2,0:T(8,128)(2,1)} %param.15, f32[8,128]{1,0:T(8,128)S(1)} %multiply_convert_fusion.7), kind=kOutput, calls=%fused_computation.38 | convolution fusion | flops 34275328 | bytes 2789376 | tf_op jit(solution)/shard_map/dot_general | solution.py:31
  14.3 0.3 copy.115
  14.6 1.0 copy.117
  15.6 0.0 all-gather.10.cloned.1.call-update
  15.7 0.0 reduce-scatter.2.cloned.1.call-start
  15.7 0.0 copy-done.8
  15.7 0.0 copy-done.3
  15.7 0.0 copy-done.4
  15.8 0.4 convolution_convert_fusion.1
  16.2 0.3 copy.109
  16.5 6.4 %copy.102 = bf16[128,128,128]{1,2,0:T(8,128)(2,1)} copy(bf16[128,128,128]{2,1,0:T(8,128)(2,1)} %param.14) | data formatting | bytes 8388608 | tf_op args[1]
  22.9 3.6 %convert_reduce_fusion = f32[128,128]{1,0:T(8,128)S(1)} fusion(bf16[128,128,128]{1,2,0:T(8,128)(2,1)} %copy.102), kind=kLoop, calls=%fused_computation.6 | loop fusion | flops 4177920 | bytes 4259840 | tf_op jit(solution)/shard_map/reduce_sum | solution.py:16
  26.5 3.9 %fusion.13 = f32[128,128]{1,0:T(8,128)S(1)} fusion(bf16[128,128,128]{1,2,0:T(8,128)(2,1)} %copy.102, f32[128,128]{1,0:T(8,128)S(1)} %broadcast_multiply_fusion.2), kind=kLoop, calls=%fused_computation.17 | loop fusion | flops 8372224 | bytes 4325376 | tf_op jit(solution)/shard_map/reduce_sum | solution.py:17
  30.4 10.7 %all-gather.10.cloned.1.call-done = bf16[8,512,256]{2,1,0:T(8,128)(2,1)} async-done(((bf16[8,128,256]{2,1,0:T(8,128)(2,1)}), bf16[8,512,256]{2,1,0:T(8,128)(2,1)}) %all-gather.10.cloned.1.call-update) | async-done | bytes 2097168 | tf_op jit(solution)/shard_map/all_gather | solution.py:123
  41.1 2.3 %fusion.63 = bf16[8,512,128]{2,1,0:T(8,128)(2,1)S(1)} fusion(bf16[8,512,256]{2,1,0:T(8,128)(2,1)} %all-gather.10.cloned.1.call-done, bf16[8,128,256]{1,2,0:T(8,128)(2,1)S(1)} %bitcast.74), kind=kOutput, calls=%fused_computation.90 | convolution fusion | flops 268435456 | bytes 3670016 | tf_op jit(solution)/shard_map/hik,hjk->hij/dot_general | solution.py:127
  43.4 1.7 %copy.134 = bf16[8,512,128]{2,0,1:T(8,128)(2,1)} copy(bf16[8,512,128]{2,1,0:T(8,128)(2,1)S(1)} %fusion.63) | data formatting | bytes 2097152 | tf_op jit(solution)/shard_map/hik,hjk->hij/dot_general | solution.py:127
  45.1 0.0 reduce-scatter.2.cloned.1.call-update
  45.1 0.0 all-gather.6.cloned.1.call-start
  45.1 0.0 copy-done.6
  45.2 5.7 %fusion.61 = (f32[8,128]{0,1:T(8,128)S(1)}, f32[8,128,128]{2,0,1:T(8,128)S(1)}) fusion(f32[128]{0:T(128)S(1)} %add_multiply_fusion, bf16[128,8]{0,1:T(8,128)(2,1)S(1)} %copy-done.7, bf16[128,128,128]{1,2,0:T(8,128)(2,1)} %copy.102, f32[128]{0:T(128)S(1)} %convert_element_type.80, f32[128,128]{1,0:T(8,128)S(1)} %add_rsqrt_fusion, ...), kind=kOutput, calls=%fused_computation.88 | convolution fusion | flops 209976320 | bytes 4856832 | tf_op jit(solution)/shard_map/ijk,kh->hij/dot_general | solution.py:72
  51.0 0.4 exponential_reduce_fusion
  51.4 5.2 %all-gather.1 = f32[32,128]{1,0:T(8,128)S(1)} all-gather(f32[8,128]{1,0:T(8,128)S(1)} %copy.105), channel_id=3, replica_groups=mesh['groups'=2,'seq'=4,'res'=2,'sub'=2] {'res','sub'}, dimensions={0}, use_global_device_ids=true | all-gather | bytes 20480 | tf_op jit(solution)/shard_map/all_gather | solution.py:8
  56.6 5.2 %all-gather = f32[32,128]{1,0:T(8,128)S(1)} all-gather(f32[8,128]{1,0:T(8,128)S(1)} %copy.104), channel_id=2, replica_groups=mesh['groups'=2,'seq'=4,'res'=2,'sub'=2] {'res','sub'}, dimensions={0}, use_global_device_ids=true | all-gather | bytes 20480 | tf_op jit(solution)/shard_map/all_gather | solution.py:8
  61.8 0.1 while.12
  61.9 0.1 copy.107
  62.0 0.1 copy.106
  62.1 10.3 %reduce-scatter.2.cloned.1.call-done = bf16[8,128,128]{2,0,1:T(8,128)(2,1)} async-done(((bf16[8,512,128]{2,0,1:T(8,128)(2,1)}), bf16[8,128,128]{2,0,1:T(8,128)(2,1)}) %reduce-scatter.2.cloned.1.call-update) | async-done | bytes 262160 | tf_op jit(solution)/shard_map/reduce_scatter | solution.py:132
  72.4 2.0 %fusion.29 = (f32[8,128]{0,1:T(8,128)S(1)}, bf16[8,128,128]{2,0,1:T(8,128)(2,1)}) fusion(bf16[8,128,128]{2,0,1:T(8,128)(2,1)} %reduce-scatter.2.cloned.1.call-done, f32[8,128]{0,1:T(8,128)S(1)} %copy.107, f32[8,128,128]{2,0,1:T(8,128)S(1)} %get-tuple-element.79, f32[8,128]{0,1:T(8,128)S(1)} %copy.106), kind=kLoop, calls=%fused_computation.42 | loop fusion | flops 785408 | bytes 1060864 | tf_op jit(solution)/shard_map/reduce_sum | solution.py:135
  74.4 0.0 all-gather.6.cloned.1.call-update
  74.4 0.0 all-gather.8.cloned.1.call-start
  74.5 1.0 copy.111
  75.5 0.0 all-gather.8.cloned.1.call-update
  75.5 12.1 %psum.7 = f32[8,128]{0,1:T(8,128)S(1)} all-reduce(f32[8,128]{0,1:T(8,128)S(1)} %get-tuple-element.74), channel_id=1, replica_groups=mesh['groups'=2,'seq'=4,'res'=2,'sub'=2] {'res','sub'}, use_global_device_ids=true, to_apply=%region_12.13 | all-reduce | flops 1024 | bytes 8192 | tf_op jit(solution)/shard_map/psum | solution.py:135
  87.6 9.1 %multiply_reduce_fusion = (f32[128,128]{1,0:T(8,128)S(1)}, f32[128,128]{1,0:T(8,128)S(1)}, f32[128,128,128]{1,2,0:T(8,128)}) fusion(f32[128]{0:T(128)S(1)} %convert_element_type.80, f32[128,128]{1,0:T(8,128)S(1)} %add_rsqrt_fusion, f32[128,128]{1,0:T(8,128)S(1)} %broadcast_multiply_fusion.2, bf16[128,128,128]{1,2,0:T(8,128)(2,1)} %copy.102, ...), kind=kOutput, calls=%fused_computation.18 | convolution fusion | flops 216629248 | bytes 13646336 | tf_op jit(solution)/shard_map/hij,kh->ijk/dot_general | solution.py:137
  96.7 4.4 %all-gather.6.cloned.1.call-done = bf16[8,512,128]{2,0,1:T(8,128)(2,1)} async-done(((bf16[8,128,128]{2,0,1:T(8,128)(2,1)}), bf16[8,512,128]{2,0,1:T(8,128)(2,1)}) %all-gather.6.cloned.1.call-update) | async-done | bytes 1048592 | tf_op jit(solution)/shard_map/all_gather | solution.py:85
  101.2 4.3 %all-to-all-start = ((bf16[8,512,128]{2,0,1:T(8,128)(2,1)}), bf16[8,512,128]{2,0,1:T(8,128)(2,1)}, u32[]{:S(2)}, u32[]{:S(2)}) async-start(bf16[8,512,128]{2,0,1:T(8,128)(2,1)} %all-gather.6.cloned.1.call-done), calls=%async_computation | async-start | bytes 2097152 | tf_op jit(solution)/shard_map/all_to_all | solution.py:91
  105.4 7.7 %fusion.12 = bf16[128,128,128]{1,2,0:T(8,128)(2,1)} fusion(bf16[128,128,128]{1,2,0:T(8,128)(2,1)} %copy.102, f32[128,128,128]{1,2,0:T(8,128)} %get-tuple-element.81, f32[128,128]{1,0:T(8,128)S(1)} %get-tuple-element.84, f32[128,128]{1,0:T(8,128)S(1)} %get-tuple-element.85, f32[128]{0:T(128)S(1)} %convert_element_type.80, f32[128,128]{1,0:T(8,128)S(1)} %add_rsqrt_fusion, ...), kind=kLoop, calls=%fused_computation.16 | loop fusion | flops 18874368 | bytes 17039872 | tf_op jit(solution)/shard_map/convert_element_type | solution.py:145
  113.1 6.5 %copy.125 = bf16[128,128,128]{2,1,0:T(8,128)(2,1)} copy(bf16[128,128,128]{1,2,0:T(8,128)(2,1)} %fusion.12) | data formatting | bytes 8388608
  119.6 2.6 %convolution_convert_fusion = bf16[8,128,256]{2,1,0:T(8,128)(2,1)} fusion(bf16[8,512,256]{2,1,0:T(8,128)(2,1)S(1)} %copy-done.1, bf16[8,512,128]{2,0,1:T(8,128)(2,1)} %all-gather.6.cloned.1.call-done), kind=kOutput, calls=%fused_computation.27 | convolution fusion | flops 268697600 | bytes 3670016 | tf_op jit(solution)/shard_map/hij,hik->hjk/dot_general | solution.py:124
  122.2 1.4 copy.119
  123.6 0.8 copy.120
  124.4 3.7 %all-to-all-done = bf16[8,512,128]{2,0,1:T(8,128)(2,1)} async-done(((bf16[8,512,128]{2,0,1:T(8,128)(2,1)}), bf16[8,512,128]{2,0,1:T(8,128)(2,1)}, u32[]{:S(2)}, u32[]{:S(2)}) %all-to-all-start) | async-done | bytes 1048608 | tf_op jit(solution)/shard_map/all_to_all | solution.py:91
  128.1 2.0 %copy.135 = bf16[8,4,128,128]{3,1,2,0:T(4,128)(2,1)S(1)} copy(bf16[8,4,128,128]{3,0,2,1:T(8,128)(2,1)} %bitcast.6) | data formatting | bytes 2097152 | tf_op jit(solution)/shard_map/all_to_all | solution.py:91
  130.2 1.2 all_to_all.16
  131.4 1.2 all-gather.8.cloned.1.call-done
  132.6 2.7 %fusion.62 = f32[8,128,256]{1,2,0:T(8,128)S(1)} fusion(bf16[8,128,512]{2,1,0:T(8,128)(2,1)} %all_to_all.16, bf16[8,512,256]{2,1,0:T(8,128)(2,1)} %all-gather.8.cloned.1.call-done), kind=kOutput, calls=%fused_computation.89 | convolution fusion | flops 268435456 | bytes 4194304 | tf_op jit(solution)/shard_map/hij,hjk->hik/dot_general | solution.py:94
  135.3 1.1 copy.113
  136.4 1.6 %copy.114 = f32[8,128,256]{2,1,0:T(8,128)S(1)} copy(f32[8,128,256]{1,2,0:T(8,128)} %bitcast.77) | data formatting | bytes 2097152 | tf_op jit(solution)/shard_map/reshape | solution.py:103
  137.9 0.9 fusion.27
  138.9 0.0 copy-done.5
  138.9 0.3 fusion.33
  139.2 1.3 fusion.60
  140.5 0.7 fusion.43
  (27 shorter events, 0.3 us)
Async XLA Ops:
  7.2 4.9 %copy-start = (bf16[256,64]{0,1:T(8,128)(2,1)S(1)}, bf16[256,64]{0,1:T(8,128)(2,1)}, u32[]{:S(2)}) copy-start(bf16[256,64]{0,1:T(8,128)(2,1)} %param.20) | copy-start | bytes 98308
  7.2 8.6 %copy-start.3 = (bf16[8,128,64]{1,2,0:T(8,128)(2,1)S(1)}, bf16[8,128,64]{1,2,0:T(8,128)(2,1)}, u32[]{:S(2)}) copy-start(bf16[8,128,64]{1,2,0:T(8,128)(2,1)} %param.13) | copy-start | bytes 393220
  7.2 8.5 %copy-start.8 = (bf16[128]{0:T(256)(128)(2,1)S(1)}, bf16[128]{0:T(256)(128)(2,1)}, u32[]{:S(2)}) copy-start(bf16[128]{0:T(256)(128)(2,1)} %param.17) | copy-start | bytes 772
  7.2 8.5 %copy-start.4 = (bf16[64,256]{1,0:T(8,128)(2,1)S(1)}, bf16[64,256]{1,0:T(8,128)(2,1)}, u32[]{:S(2)}) copy-start(bf16[64,256]{1,0:T(8,128)(2,1)} %param.18) | copy-start | bytes 98308
  7.2 33.9 %all-gather.10.cloned.1.call-start = ((), (), s32[]{:S(2)}) async-start(), calls=%async_computation.4 | async-start | bytes 2621440 | tf_op jit(solution)/shard_map/all_gather | solution.py:123
  15.7 56.7 %reduce-scatter.2.cloned.1.call-start = ((), (), s32[]{:S(2)}) async-start(), calls=%async_computation.5 | async-start | bytes 1310720 | tf_op jit(solution)/shard_map/reduce_scatter | solution.py:132
  22.8 22.3 %copy-start.6 = (s32[128]{0:T(128)S(1)}, s32[128]{0:T(128)}, u32[]{:S(2)}) copy-start(s32[128]{0:T(128)} %param.23) | copy-start | bytes 1540
  22.9 22.3 %copy-start.7 = (bf16[128,8]{0,1:T(8,128)(2,1)S(1)}, bf16[128,8]{0,1:T(8,128)(2,1)}, u32[]{:S(2)}) copy-start(bf16[128,8]{0,1:T(8,128)(2,1)} %param.21) | copy-start | bytes 6148
  45.1 56.1 %all-gather.6.cloned.1.call-start = ((), (), s32[]{:S(2)}) async-start(), calls=%async_computation.2 | async-start | bytes 1310720 | tf_op jit(solution)/shard_map/all_gather | solution.py:85
  74.4 58.2 %all-gather.8.cloned.1.call-start = ((), (), s32[]{:S(2)}) async-start(), calls=%async_computation.3 | async-start | bytes 2621440 | tf_op jit(solution)/shard_map/all_gather | solution.py:97
  101.2 27.0 %all-to-all-start = ((bf16[8,512,128]{2,0,1:T(8,128)(2,1)}), bf16[8,512,128]{2,0,1:T(8,128)(2,1)}, u32[]{:S(2)}, u32[]{:S(2)}) async-start(bf16[8,512,128]{2,0,1:T(8,128)(2,1)} %all-gather.6.cloned.1.call-done), calls=%async_computation | async-start | bytes 2097152 | tf_op jit(solution)/shard_map/all_to_all | solution.py:91
  113.1 6.5 %copy-start.1 = (bf16[8,512,256]{2,1,0:T(8,128)(2,1)S(1)}, bf16[8,512,256]{2,1,0:T(8,128)(2,1)}, u32[]{:S(2)}) copy-start(bf16[8,512,256]{2,1,0:T(8,128)(2,1)} %all-gather.10.cloned.1.call-done) | copy-start | bytes 6291460
  122.2 16.7 %copy-start.2 = (f32[8,128,256]{2,1,0:T(8,128)S(1)}, f32[8,128,256]{2,1,0:T(8,128)}, u32[]{:S(2)}) copy-start(f32[8,128,256]{2,1,0:T(8,128)} %get-tuple-element.77) | copy-start | bytes 3145732
  122.2 16.7 %copy-start.5 = (bf16[64,256]{1,0:T(8,128)(2,1)S(1)}, bf16[64,256]{1,0:T(8,128)(2,1)}, u32[]{:S(2)}) copy-start(bf16[64,256]{1,0:T(8,128)(2,1)} %param.19) | copy-start | bytes 98308
Sparse Core Ops, SparseCore 0:
  15.8 25.2 all-gather.9
  45.2 27.1 reduce-scatter.1
  74.5 26.5 all-gather.5
  102.7 29.9 all-gather.7
where the time goes:
time: 149 us; the launch traced here: 148 us
  waiting for transfers between devices  30.4 us (20%)
  matrix products  29 us (19%)
  local copies, waits for them, and re-layouts  25.7 us (17%)
  blocking collectives  22.5 us (15%)
  other arithmetic  21.7 us (15%)
  between operations  14.1 us (9%)
  starting transfers between devices  4.42 us (3%)
    unnamed x20, local copies, waits for them, and re-layouts  12.9 us
    psum x1, blocking collectives, shards(): row_weight = lax.psum(jnp.sum(probs * score_sums, axis=-1), ('res', 'sub'))  12.1 us
    all_gather x1, waiting for transfers between devices, shards(): grad_piece = lax.all_gather(grad_heads, ('res', 'sub'), axis=1, tiled=True)  10.7 us
    all_gather x2, blocking collectives, joined(): pieces = jax.tree.map(lambda part: lax.all_gather(part, axis), value)  10.4 us
    reduce_scatter x1, waiting for transfers between devices, shards(): lax.psum_scatter(score_grads.astype(jnp.bfloat16), 'seq', scatter_dimensi...  10.3 us
    dot_general x1, matrix products, shards(): jnp.einsum('hij,kh->ijk', d_logits, head_bias_matrix.astype(jnp.float32),...  9.11 us
    convert_element_type x1, other arithmetic, shards(): pair_gradient = recover_normalized(pair_scaled, pair_inverse, pair_norm_g...  7.65 us
    dot_general x6, matrix products, matrix_multiply(): product = jnp.dot(flat, right_side, preferred_element_type=jnp.float32)  6.6 us
  transfers between devices with their start and end apart: 5, of which 5 were waited for; matrix products, arithmetic and copies ran while one was open for 35% of the time, Pallas kernels for 0%

commit v1 on v0

v1 whole, which is shorter than its diff:
```python
import functools

import jax
import jax.numpy as jnp
from jax import lax
from jax.experimental import pallas as pl
from jax.experimental.pallas import tpu as pltpu
from jax.sharding import PartitionSpec as P

F32 = jnp.float32
BF16 = jnp.bfloat16
EPS = 1e-05
QUAD = 4
GROUP = 4
SLOTS = 32
VMEM = 56 * 1024 * 1024


def dot(a, b):
    return jnp.dot(a, b, preferred_element_type=F32)


def dot_nt(a, b):
    return lax.dot_general(a, b, (((1,), (1,)), ((), ())), preferred_element_type=F32)


def dot_tn(a, b):
    return lax.dot_general(a, b, (((0,), (0,)), ((), ())), preferred_element_type=F32)


def iota(shape, dim):
    return lax.broadcasted_iota(jnp.int32, shape, dim)


def split3(value):
    high = value.astype(BF16).astype(F32)
    rest = value - high
    middle = rest.astype(BF16).astype(F32)
    return high, middle, rest - middle


def split2(value):
    high = value.astype(BF16)
    return high, (value - high.astype(F32)).astype(BF16)


def call(kernel, out_shape, name, scratch=(), flops=10_000_000, scalars=0, operands=(), grid=None, in_specs=None, out_specs=None):
    whole = pl.BlockSpec(memory_space=pltpu.VMEM)
    if in_specs is None:
        in_specs = [pl.BlockSpec(memory_space=pltpu.SMEM)] * scalars + [whole] * (len(operands) - scalars)
        out_specs = [whole] * len(out_shape)
    extra = {} if grid is None else {"grid": grid}
    moved = sum(o.size * o.dtype.itemsize for o in operands) + sum(
        o.size * o.dtype.itemsize for o in out_shape
    )
    return pl.pallas_call(
        kernel,
        out_shape=out_shape,
        in_specs=in_specs,
        out_specs=out_specs,
        scratch_shapes=list(scratch),
        compiler_params=pltpu.CompilerParams(vmem_limit_bytes=VMEM),
        cost_estimate=pl.CostEstimate(flops=flops, bytes_accessed=moved, transcendentals=0),
        name=name,
        **extra,
    )(*operands)


def shape(dims, dtype):
    return jax.ShapeDtypeStruct(tuple(dims), dtype)


def spread(matrix, channels, depth):
    hidden = matrix.shape[1]
    wide = hidden * QUAD
    row, col = iota((hidden, wide), 0), iota((hidden, wide), 1)
    pick = (row // depth == col // (depth * QUAD)) & (row % depth == col % depth)
    placed = dot(matrix, pick.astype(F32).astype(BF16))
    tall = jnp.concatenate([placed] * QUAD, axis=0)
    row, col = iota(tall.shape, 0), iota(tall.shape, 1)
    return jnp.where(row // channels == (col // depth) % QUAD, tall, 0.0).astype(BF16)


def weights_kernel(
    depth, value_ref, gate_ref, output_ref, bias_ref, gain_ref,
    spread_value, spread_gate, spread_output, moments, squares, centers, back,
):
    channels = value_ref.shape[0]
    spread_value[...] = spread(value_ref[...], channels, depth)
    spread_gate[...] = spread(gate_ref[...], channels, depth)
    spread_output[...] = spread(output_ref[...], channels, depth)
    scaled = bias_ref[...].astype(F32) * gain_ref[...].astype(F32)
    heads, width = scaled.shape
    total = jnp.sum(scaled, axis=1, keepdims=True)
    centers[...] = jnp.broadcast_to(total, (heads, width))
    high, middle, low = split3(scaled)
    tail = (SLOTS - 3 * heads, width)
    row = iota(tail, 0)
    slots = jnp.concatenate([high, middle, low, jnp.where(row < 4, 1.0, 0.0)], axis=0)
    square_slots = jnp.concatenate(
        [jnp.zeros((3 * heads, width), F32), jnp.where(row >= 4, 1.0, 0.0)], axis=0
    )

    def diagonal(tile):
        tall = jnp.concatenate([tile] * GROUP, axis=0)
        full = jnp.concatenate([tall] * GROUP, axis=1)
        row, col = iota(full.shape, 0), iota(full.shape, 1)
        return jnp.where(row // SLOTS == col // tile.shape[1], full, 0.0).astype(BF16)

    moments[...] = diagonal(slots)
    squares[...] = diagonal(square_slots)
    high, middle, _ = split3(scaled - total * (1.0 / width))
    left = jnp.concatenate([high, middle, high, jnp.where(row < 3, 1.0, 0.0)], axis=0)
    right = jnp.concatenate(
        [jnp.zeros((3 * heads, width), F32), jnp.where((row >= 3) & (row < 6), 1.0, 0.0)], axis=0
    )
    back[...] = diagonal(jnp.concatenate([left, right], axis=1))


def side_by_side(ref, pair, channels):
    col = iota((channels, 2 * channels), 1)
    row = iota((channels, 2 * channels), 0)
    first = (col == row).astype(F32).astype(BF16)
    second = (col == row + channels).astype(F32).astype(BF16)
    return dot(ref[2 * pair], first) + dot(ref[2 * pair + 1], second)


def averaging(channels):
    row, col = iota((2 * channels, 2 * channels), 0), iota((2 * channels, 2 * channels), 1)
    return jnp.where(row // channels == col // channels, 1.0 / channels, 0.0).astype(BF16)


def average(value, mean_matrix):
    high, low = split2(value)
    return dot(high, mean_matrix) + dot(low, mean_matrix)


def normalized(value, mean_matrix):
    center = value - dot(value.astype(BF16), mean_matrix)
    inverse = lax.rsqrt(average(center * center, mean_matrix) + EPS)
    return center * inverse, inverse


def column(row_value, lanes):
    return jnp.transpose(jnp.broadcast_to(row_value, (lanes, row_value.shape[1])))


def first_kernel(dims, place_ref, seq_mask_ref, x_ref, u_ref, gain_ref, token_ref, spread_out, *messages):
    Z, R, rows, ways, width, lanes = dims
    channels = x_ref.shape[2]
    mean_matrix = averaging(channels)
    live = column(token_ref[...].astype(F32), 2 * channels)
    gain = gain_ref[...].astype(F32)
    second_half = iota(live.shape, 1) >= channels
    normed, masked = [], []
    for pair in range(x_ref.shape[0] // 2):
        scaled, _ = normalized(side_by_side(x_ref, pair, channels), mean_matrix)
        normed.append((scaled * gain).astype(BF16))
        keep = jnp.where(second_half, seq_mask_ref[2 * pair + 1], seq_mask_ref[2 * pair]).astype(F32)
        masked.append((side_by_side(u_ref, pair, channels) * keep * live).astype(BF16))
    per = width // (2 * channels)
    normed = [jnp.concatenate(normed[x * per : (x + 1) * per], axis=1) for x in range(R)]
    masked = [jnp.concatenate(masked[x * per : (x + 1) * per], axis=1) for x in range(R)]
    for z in range(Z):
        for x in range(R):
            spread_out[z * R + x] = normed[x]
    turn = place_ref[0]
    for k, message in enumerate(messages):
        for e in range(ways):
            part, x = e // R, e % R

            @pl.when(lax.rem(turn + k, ways) == e)
            def _():
                message[0:rows] = normed[x][part * rows : (part + 1) * rows]
                message[rows : 2 * rows] = masked[x][part * rows : (part + 1) * rows]


def pair_kernel(heads, x_ref, moments, squares, centers, token_ref, e_ref, logit_ref, mean_ref, inverse_ref, scratch, stat):
    count, columns, width = x_ref.shape
    groups = count // GROUP
    x = x_ref[...].reshape(groups, GROUP, columns, width)
    parts, highs, lows = [], [], []
    for g in range(GROUP):
        part = x[:, g].reshape(groups * columns, width)
        value = part.astype(F32)
        high, low = split2(value * value)
        parts.append(part)
        highs.append(high)
        lows.append(low)
    both = squares[...]
    product = (
        dot_nt(jnp.concatenate(parts, axis=1), moments[...])
        + dot_nt(jnp.concatenate(highs, axis=1), both)
        + dot_nt(jnp.concatenate(lows, axis=1), both)
    )
    padding = 1000000000.0 * (token_ref[...].astype(F32) - 1.0)
    center = centers[...]
    for group in range(groups):
        turned = jnp.transpose(product[group * columns : (group + 1) * columns])
        for g in range(GROUP):
            i = group * GROUP + g
            base = g * SLOTS
            raw = (
                turned[base : base + heads]
                + turned[base + heads : base + 2 * heads]
                + turned[base + 2 * heads : base + 3 * heads]
            )
            total = turned[base + 3 * heads : base + 3 * heads + 1]
            square = turned[base + 3 * heads + 4 : base + 3 * heads + 5]
            mean = total * (1.0 / width)
            upper = total.astype(BF16).astype(F32)
            lower = total - upper
            spread_sum = (square - upper * upper * (1.0 / width)) - (
                2.0 * upper * lower + lower * lower
            ) * (1.0 / width)
            inverse = lax.rsqrt(jnp.maximum(spread_sum, 0.0) * (1.0 / width) + EPS)
            scratch[i * heads : (i + 1) * heads] = inverse * (raw - mean * center)
            mean_ref[i : i + 1] = mean
            inverse_ref[i : i + 1] = inverse
    lane = iota((count, columns), 1)
    stats = jnp.zeros((count, columns), F32)
    for h in range(heads):
        logit = scratch[pl.ds(h, count, stride=heads), :]
        logit_ref[h] = logit
        logit = logit + padding
        peak = jnp.max(logit, axis=1, keepdims=True)
        e = jnp.exp(logit - peak).astype(BF16)
        e_ref[h] = e
        total = jnp.sum(e.astype(F32), axis=1, keepdims=True)
        for t, part in enumerate(split3(peak)):
            stats = jnp.where(lane == t * heads + h, part, stats)
        for t, part in enumerate(split3(total)):
            stats = jnp.where(lane == (t + 3) * heads + h, part, stats)
    e_ref[heads] = stats.astype(BF16)


def joined_thirds(stats, heads):
    lanes = stats.shape[1]
    return (
        stats
        + pltpu.roll(stats, lanes - heads, 1)
        + pltpu.roll(stats, lanes - 2 * heads, 1)
    )


def quads_of(dims, place_ref, own, other, scratch):
    Z, R, rows, ways, width, lanes = dims
    core, slot = place_ref[1], place_ref[2]
    for plane in range(Z):
        half, n = plane // ways, plane % ways
        k = lax.rem(slot - n + ways, ways)
        for index in range(ways):
            for mine, refs in ((True, own), (False, other)):

                @pl.when((k == index) & ((core == half) if mine else (core != half)))
                def _():
                    scratch[plane] = refs[index][...]


def quad_rows(dims, scratch, quad, low):
    Z, R, rows, ways, width, lanes = dims
    per = lanes // width
    return jnp.concatenate(
        [scratch[quad * per + g, low : low + rows] for g in range(per)], axis=1
    )


def rows_kernel(dims, heads, place_ref, *refs):
    Z, R, rows, ways, width, lanes = dims
    refs = list(refs)
    own, refs = refs[:ways], refs[ways:]
    other, refs = refs[:ways], refs[ways:]
    exps, refs = refs[:R], refs[R:]
    far, refs = refs[:R], refs[R:]
    value_ref, gate_ref, output_ref = refs[:3]
    partial_out, mixed_grad, probs, scales, gathered, turned = refs[3:]
    columns = exps[0].shape[2]
    quads_of(dims, place_ref, own, other, gathered)
    x_place = place_ref[3]
    near = [joined_thirds(e[heads].astype(F32), heads) for e in exps]
    away = [joined_thirds(s[...].astype(F32), heads) for s in far]
    everything = near + away
    peak = functools.reduce(jnp.maximum, everything)
    total = 0.0
    for s in everything:
        total = total + jnp.exp(s - peak) * pltpu.roll(s, s.shape[1] - 3 * heads, 1)
    for r in range(R):
        scale = jnp.exp(near[r] - peak) / total
        scales[r] = scale
        at = pl.multiple_of(lax.rem(x_place + r, R) * columns, columns)
        for h in range(heads):
            weight = exps[r][h].astype(F32) * scale[:, h : h + 1]
            probs[h, :, pl.ds(at, columns)] = weight.astype(BF16)
    quads = Z * width // lanes
    step = value_ref.shape[1] // heads
    for q in range(quads):
        gate = jax.nn.sigmoid(dot(quad_rows(dims, gathered, q, 0), gate_ref[...]))
        grad = dot(quad_rows(dims, gathered, q, rows), output_ref[...])
        product = (gate * grad).astype(BF16)
        for h in range(heads):
            mixed_grad[h, :, q * step : (q + 1) * step] = product[:, h * step : (h + 1) * step]
    for h in range(heads):
        grads = dot_tn(probs[h], mixed_grad[h]).astype(BF16)
        for q in range(quads):
            turned[q, :, h * step : (h + 1) * step] = grads[:, q * step : (q + 1) * step]
    for q in range(quads):
        partial = dot_nt(turned[q], value_ref[...]).astype(BF16)
        per = lanes // width
        for g in range(per):
            for x in range(R):
                partial_out[(q * per + g) * R + x] = partial[
                    x * columns : (x + 1) * columns, g * width : (g + 1) * width
                ]


def scores_kernel(dims, heads, place_ref, x_ref, value_ref, mixed_grad, scales, *refs):
    Z, R, rows, ways, width, lanes = dims
    exps, refs = refs[:R], refs[R:]
    values, own_scores = refs[:2]
    messages = refs[2 : 1 + R]
    scratch = refs[1 + R]
    columns = exps[0].shape[2]
    x_place = place_ref[3]
    quads, per = Z * width // lanes, lanes // width
    step = value_ref.shape[1] // heads
    for q in range(quads):
        tokens = [
            jnp.concatenate([x_ref[(q * per + g) * R + x] for g in range(per)], axis=1)
            for x in range(R)
        ]
        product = dot(jnp.concatenate(tokens, axis=0), value_ref[...]).astype(BF16)
        for h in range(heads):
            values[h, :, q * step : (q + 1) * step] = product[:, h * step : (h + 1) * step]
    lane = iota((rows, columns), 1)
    sums = jnp.zeros((rows, columns), F32)
    for h in range(heads):
        scratch[...] = dot_nt(mixed_grad[h], values[h])
        total = 0.0
        for r in range(R):
            at = pl.multiple_of(lax.rem(x_place + r, R) * columns, columns)
            part = scratch[:, pl.ds(at, columns)]
            if r == 0:
                own_scores[h] = part
            else:
                part = part.astype(BF16)
                messages[r - 1][h] = part
                part = part.astype(F32)
            weight = exps[r][h].astype(F32) * scales[r][:, h : h + 1]
            total = total + jnp.sum(weight * part, axis=1, keepdims=True)
        for t, part in enumerate(split3(total)):
            sums = jnp.where(lane == t * heads + h, part, sums)
    for message in messages:
        message[heads] = sums.astype(BF16)


def mixed_kernel(dims, heads, place_ref, *refs):
    Z, R, rows, ways, width, lanes = dims
    own, refs = refs[:ways], refs[ways:]
    other, refs = refs[:ways], refs[ways:]
    values, probs, gate_ref, output_ref, keep, send, gathered, turned, sums = refs
    quads_of(dims, place_ref, own, other, gathered)
    quads, per = Z * width // lanes, lanes // width
    step = gate_ref.shape[1] // heads
    for h in range(heads):
        mixed = dot(probs[h], values[h])
        for q in range(quads):
            turned[q, :, h * step : (h + 1) * step] = mixed[:, q * step : (q + 1) * step]
    for q in range(quads):
        mixed = turned[q]
        gate = jax.nn.sigmoid(dot(quad_rows(dims, gathered, q, 0), gate_ref[...]))
        grad = dot(quad_rows(dims, gathered, q, rows), output_ref[...])
        gated = mixed * gate
        update = dot_nt(gated.astype(BF16), output_ref[...])
        gate_grad = (grad * gated * (1.0 - gate)).astype(BF16)
        through_gate = dot_nt(gate_grad, gate_ref[...])
        for g in range(per):
            sums[q * per + g, 0:rows] = update[:, g * width : (g + 1) * width]
            sums[q * per + g, rows : 2 * rows] = through_gate[:, g * width : (g + 1) * width]
    core = place_ref[1]
    keep[...] = sums[pl.ds(core * ways, ways)]
    send[...] = sums[pl.ds((1 - core) * ways, ways)].astype(BF16)


def reply_kernel(dims, place_ref, keep, received, *messages):
    Z, R, rows, ways, width, lanes = dims
    slot = place_ref[2]
    for k, message in enumerate(messages):
        n = lax.rem(slot - k + ways, ways)
        message[...] = (keep[n] + received[n].astype(F32)).astype(BF16)


def pair_back_kernel(R, heads, x_ref, logit_ref, mean_ref, inverse_ref, e_ref, scale_ref, own_ref, back_ref, *refs):
    received, refs = refs[: R - 1], refs[R - 1 :]
    totals, refs = refs[: R + 1], refs[R + 1 :]
    out_ref, scratch = refs
    count, columns, width = x_ref.shape
    total = sum(t[0].astype(F32) for t in totals) + sum(m[heads].astype(F32) for m in received)
    total = joined_thirds(total, heads)
    scale = scale_ref[0]
    inverse = inverse_ref[...]
    cross = 0.0
    for h in range(heads):
        scores = own_ref[h]
        for m in received:
            scores = scores + m[h].astype(F32)
        prob = e_ref[h].astype(F32) * scale[:, h : h + 1]
        grad = prob * (scores - total[:, h : h + 1])
        cross = cross + grad * logit_ref[h]
        scaled = grad * inverse
        high = scaled.astype(BF16).astype(F32)
        scratch[pl.ds(h, count, stride=SLOTS), :] = high
        scratch[pl.ds(heads + h, count, stride=SLOTS), :] = high
        scratch[pl.ds(2 * heads + h, count, stride=SLOTS), :] = scaled - high
    factor = inverse * inverse * cross * (1.0 / width)
    rest = list(split3(factor * mean_ref[...])) + list(split3(factor))
    rest += [jnp.zeros_like(factor)] * (SLOTS - 3 * heads - len(rest))
    for t, part in enumerate(rest):
        scratch[pl.ds(3 * heads + t, count, stride=SLOTS), :] = part
    back = back_ref[...]
    for group in range(count // GROUP):
        tile = scratch[group * GROUP * SLOTS : (group + 1) * GROUP * SLOTS]
        product = dot(jnp.transpose(tile).astype(BF16), back)
        for g in range(GROUP):
            i = group * GROUP + g
            plain = product[:, 2 * g * width : (2 * g + 1) * width]
            slope = product[:, (2 * g + 1) * width : (2 * g + 2) * width]
            out_ref[i] = (plain - slope * x_ref[i].astype(F32)).astype(BF16)


def last_kernel(dims, place_ref, seq_mask_ref, x_ref, gain_ref, token_ref, partial_ref, *refs):
    Z, R, rows, ways, width, lanes = dims
    messages, refs = refs[:ways], refs[ways:]
    update_ref, grad_ref, updates, through = refs
    channels = x_ref.shape[2]
    turn = place_ref[0]
    for k, message in enumerate(messages):
        for e in range(ways):
            part, x = e // R, e % R

            @pl.when(lax.rem(turn + k, ways) == e)
            def _():
                at = slice(part * rows, (part + 1) * rows), slice(x * width, (x + 1) * width)
                updates[at] = message[0:rows].astype(F32)
                through[at] = message[rows : 2 * rows].astype(F32)

    mean_matrix = averaging(channels)
    live = column(token_ref[...].astype(F32), 2 * channels)
    gain = gain_ref[...].astype(F32)
    second_half = iota(live.shape, 1) >= channels
    row, col = iota((2 * channels, channels), 0), iota((2 * channels, channels), 1)
    first = (row == col).astype(F32).astype(BF16)
    second = (row == col + channels).astype(F32).astype(BF16)
    for x in range(R):
        grads = through[:, x * width : (x + 1) * width]
        for z in range(Z):
            grads = grads + partial_ref[z * R + x].astype(F32)
        for p in range(width // (2 * channels)):
            pair = x * (width // (2 * channels)) + p
            at = slice(p * 2 * channels, (p + 1) * 2 * channels)
            scaled, inverse = normalized(side_by_side(x_ref, pair, channels), mean_matrix)
            grad = grads[:, at] * gain
            grad = inverse * (
                grad - average(grad, mean_matrix) - scaled * average(grad * scaled, mean_matrix)
            )
            grad = grad.astype(BF16)
            keep = jnp.where(second_half, seq_mask_ref[2 * pair + 1], seq_mask_ref[2 * pair]).astype(F32)
            update = updates[:, pair * 2 * channels : (pair + 1) * 2 * channels] * keep * live
            update = update.astype(BF16)
            for s, pick in enumerate((first, second)):
                grad_ref[2 * pair + s] = dot(grad, pick).astype(BF16)
                update_ref[2 * pair + s] = dot(update, pick).astype(BF16)


def shards(
    Z, R, C,
    alignment_input, pair_features, update_cotangent, alignment_norm_gain, pair_norm_gain,
    value_matrix, gate_matrix, output_matrix, head_bias_matrix, sequence_mask, token_padding_mask,
):
    sequences, columns, channels = alignment_input.shape
    rows, _, pair_width = pair_features.shape
    heads = head_bias_matrix.shape[1]
    hidden = value_matrix.shape[1]
    depth = hidden // heads
    ways = Z // C
    width = sequences // R * channels
    lanes = QUAD * channels
    step = QUAD * depth
    quads = Z * width // lanes
    dims = (Z, R, rows, ways, width, lanes)
    parts = columns // rows
    z, x, c = lax.axis_index("seq"), lax.axis_index("res"), lax.axis_index("sub")
    place = jnp.stack([z % ways, c, (z % parts) * R + x, x]).astype(jnp.int32)
    everyone = ("seq", "res", "sub")

    def device(z, x, c):
        return (z * R + x) * C + c

    def owner_moves(k):
        moves = []
        for plane in range(Z):
            for block in range(R * C):
                e = (plane % ways + k) % ways
                to = device(block * parts + e // R, e % R, plane // ways)
                moves.append((device(plane, block // C, block % C), to))
        return moves

    swap = [(i, C - 1 - i) for i in range(C)]

    def along_res(value, k):
        return lax.ppermute(value, "res", [((i + k) % R, i) for i in range(R)])

    other_core = lambda value: lax.ppermute(value, "sub", swap)

    gain2 = jnp.concatenate([alignment_norm_gain] * 2).reshape(1, 2 * channels)
    token_row = token_padding_mask.reshape(1, columns)
    message = shape((2 * rows, width), BF16)

    first = call(
        functools.partial(first_kernel, dims),
        [shape((Z * R, columns, width), BF16)] + [message] * ways,
        "first",
        scalars=2,
        operands=(place, sequence_mask, alignment_input, update_cotangent, gain2, token_row),
    )
    outgoing, to_rows = first[0], first[1:]
    own = [lax.ppermute(m, everyone, owner_moves(k)) for k, m in enumerate(to_rows)]
    everywhere = lax.all_to_all(outgoing, ("seq", "res"), 0, 0, tiled=True)
    other = [other_core(m) for m in own]

    spread_value, spread_gate, spread_output, moments, squares, centers, back = call(
        functools.partial(weights_kernel, depth),
        [shape((lanes, hidden * QUAD), BF16)] * 3
        + [shape((GROUP * SLOTS, GROUP * pair_width), BF16)] * 2
        + [shape((heads, pair_width), F32), shape((GROUP * SLOTS, 2 * GROUP * pair_width), BF16)],
        "weights",
        operands=(
            value_matrix, gate_matrix, output_matrix.T, head_bias_matrix.T,
            pair_norm_gain.reshape(1, pair_width),
        ),
    )

    block = min(32, rows)
    steps = rows // block
    whole = pl.BlockSpec(memory_space=pltpu.VMEM)
    by_row = lambda *tail: pl.BlockSpec((block, *tail), lambda i: (i,) + (0,) * len(tail))
    by_middle = lambda lead: pl.BlockSpec((lead, block, columns), lambda i: (0, i, 0))
    exps, logits, means, inverses = call(
        functools.partial(pair_kernel, heads),
        [
            shape((heads + 1, rows, columns), BF16),
            shape((heads, rows, columns), F32),
            shape((rows, columns), F32),
            shape((rows, columns), F32),
        ],
        "pair",
        operands=(pair_features, moments, squares, centers, token_row),
        scratch=[pltpu.VMEM((block * heads, columns), F32), pltpu.VMEM((block, columns), F32)],
        grid=(steps,),
        in_specs=[by_row(columns, pair_width)] + [whole] * 4,
        out_specs=[by_middle(heads + 1), by_middle(heads), by_row(columns), by_row(columns)],
    )
    exps = [exps] + [along_res(exps, k) for k in range(1, R)]
    far = [other_core(e[heads]) for e in exps]

    partial, mixed_grad, probs, scales = call(
        functools.partial(rows_kernel, dims, heads),
        [
            shape((Z * R, columns, width), BF16),
            shape((heads, rows, quads * step), BF16),
            shape((heads, rows, R * columns), BF16),
            shape((R, rows, columns), F32),
        ],
        "rows",
        scalars=1,
        operands=(place, *own, *other, *exps, *far, spread_value, spread_gate, spread_output),
        scratch=[
            pltpu.VMEM((Z, 2 * rows, width), BF16),
            pltpu.VMEM((quads, R * columns, heads * step), BF16),
        ],
    )
    collected = lax.all_to_all(partial, ("seq", "res"), 0, 0, tiled=True)

    values, own_scores, *score_messages = call(
        functools.partial(scores_kernel, dims, heads),
        [shape((heads, R * columns, quads * step), BF16), shape((heads, rows, columns), F32)]
        + [shape((heads + 1, rows, columns), BF16)] * (R - 1),
        "scores",
        scalars=1,
        operands=(place, everywhere, spread_value, mixed_grad, scales, *exps),
        scratch=[pltpu.VMEM((rows, R * columns), F32)],
    )
    scores = [along_res(m, R - r) for r, m in enumerate(score_messages, 1)]
    own_total = score_messages[0][heads:]
    totals = [own_total, other_core(own_total)] + [other_core(m[heads:]) for m in scores]

    keep, send = call(
        functools.partial(mixed_kernel, dims, heads),
        [shape((ways, 2 * rows, width), F32), shape((ways, 2 * rows, width), BF16)],
        "mixed",
        scalars=1,
        operands=(place, *own, *other, values, probs, spread_gate, spread_output),
        scratch=[
            pltpu.VMEM((Z, 2 * rows, width), BF16),
            pltpu.VMEM((quads, rows, heads * step), F32),
            pltpu.VMEM((Z, 2 * rows, width), F32),
        ],
    )
    replies = call(
        functools.partial(reply_kernel, dims),
        [message] * ways,
        "reply",
        scalars=1,
        operands=(place, keep, other_core(send)),
    )
    replies = [
        lax.ppermute(m, everyone, [(b, a) for a, b in owner_moves(k)]) for k, m in enumerate(replies)
    ]

    (pair_gradient,) = call(
        functools.partial(pair_back_kernel, R, heads),
        [shape(pair_features.shape, BF16)],
        "pair_back",
        operands=(
            pair_features, logits, means, inverses, exps[0], scales, own_scores, back, *scores, *totals,
        ),
        scratch=[pltpu.VMEM((block * SLOTS, columns), F32)],
        grid=(steps,),
        in_specs=[
            by_row(columns, pair_width), by_middle(heads), by_row(columns), by_row(columns),
            by_middle(heads + 1), by_middle(1), by_middle(heads), whole,
        ]
        + [by_middle(heads + 1)] * (R - 1)
        + [by_middle(1)] * (R + 1),
        out_specs=[by_row(columns, pair_width)],
    )
    alignment_update, alignment_gradient = call(
        functools.partial(last_kernel, dims),
        [shape(alignment_input.shape, BF16)] * 2,
        "last",
        scalars=2,
        operands=(place, sequence_mask, alignment_input, gain2, token_row, collected, *replies),
        scratch=[pltpu.VMEM((columns, R * width), F32), pltpu.VMEM((columns, R * width), F32)],
    )
    return alignment_update, alignment_gradient, pair_gradient


def solution(mesh):
    split = P(("groups", "seq"), ("res", "sub"), None)
    sizes = (mesh.shape["seq"], mesh.shape["res"], mesh.shape["sub"])
    return jax.shard_map(
        functools.partial(shards, *sizes),
        mesh=mesh,
        in_specs=(split, split, split, P(), P(), P(), P(), P(), P())
        + (P(("groups", "seq")), P(("groups", "res", "sub"))),
        out_specs=(split, split, split),
        check_vma=False,
    )
```

time: 149 us -> 98.5 us (0.66)
  Pallas kernels: 0 us -> 42.5 us
  starting transfers between devices: 4.42 us -> 39.3 us
  matrix products: 29 us -> 0 us
  waiting for transfers between devices: 30.4 us -> 2.05 us
  blocking collectives: 22.5 us -> 0 us
  other arithmetic: 21.7 us -> 1.94 us
  local copies, waits for them, and re-layouts: 25.7 us -> 11.1 us
  between operations: 14.1 us -> 0.77 us
    pallas_call x0 -> x9, Pallas kernels: none -> 42.5 us  [call(): pl.pallas_call(kernel, out_shape=out_shape, in_specs=in_specs, out_specs=...]
    dot_general x11 -> x0, matrix products: 29 us -> none  [the longest x1 9.11 us: shards(): jnp.einsum('hij,kh->ijk', d_logits, head_bias_matrix.astype(jnp.float32),...]
    ppermute x0 -> x13, starting transfers between devices: none -> 24.4 us  [the longest x7 10.8 us: shards(): other_core = lambda value: lax.ppermute(value, 'sub', swap)]
    all_gather x3 -> x0, waiting for transfers between devices: 16.3 us -> none  [the longest x1 10.7 us: shards(): grad_piece = lax.all_gather(grad_heads, ('res', 'sub'), axis=1, tiled=True)]
    psum x1 -> x0, blocking collectives: 12.1 us -> none  [shards(): row_weight = lax.psum(jnp.sum(probs * score_sums, axis=-1), ('res', 'sub'))]
    reduce_sum x6 -> x0, other arithmetic: 11.8 us -> none  [the longest x2 4.88 us: layer_normalize(): jnp.mean(center * center, axis=-1, keepdims=True) + 1e-05]
    all_to_all x1 -> x2, starting transfers between devices: 4.26 us -> 14.9 us  [the longest x1 7.53 us: shards(): collected = lax.all_to_all(partial, ('seq', 'res'), 0, 0, tiled=True)]
    all_gather x2 -> x0, blocking collectives: 10.4 us -> none  [joined(): pieces = jax.tree.map(lambda part: lax.all_gather(part, axis), value)]
  transfers between devices with their start and end apart: 5 -> 15, of which waited for: 5 -> 5; matrix products, arithmetic and copies ran while one was open for 35% -> 1% of each run, Pallas kernels for 0% -> 36%
where the time goes in v1:
time: 98.5 us; the launch traced here: 97.7 us
  Pallas kernels  42.5 us (43%)
  starting transfers between devices  39.3 us (40%)
  local copies, waits for them, and re-layouts  11.1 us (11%)
  waiting for transfers between devices  2.05 us (2%)
  other arithmetic  1.94 us (2%)
    pallas_call x9, Pallas kernels, call(): pl.pallas_call(kernel, out_shape=out_shape, in_specs=in_specs, out_specs=...  42.5 us
    ppermute x7, starting transfers between devices, shards(): other_core = lambda value: lax.ppermute(value, 'sub', swap)  10.8 us
    unnamed x42, local copies, waits for them, and re-layouts  10.3 us
    all_to_all x1, starting transfers between devices, shards(): collected = lax.all_to_all(partial, ('seq', 'res'), 0, 0, tiled=True)  7.53 us
    all_to_all x1, starting transfers between devices, shards(): everywhere = lax.all_to_all(outgoing, ('seq', 'res'), 0, 0, tiled=True)  7.38 us
    ppermute x2, starting transfers between devices, shards(): lax.ppermute(m, everyone, owner_moves(k))  5.78 us
    ppermute x2, starting transfers between devices, along_res(): return lax.ppermute(value, 'res', [((i + k) % R, i) for i in range(R)])  4.06 us
    ppermute x2, starting transfers between devices, shards(): lax.ppermute(m, everyone, [(b, a) for a, b in owner_moves(k)])  3.75 us
  transfers between devices with their start and end apart: 15, of which 5 were waited for; matrix products, arithmetic and copies ran while one was open for 1% of the time, Pallas kernels for 36%

profile of v1, /device:TPU:0, one launch (start us, length us, event | category | flops | bytes accessed | tf_op | source)
XLA Modules:
  0.0 97.7 jit_solution(13884502521172046985)
XLA Ops:
  0.6 1.3 %maximum_bitcast_fusion.gain_ref = bf16[1,128]{1,0:T(2,128)(2,1)} fusion(bf16[64]{0:T(256)(128)(2,1)} %param.14), kind=kLoop, calls=%fused_computation.3 | loop fusion | flops 512 | bytes 384 | tf_op jit(solution)/shard_map/reshape | solution.py:514
  1.9 1.8 %copy.16.x_ref = bf16[8,128,64]{2,1,0:T(8,128)(2,1)} copy(bf16[8,128,64]{1,2,0:T(8,128)(2,1)} %param.11) | data formatting | bytes 262144 | tf_op args[0]
  3.7 1.7 %copy.15.u_ref = bf16[8,128,64]{2,1,0:T(8,128)(2,1)} copy(bf16[8,128,64]{1,2,0:T(8,128)(2,1)} %param.13) | data formatting | bytes 262144 | tf_op args[2]
  5.4 0.7 pad_add_fusion.place_ref
  6.1 3.3 %first.1 = (bf16[8,128,256]{2,1,0:T(8,128)(2,1)}, bf16[256,256]{1,0:T(8,128)(2,1)}, bf16[256,256]{1,0:T(8,128)(2,1)}) custom-call(s32[4]{0:T(128)} %pad_add_fusion.place_ref, s32[8]{0:T(128)} %seq_mask_ref.3, bf16[8,128,64]{2,1,0:T(8,128)(2,1)} %copy.16.x_ref, bf16[8,128,64]{2,1,0:T(8,128)(2,1)} %copy.15.u_ref, bf16[1,128]{1,0:T(2,128)(2,1)} %maximum_bitcast_fusion.gain_ref, ...), custom_call_target="tpu_custom_call" | custom-call | flops 10000000 | bytes 1049392 | tf_op jit(solution)/shard_map/first/pallas_call | solution.py:56
  9.4 7.4 %all-to-all-start.1 = ((bf16[8,128,256]{2,1,0:T(8,128)(2,1)}), bf16[8,128,256]{2,1,0:T(8,128)(2,1)S(1)}, u32[]{:S(2)}, u32[]{:S(2)}) async-start(bf16[8,128,256]{2,1,0:T(8,128)(2,1)} %get-tuple-element.40), calls=%async_computation.1 | async-start | bytes 1048576 | tf_op jit(solution)/shard_map/all_to_all | solution.py:527
  16.8 2.4 %weights.1 = (bf16[256,1024]{1,0:T(8,128)(2,1)}, bf16[256,1024]{1,0:T(8,128)(2,1)}, bf16[256,1024]{1,0:T(8,128)(2,1)}, bf16[128,512]{1,0:T(8,128)(2,1)}, bf16[12...) custom-call(bf16[64,256]{1,0:T(8,128)(2,1)} %value_ref.1, bf16[64,256]{1,0:T(8,128)(2,1)} %gate_ref.1, ...), custom_call_target="tpu_custom_call" | custom-call | flops 10000000 | bytes 2201856 | tf_op jit(solution)/shard_map/weights/pallas_call | solution.py:56
  19.2 7.3 %pair.1 = (bf16[9,128,128]{2,1,0:T(8,128)(2,1)}, f32[8,128,128]{2,1,0:T(8,128)}, f32[128,128]{1,0:T(8,128)}, f32[128,128]{1,0:T(8,128)}) custom-call(bf16[128,128,128]{2,1,0:T(8,128)(2,1)} %x_ref.5, bf16[128,512]{1,0:T(8,128)(2,1)} %get-tuple-element.32.moments, bf16[128,512]{1,0:T(8,128)(2,1)} %get-tuple-element.33.squares, ...), custom_call_target="tpu_custom_call" | custom-call | flops 10000000 | bytes 5411328 | tf_op jit(solution)/shard_map/pair/pallas_call | solution.py:56
  26.5 2.0 %collective-permute-start.4 = (bf16[9,128,128]{2,1,0:T(8,128)(2,1)}, bf16[9,128,128]{2,1,0:T(8,128)(2,1)S(1)}, u32[]{:S(2)}, u32[]{:S(2)}) collective-permute-start(bf16[9,128,128]{2,1,0:T(8,128)(2,1)} %get-tuple-element.35.refs_4_.refs_0_.e_ref), channel_id=1, source_target_pairs={{2,0},{0,2},{3,1},{1,3},{6,4},{4,6},{7,5},{5,7},{10,8},{8,10},{11,... | collective-permute-start | bytes 884744 | tf_op jit(solution)/shard_map/ppermute | solution.py:510
  28.6 0.0 copy-done.18
  28.6 0.7 collective-permute-start
  29.3 0.0 copy-done.17
  29.3 5.1 %collective-permute-start.1 = (bf16[256,256]{1,0:T(8,128)(2,1)S(1)}, bf16[256,256]{1,0:T(8,128)(2,1)S(1)}, u32[]{:S(2)}, u32[]{:S(2)}) collective-permute-start(bf16[256,256]{1,0:T(8,128)(2,1)S(1)} %copy-done.17), channel_id=1, source_target_pairs={{0,2},{1,6},{2,10},{3,14},{4,0},{5,4},{6,8},{7,12},{8,3},{9,7},{10... | collective-permute-start | bytes 393224 | tf_op jit(solution)/shard_map/ppermute | solution.py:526
  34.4 0.8 slice_bitcast_fusion.1
  35.2 0.0 collective-permute-start.5
  35.2 0.0 collective-permute-done.refs_0_
  35.2 0.0 copy-start.3
  35.2 7.1 %collective-permute-start.2 = (bf16[256,256]{1,0:T(8,128)(2,1)S(1)}, bf16[256,256]{1,0:T(8,128)(2,1)S(1)}, u32[]{:S(2)}, u32[]{:S(2)}) collective-permute-start(bf16[256,256]{1,0:T(8,128)(2,1)S(1)} %collective-permute-done.refs_0_), channel_id=1, source_target_pairs={{0,1},{1,0},{2,3},{3,2},{4,5},{5,4},{6,7},{7,6},{8,9},{9,8},{10,11... | collective-permute-start | bytes 393224 | tf_op jit(solution)/shard_map/ppermute | solution.py:512
  42.3 0.0 collective-permute-done.1.refs_1_
  42.3 0.1 collective-permute-start.3
  42.4 0.0 collective-permute-done.4.refs_5_.refs_1_
  42.4 0.5 collective-permute-start.6
  42.9 0.0 collective-permute-done.5.refs_6_
  42.9 0.4 collective-permute-done.2.refs_2_
  43.3 0.4 collective-permute-done.3.refs_3_
  43.6 0.1 collective-permute-done.6.refs_7_
  43.7 0.0 copy-done.3
  43.7 0.0 copy-done.4
  43.7 0.1 copy-done.5
  43.9 0.4 copy-done.6
  44.3 0.0 copy-done.15
  44.3 4.9 %rows.1 = (bf16[8,128,256]{2,1,0:T(8,128)(2,1)}, bf16[8,128,512]{2,1,0:T(8,128)(2,1)}, bf16[8,128,256]{2,1,0:T(8,128)(2,1)}, f32[2,128,128]{2,1,0:T(8,128)}) custom-call(s32[4]{0:T(128)} %pad_add_fusion.place_ref, bf16[256,256]{1,0:T(8,128)(2,1)} %copy-done.3, bf16[256,256]{1,0:T(8,128)(2,1)} %copy-done.4, bf16[256,256]{1,0:T(8,128)(2,1)} %copy-done.5, ...), custom_call_target="tpu_custom_call" | custom-call | flops 10000000 | bytes 4980752 | tf_op jit(solution)/shard_map/rows/pallas_call | solution.py:56
  49.2 0.0 all-to-all-done.1.x_ref
  49.2 0.0 copy-start.1
  49.2 7.5 %all-to-all-start = ((bf16[8,128,256]{2,1,0:T(8,128)(2,1)}), bf16[8,128,256]{2,1,0:T(8,128)(2,1)S(1)}, u32[]{:S(2)}, u32[]{:S(2)}) async-start(bf16[8,128,256]{2,1,0:T(8,128)(2,1)} %get-tuple-element.39), calls=%async_computation | async-start | bytes 1048576 | tf_op jit(solution)/shard_map/all_to_all | solution.py:581
  56.7 0.0 copy-done.1
  56.7 4.2 %scores.1 = (bf16[8,256,512]{2,1,0:T(8,128)(2,1)}, f32[8,128,128]{2,1,0:T(8,128)}, bf16[9,128,128]{2,1,0:T(8,128)(2,1)}) custom-call(s32[4]{0:T(128)} %pad_add_fusion.place_ref, bf16[8,128,256]{2,1,0:T(8,128)(2,1)} %copy-done.1, bf16[256,1024]{1,0:T(8,128)(2,1)} %get-tuple-element.36.refs_8_.value_ref, bf16[8,128,512]{2,1,0:T(8,128)(2,1)} %get-tuple-element.41.mixed_grad, ...), custom_call_target="tpu_custom_call" | custom-call | flops 10000000 | bytes 5734416 | tf_op jit(solution)/shard_map/scores/pallas_call | solution.py:56
  60.9 5.6 %mixed.1 = (f32[2,256,256]{2,1,0:T(8,128)}, bf16[2,256,256]{2,1,0:T(8,128)(2,1)}) custom-call(s32[4]{0:T(128)} %pad_add_fusion.place_ref, bf16[256,256]{1,0:T(8,128)(2,1)} %copy-done.3, bf16[256,256]{1,0:T(8,128)(2,1)} %copy-done.4, bf16[256,256]{1,0:T(8,128)(2,1)} %copy-done.5, bf16[256,256]{1,0:T(8,128)(2,1)} %copy-done.6, ...), custom_call_target="tpu_custom_call" | custom-call | flops 10000000 | bytes 4980752 | tf_op jit(solution)/shard_map/mixed/pallas_call | solution.py:56
  66.5 0.1 collective-permute-start.7
  66.6 0.0 copy-done.16
  66.6 2.0 %collective-permute-start.10 = (bf16[9,128,128]{2,1,0:T(8,128)(2,1)S(1)}, bf16[9,128,128]{2,1,0:T(8,128)(2,1)S(1)}, u32[]{:S(2)}, u32[]{:S(2)}) collective-permute-start(bf16[9,128,128]{2,1,0:T(8,128)(2,1)S(1)} %copy-done.16), channel_id=1, source_target_pairs={{2,0},{0,2},{3,1},{1,3},{6,4},{4,6},{7,5},{5,7},{10,8},{8,10},{11,... | collective-permute-start | bytes 884744 | tf_op jit(solution)/shard_map/ppermute | solution.py:510
  68.6 0.0 collective-permute-done.7.received
  68.6 0.7 copy-done.8
  69.3 1.9 %reply.1 = (bf16[256,256]{1,0:T(8,128)(2,1)}, bf16[256,256]{1,0:T(8,128)(2,1)}) custom-call(s32[4]{0:T(128)} %pad_add_fusion.place_ref, f32[2,256,256]{2,1,0:T(8,128)} %get-tuple-element.45.keep, bf16[2,256,256]{2,1,0:T(8,128)(2,1)} %copy-done.8), custom_call_target="tpu_custom_call" | custom-call | flops 10000000 | bytes 1048592 | tf_op jit(solution)/shard_map/reply/pallas_call | solution.py:56
  71.2 1.6 %collective-permute-start.8 = (bf16[256,256]{1,0:T(8,128)(2,1)}, bf16[256,256]{1,0:T(8,128)(2,1)S(1)}, u32[]{:S(2)}, u32[]{:S(2)}) collective-permute-start(bf16[256,256]{1,0:T(8,128)(2,1)} %get-tuple-element.47), channel_id=1, source_target_pairs={{0,0},{4,1},{8,2},{12,3},{2,4},{6,5},{10,6},{14,7},{1,8},{5,9},{9,... | collective-permute-start | bytes 393224 | tf_op jit(solution)/shard_map/ppermute | solution.py:616
  72.7 2.2 %collective-permute-start.9 = (bf16[256,256]{1,0:T(8,128)(2,1)}, bf16[256,256]{1,0:T(8,128)(2,1)S(1)}, u32[]{:S(2)}, u32[]{:S(2)}) collective-permute-start(bf16[256,256]{1,0:T(8,128)(2,1)} %get-tuple-element.48), channel_id=1, source_target_pairs={{2,0},{6,1},{10,2},{14,3},{0,4},{4,5},{8,6},{12,7},{3,8},{7,9},{11... | collective-permute-start | bytes 393224 | tf_op jit(solution)/shard_map/ppermute | solution.py:616
  74.9 3.0 %collective-permute-start.11 = (bf16[1,128,128]{2,1,0:T(8,128)(2,1)S(1)}, bf16[1,128,128]{2,1,0:T(8,128)(2,1)S(1)}, u32[]{:S(2)}, u32[]{:S(2)}) collective-permute-start(bf16[1,128,128]{2,1,0:T(8,128)(2,1)S(1)} %slice.14.refs_1_), channel_id=1, source_target_pairs={{0,1},{1,0},{2,3},{3,2},{4,5},{5,4},{6,7},{7,6},{8,9},{9,8},{10,11... | collective-permute-start | bytes 98312 | tf_op jit(solution)/shard_map/ppermute | solution.py:512
  77.9 0.0 collective-permute-done.10.refs_0_
  77.9 0.1 collective-permute-start.12
  78.0 0.8 collective-permute-done.11.refs_2_
  78.8 0.4 collective-permute-done.12.refs_3_
  79.2 0.2 copy-done.13
  79.4 0.4 copy-done.14
  79.8 8.4 %pair_back.1 = bf16[128,128,128]{2,1,0:T(8,128)(2,1)} custom-call(bf16[128,128,128]{2,1,0:T(8,128)(2,1)} %x_ref.5, f32[8,128,128]{2,1,0:T(8,128)} %get-tuple-element.51.logit_ref, f32[128,128]{1,0:T(8,128)} %get-tuple-element.52.mean_ref, f32[128,128]{1,0:T(8,128)} %get-tuple-element.53.inverse_ref, ...), custom_call_target="tpu_custom_call" | custom-call | flops 10000000 | bytes 10649600 | tf_op jit(solution)/shard_map/pair_back/pallas_call | solution.py:56
  88.2 0.0 all-to-all-done.partial_ref
  88.2 0.0 collective-permute-done.8.refs_0_
  88.2 0.0 copy-start.10
  88.3 0.0 collective-permute-done.9.refs_1_
  88.3 0.7 copy-done
  89.0 0.0 copy-done.10
  89.0 0.7 copy-done.11
  89.7 4.5 %last.1 = (bf16[8,128,64]{2,1,0:T(8,128)(2,1)}, bf16[8,128,64]{2,1,0:T(8,128)(2,1)}) custom-call(s32[4]{0:T(128)} %pad_add_fusion.place_ref, s32[8]{0:T(128)} %seq_mask_ref.3, bf16[8,128,64]{2,1,0:T(8,128)(2,1)} %copy.16.x_ref, bf16[1,128]{1,0:T(2,128)(2,1)} %maximum_bitcast_fusion.gain_ref, s32[1,128]{1,0:T(1,128)} %bitcast.16, ...), custom_call_target="tpu_custom_call" | custom-call | flops 10000000 | bytes 1180464 | tf_op jit(solution)/shard_map/last/pallas_call | solution.py:56
  94.2 1.7 %copy.17 = bf16[8,128,64]{1,2,0:T(8,128)(2,1)} copy(bf16[8,128,64]{2,1,0:T(8,128)(2,1)} %get-tuple-element.57) | data formatting | bytes 262144
  95.9 1.7 %copy.18 = bf16[8,128,64]{1,2,0:T(8,128)(2,1)} copy(bf16[8,128,64]{2,1,0:T(8,128)(2,1)} %get-tuple-element.58) | data formatting | bytes 262144
  (23 shorter events, 0.0 us)
Async XLA Ops:
  9.4 19.2 %copy-start.18 = (bf16[256,256]{1,0:T(8,128)(2,1)S(1)}, bf16[256,256]{1,0:T(8,128)(2,1)}, u32[]{:S(2)}) copy-start(bf16[256,256]{1,0:T(8,128)(2,1)} %get-tuple-element.30) | copy-start | bytes 393220
  9.4 19.9 %copy-start.17 = (bf16[256,256]{1,0:T(8,128)(2,1)S(1)}, bf16[256,256]{1,0:T(8,128)(2,1)}, u32[]{:S(2)}) copy-start(bf16[256,256]{1,0:T(8,128)(2,1)} %get-tuple-element.31) | copy-start | bytes 393220
  9.4 39.8 %all-to-all-start.1 = ((bf16[8,128,256]{2,1,0:T(8,128)(2,1)}), bf16[8,128,256]{2,1,0:T(8,128)(2,1)S(1)}, u32[]{:S(2)}, u32[]{:S(2)}) async-start(bf16[8,128,256]{2,1,0:T(8,128)(2,1)} %get-tuple-element.40), calls=%async_computation.1 | async-start | bytes 1048576 | tf_op jit(solution)/shard_map/all_to_all | solution.py:527
  26.5 15.8 %collective-permute-start.4 = (bf16[9,128,128]{2,1,0:T(8,128)(2,1)}, bf16[9,128,128]{2,1,0:T(8,128)(2,1)S(1)}, u32[]{:S(2)}, u32[]{:S(2)}) collective-permute-start(bf16[9,128,128]{2,1,0:T(8,128)(2,1)} %get-tuple-element.35.refs_4_.refs_0_.e_ref), channel_id=1, source_target_pairs={{2,0},{0,2},{3,1},{1,3},{6,4},{4,6},{7,5},{5,7},{10,8},{8,10},{11,... | collective-permute-start | bytes 884744 | tf_op jit(solution)/shard_map/ppermute | solution.py:510
  28.6 6.6 %collective-permute-start = (bf16[256,256]{1,0:T(8,128)(2,1)S(1)}, bf16[256,256]{1,0:T(8,128)(2,1)S(1)}, u32[]{:S(2)}, u32[]{:S(2)}) collective-permute-start(bf16[256,256]{1,0:T(8,128)(2,1)S(1)} %copy-done.18), channel_id=1, source_target_pairs={{0,0},{1,4},{2,8},{3,12},{4,2},{5,6},{6,10},{7,14},{8,1},{9,5},{10... | collective-permute-start | bytes 393224 | tf_op jit(solution)/shard_map/ppermute | solution.py:526
  29.3 13.0 %collective-permute-start.1 = (bf16[256,256]{1,0:T(8,128)(2,1)S(1)}, bf16[256,256]{1,0:T(8,128)(2,1)S(1)}, u32[]{:S(2)}, u32[]{:S(2)}) collective-permute-start(bf16[256,256]{1,0:T(8,128)(2,1)S(1)} %copy-done.17), channel_id=1, source_target_pairs={{0,2},{1,6},{2,10},{3,14},{4,0},{5,4},{6,8},{7,12},{8,3},{9,7},{10... | collective-permute-start | bytes 393224 | tf_op jit(solution)/shard_map/ppermute | solution.py:526
  35.2 7.7 %collective-permute-start.5 = (bf16[128,128]{1,0:T(8,128)(2,1)S(1)}, bf16[128,128]{1,0:T(8,128)(2,1)S(1)}, u32[]{:S(2)}, u32[]{:S(2)}) collective-permute-start(bf16[128,128]{1,0:T(8,128)(2,1)S(1)} %slice_bitcast_fusion.1), channel_id=1, source_target_pairs={{0,1},{1,0},{2,3},{3,2},{4,5},{5,4},{6,7},{7,6},{8,9},{9,8},{10,11... | collective-permute-start | bytes 98312 | tf_op jit(solution)/shard_map/ppermute | solution.py:512
  35.2 8.6 %copy-start.3 = (bf16[256,256]{1,0:T(8,128)(2,1)}, bf16[256,256]{1,0:T(8,128)(2,1)S(1)}, u32[]{:S(2)}) copy-start(bf16[256,256]{1,0:T(8,128)(2,1)S(1)} %collective-permute-done.refs_0_) | copy-start | bytes 393220
  35.2 8.1 %collective-permute-start.2 = (bf16[256,256]{1,0:T(8,128)(2,1)S(1)}, bf16[256,256]{1,0:T(8,128)(2,1)S(1)}, u32[]{:S(2)}, u32[]{:S(2)}) collective-permute-start(bf16[256,256]{1,0:T(8,128)(2,1)S(1)} %collective-permute-done.refs_0_), channel_id=1, source_target_pairs={{0,1},{1,0},{2,3},{3,2},{4,5},{5,4},{6,7},{7,6},{8,9},{9,8},{10,11... | collective-permute-start | bytes 393224 | tf_op jit(solution)/shard_map/ppermute | solution.py:512
  42.3 1.5 %copy-start.4 = (bf16[256,256]{1,0:T(8,128)(2,1)}, bf16[256,256]{1,0:T(8,128)(2,1)S(1)}, u32[]{:S(2)}) copy-start(bf16[256,256]{1,0:T(8,128)(2,1)S(1)} %collective-permute-done.1.refs_1_) | copy-start | bytes 393220
  42.3 1.3 %collective-permute-start.3 = (bf16[256,256]{1,0:T(8,128)(2,1)S(1)}, bf16[256,256]{1,0:T(8,128)(2,1)S(1)}, u32[]{:S(2)}, u32[]{:S(2)}) collective-permute-start(bf16[256,256]{1,0:T(8,128)(2,1)S(1)} %collective-permute-done.1.refs_1_), channel_id=1, source_target_pairs={{0,1},{1,0},{2,3},{3,2},{4,5},{5,4},{6,7},{7,6},{8,9},{9,8},{10,11... | collective-permute-start | bytes 393224 | tf_op jit(solution)/shard_map/ppermute | solution.py:512
  42.4 1.4 %copy-start.2 = (bf16[9,128,128]{2,1,0:T(8,128)(2,1)}, bf16[9,128,128]{2,1,0:T(8,128)(2,1)S(1)}, u32[]{:S(2)}) copy-start(bf16[9,128,128]{2,1,0:T(8,128)(2,1)S(1)} %collective-permute-done.4.refs_5_.refs_1_) | copy-start | bytes 884740
  42.4 1.4 %collective-permute-start.6 = (bf16[128,128]{1,0:T(8,128)(2,1)S(1)}, bf16[128,128]{1,0:T(8,128)(2,1)S(1)}, u32[]{:S(2)}, u32[]{:S(2)}) collective-permute-start(bf16[128,128]{1,0:T(8,128)(2,1)S(1)} %slice_bitcast_fusion), channel_id=1, source_target_pairs={{0,1},{1,0},{2,3},{3,2},{4,5},{5,4},{6,7},{7,6},{8,9},{9,8},{10,11... | collective-permute-start | bytes 98312 | tf_op jit(solution)/shard_map/ppermute | solution.py:512
  42.9 0.9 copy-start.12
  43.3 0.6 copy-start.5
  43.6 0.7 copy-start.6
  43.7 0.6 copy-start.15
  49.2 7.5 %copy-start.1 = (bf16[8,128,256]{2,1,0:T(8,128)(2,1)}, bf16[8,128,256]{2,1,0:T(8,128)(2,1)S(1)}, u32[]{:S(2)}) copy-start(bf16[8,128,256]{2,1,0:T(8,128)(2,1)S(1)} %all-to-all-done.1.x_ref) | copy-start | bytes 1572868
  49.2 39.0 %all-to-all-start = ((bf16[8,128,256]{2,1,0:T(8,128)(2,1)}), bf16[8,128,256]{2,1,0:T(8,128)(2,1)S(1)}, u32[]{:S(2)}, u32[]{:S(2)}) async-start(bf16[8,128,256]{2,1,0:T(8,128)(2,1)} %get-tuple-element.39), calls=%async_computation | async-start | bytes 1048576 | tf_op jit(solution)/shard_map/all_to_all | solution.py:581
  60.9 5.7 %copy-start.16 = (bf16[9,128,128]{2,1,0:T(8,128)(2,1)S(1)}, bf16[9,128,128]{2,1,0:T(8,128)(2,1)}, u32[]{:S(2)}) copy-start(bf16[9,128,128]{2,1,0:T(8,128)(2,1)} %get-tuple-element.56) | copy-start | bytes 884740
  66.5 2.1 %collective-permute-start.7 = (bf16[2,256,256]{2,1,0:T(8,128)(2,1)}, bf16[2,256,256]{2,1,0:T(8,128)(2,1)S(1)}, u32[]{:S(2)}, u32[]{:S(2)}) collective-permute-start(bf16[2,256,256]{2,1,0:T(8,128)(2,1)} %get-tuple-element.46), channel_id=1, source_target_pairs={{0,1},{1,0},{2,3},{3,2},{4,5},{5,4},{6,7},{7,6},{8,9},{9,8},{10,11... | collective-permute-start | bytes 786440 | tf_op jit(solution)/shard_map/ppermute | solution.py:512
  66.6 11.3 %collective-permute-start.10 = (bf16[9,128,128]{2,1,0:T(8,128)(2,1)S(1)}, bf16[9,128,128]{2,1,0:T(8,128)(2,1)S(1)}, u32[]{:S(2)}, u32[]{:S(2)}) collective-permute-start(bf16[9,128,128]{2,1,0:T(8,128)(2,1)S(1)} %copy-done.16), channel_id=1, source_target_pairs={{2,0},{0,2},{3,1},{1,3},{6,4},{4,6},{7,5},{5,7},{10,8},{8,10},{11,... | collective-permute-start | bytes 884744 | tf_op jit(solution)/shard_map/ppermute | solution.py:510
  68.6 0.7 copy-start.8
  71.2 17.1 %collective-permute-start.8 = (bf16[256,256]{1,0:T(8,128)(2,1)}, bf16[256,256]{1,0:T(8,128)(2,1)S(1)}, u32[]{:S(2)}, u32[]{:S(2)}) collective-permute-start(bf16[256,256]{1,0:T(8,128)(2,1)} %get-tuple-element.47), channel_id=1, source_target_pairs={{0,0},{4,1},{8,2},{12,3},{2,4},{6,5},{10,6},{14,7},{1,8},{5,9},{9,... | collective-permute-start | bytes 393224 | tf_op jit(solution)/shard_map/ppermute | solution.py:616
  72.7 15.5 %collective-permute-start.9 = (bf16[256,256]{1,0:T(8,128)(2,1)}, bf16[256,256]{1,0:T(8,128)(2,1)S(1)}, u32[]{:S(2)}, u32[]{:S(2)}) collective-permute-start(bf16[256,256]{1,0:T(8,128)(2,1)} %get-tuple-element.48), channel_id=1, source_target_pairs={{2,0},{6,1},{10,2},{14,3},{0,4},{4,5},{8,6},{12,7},{3,8},{7,9},{11... | collective-permute-start | bytes 393224 | tf_op jit(solution)/shard_map/ppermute | solution.py:616
  74.9 4.3 %copy-start.9 = (bf16[1,128,128]{2,1,0:T(8,128)(2,1)}, bf16[1,128,128]{2,1,0:T(8,128)(2,1)S(1)}, u32[]{:S(2)}) copy-start(bf16[1,128,128]{2,1,0:T(8,128)(2,1)S(1)} %slice.14.refs_1_) | copy-start | bytes 98308
  74.9 3.9 %collective-permute-start.11 = (bf16[1,128,128]{2,1,0:T(8,128)(2,1)S(1)}, bf16[1,128,128]{2,1,0:T(8,128)(2,1)S(1)}, u32[]{:S(2)}, u32[]{:S(2)}) collective-permute-start(bf16[1,128,128]{2,1,0:T(8,128)(2,1)S(1)} %slice.14.refs_1_), channel_id=1, source_target_pairs={{0,1},{1,0},{2,3},{3,2},{4,5},{5,4},{6,7},{7,6},{8,9},{9,8},{10,11... | collective-permute-start | bytes 98312 | tf_op jit(solution)/shard_map/ppermute | solution.py:512
  77.9 1.3 %copy-start.7 = (bf16[9,128,128]{2,1,0:T(8,128)(2,1)}, bf16[9,128,128]{2,1,0:T(8,128)(2,1)S(1)}, u32[]{:S(2)}) copy-start(bf16[9,128,128]{2,1,0:T(8,128)(2,1)S(1)} %collective-permute-done.10.refs_0_) | copy-start | bytes 884740
  77.9 1.3 %collective-permute-start.12 = (bf16[1,128,128]{2,1,0:T(8,128)(2,1)S(1)}, bf16[1,128,128]{2,1,0:T(8,128)(2,1)S(1)}, u32[]{:S(2)}, u32[]{:S(2)}) collective-permute-start(bf16[1,128,128]{2,1,0:T(8,128)(2,1)S(1)} %slice.17), channel_id=1, source_target_pairs={{0,1},{1,0},{2,3},{3,2},{4,5},{5,4},{6,7},{7,6},{8,9},{9,8},{10,11... | collective-permute-start | bytes 98312 | tf_op jit(solution)/shard_map/ppermute | solution.py:512
  78.8 0.6 copy-start.13
  79.2 0.6 copy-start.14
  88.2 0.8 copy-start
  88.2 0.8 copy-start.10
  89.0 0.7 copy-start.11

commit v2 on v1

v2 whole, which is shorter than its diff:
```python
import functools

import jax
import jax.numpy as jnp
from jax import lax
from jax.experimental import pallas as pl
from jax.experimental.pallas import tpu as pltpu
from jax.sharding import PartitionSpec as P

F32 = jnp.float32
BF16 = jnp.bfloat16
EPS = 1e-05
QUAD = 4
GROUP = 4
SLOTS = 32
COST = dict(
    first=1.5, pack=0.4, weights=1.3, pair=6.5, pick=0.4, probs=0.8, work=4.0, scores=1.5, finish=0.6,
    pair_back=8.0, fold=0.6, last=2.7,
)
VMEM = 20 * 1024 * 1024


def dot(a, b):
    return jnp.dot(a, b, preferred_element_type=F32)


def dot_nt(a, b):
    return lax.dot_general(a, b, (((1,), (1,)), ((), ())), preferred_element_type=F32)


def dot_tn(a, b):
    return lax.dot_general(a, b, (((0,), (0,)), ((), ())), preferred_element_type=F32)


def iota(shape, dim):
    return lax.broadcasted_iota(jnp.int32, shape, dim)


def split3(value):
    high = value.astype(BF16).astype(F32)
    rest = value - high
    middle = rest.astype(BF16).astype(F32)
    return high, middle, rest - middle


def split2(value):
    high = value.astype(BF16)
    return high, (value - high.astype(F32)).astype(BF16)


def call(kernel, out_shape, name, scratch=(), flops=None, scalars=0, operands=(), grid=None, in_specs=None, out_specs=None):
    whole = pl.BlockSpec(memory_space=pltpu.VMEM)
    if in_specs is None:
        in_specs = [pl.BlockSpec(memory_space=pltpu.SMEM)] * scalars + [whole] * (len(operands) - scalars)
        out_specs = [whole] * len(out_shape)
    extra = {} if grid is None else {"grid": grid}
    moved = sum(o.size * o.dtype.itemsize for o in operands) + sum(
        o.size * o.dtype.itemsize for o in out_shape
    )
    return pl.pallas_call(
        kernel,
        out_shape=out_shape,
        in_specs=in_specs,
        out_specs=out_specs,
        scratch_shapes=list(scratch),
        compiler_params=pltpu.CompilerParams(vmem_limit_bytes=VMEM),
        cost_estimate=pl.CostEstimate(flops=int(COST[name] * 3e9), bytes_accessed=0, transcendentals=0),
        name=name,
        **extra,
    )(*operands)


def shape(dims, dtype):
    return jax.ShapeDtypeStruct(tuple(dims), dtype)


def spread(matrix, channels, depth):
    hidden = matrix.shape[1]
    wide = hidden * QUAD
    row, col = iota((hidden, wide), 0), iota((hidden, wide), 1)
    pick = (row // depth == col // (depth * QUAD)) & (row % depth == col % depth)
    placed = dot(matrix, pick.astype(F32).astype(BF16))
    tall = jnp.concatenate([placed] * QUAD, axis=0)
    row, col = iota(tall.shape, 0), iota(tall.shape, 1)
    return jnp.where(row // channels == (col // depth) % QUAD, tall, 0.0).astype(BF16)


def weights_kernel(
    depth, value_ref, gate_ref, output_ref, bias_ref, gain_ref,
    spread_value, spread_gate, spread_output, moments, squares, centers, back,
):
    channels = value_ref.shape[0]
    spread_value[...] = spread(value_ref[...], channels, depth)
    spread_gate[...] = spread(gate_ref[...], channels, depth)
    spread_output[...] = spread(output_ref[...], channels, depth)
    scaled = bias_ref[...].astype(F32) * gain_ref[...].astype(F32)
    heads, width = scaled.shape
    total = jnp.sum(scaled, axis=1, keepdims=True)
    centers[...] = jnp.broadcast_to(total, (heads, width))
    high, middle, low = split3(scaled)
    tail = (SLOTS - 3 * heads, width)
    row = iota(tail, 0)
    slots = jnp.concatenate([high, middle, low, jnp.where(row < 4, 1.0, 0.0)], axis=0)
    square_slots = jnp.concatenate(
        [jnp.zeros((3 * heads, width), F32), jnp.where(row >= 4, 1.0, 0.0)], axis=0
    )

    def diagonal(tile):
        tall = jnp.concatenate([tile] * GROUP, axis=0)
        full = jnp.concatenate([tall] * GROUP, axis=1)
        row, col = iota(full.shape, 0), iota(full.shape, 1)
        return jnp.where(row // SLOTS == col // tile.shape[1], full, 0.0).astype(BF16)

    moments[...] = diagonal(slots)
    squares[...] = diagonal(square_slots)
    high, middle, _ = split3(scaled - total * (1.0 / width))
    left = jnp.concatenate([high, middle, high, jnp.where(row < 3, 1.0, 0.0)], axis=0)
    right = jnp.concatenate(
        [jnp.zeros((3 * heads, width), F32), jnp.where((row >= 3) & (row < 6), 1.0, 0.0)], axis=0
    )
    back[...] = diagonal(jnp.concatenate([left, right], axis=1))


def side_by_side(ref, pair, channels):
    both = jnp.concatenate([ref[2 * pair], ref[2 * pair + 1]], axis=0)
    return jnp.transpose(both.astype(F32))


def averaging(channels):
    row, col = iota((2 * channels, 2 * channels), 0), iota((2 * channels, 2 * channels), 1)
    return jnp.where(row // channels == col // channels, 1.0 / channels, 0.0).astype(BF16)


def average(value, mean_matrix):
    high, low = split2(value)
    return dot(high, mean_matrix) + dot(low, mean_matrix)


def normalized(value, mean_matrix):
    center = value - dot(value.astype(BF16), mean_matrix)
    inverse = lax.rsqrt(average(center * center, mean_matrix) + EPS)
    return center * inverse, inverse


def column(row_value, lanes):
    return jnp.transpose(jnp.broadcast_to(row_value, (lanes, row_value.shape[1])))


def place_of(dims):
    return lax.axis_index("seq"), lax.axis_index("res"), lax.axis_index("sub")


def rows_place(dims):
    Z, R, C, rows, parts, width = dims
    z, x, c = place_of(dims)
    block = z // parts
    return c == lax.rem(block, C), x ^ (block // C), lax.rem(z, parts)


def first_kernel(dims, seq_mask_ref, x_ref, u_ref, gain_ref, token_ref, *shares):
    Z, R, C, rows, parts, width = dims
    channels, columns = x_ref.shape[1:]
    mean_matrix = averaging(channels)
    live = column(token_ref[...].astype(F32), 2 * channels)
    gain = jnp.concatenate([gain_ref[...].astype(F32)] * 2, axis=1)
    second_half = iota(live.shape, 1) >= channels
    normed, masked = [], []
    for pair in range(x_ref.shape[0] // 2):
        scaled, _ = normalized(side_by_side(x_ref, pair, channels), mean_matrix)
        normed.append((scaled * gain).astype(BF16))
        keep = jnp.where(second_half, seq_mask_ref[2 * pair + 1], seq_mask_ref[2 * pair]).astype(F32)
        masked.append((side_by_side(u_ref, pair, channels) * keep * live).astype(BF16))
    both = jnp.concatenate(
        [jnp.concatenate(normed, axis=1), jnp.concatenate(masked, axis=1)], axis=0
    )
    x = place_of(dims)[1]
    for b, share in enumerate(shares):
        for group in range(R):

            @pl.when(x ^ b == group)
            def _():
                share[...] = both[:, group * width : (group + 1) * width]


def pack_kernel(dims, slim, *refs):
    Z, R, C, rows, parts, width = dims
    held, messages = refs[:R], refs[R:]
    columns = held[0].shape[0] // 2
    for message in messages:
        for b in range(R):
            message[b * columns : (b + 1) * columns] = held[b][0:columns]
    if slim:
        near = rows_place(dims)[1]
        for far, message in enumerate(messages):
            for b in range(R):

                @pl.when(near ^ far == b)
                def _():
                    message[R * columns :] = held[b][columns:]
    else:
        for b in range(R):
            messages[0][(R + b) * columns : (R + b + 1) * columns] = held[b][columns:]


def pick_kernel(dims, slim, *refs):
    Z, R, C, rows, parts, width = dims
    messages, picked = refs[:-1], refs[-1]
    columns = messages[0].shape[0] // (R + 1 if slim else 2 * R)
    _, block, part = rows_place(dims)
    at = pl.multiple_of(block * columns + part * rows, rows)
    for n, message in enumerate(messages):
        picked[n, 0:rows] = message[pl.ds(at, rows)]
        picked[n, rows : 2 * rows] = message[R * columns :] if slim else message[pl.ds(R * columns + at, rows)]


def pair_kernel(heads, x_ref, moments, squares, centers, token_ref, e_ref, stat_ref, logit_ref, mean_ref, inverse_ref, scratch):
    count, columns, width = x_ref.shape
    groups = count // GROUP
    x = x_ref[...].reshape(groups, GROUP, columns, width)
    parts, highs, lows = [], [], []
    for g in range(GROUP):
        part = x[:, g].reshape(groups * columns, width)
        value = part.astype(F32)
        high, low = split2(value * value)
        parts.append(part)
        highs.append(high)
        lows.append(low)
    both = squares[...]
    product = (
        dot_nt(jnp.concatenate(parts, axis=1), moments[...])
        + dot_nt(jnp.concatenate(highs, axis=1), both)
        + dot_nt(jnp.concatenate(lows, axis=1), both)
    )
    padding = 1000000000.0 * (token_ref[...].astype(F32) - 1.0)
    center = centers[...]
    for group in range(groups):
        turned = jnp.transpose(product[group * columns : (group + 1) * columns])
        for g in range(GROUP):
            i = group * GROUP + g
            base = g * SLOTS
            raw = (
                turned[base : base + heads]
                + turned[base + heads : base + 2 * heads]
                + turned[base + 2 * heads : base + 3 * heads]
            )
            total = turned[base + 3 * heads : base + 3 * heads + 1]
            square = turned[base + 3 * heads + 4 : base + 3 * heads + 5]
            mean = total * (1.0 / width)
            upper = total.astype(BF16).astype(F32)
            lower = total - upper
            spread_sum = (square - upper * upper * (1.0 / width)) - (
                2.0 * upper * lower + lower * lower
            ) * (1.0 / width)
            inverse = lax.rsqrt(jnp.maximum(spread_sum, 0.0) * (1.0 / width) + EPS)
            scratch[i * heads : (i + 1) * heads] = inverse * (raw - mean * center)
            mean_ref[i : i + 1] = mean
            inverse_ref[i : i + 1] = inverse
    lane = iota((count, columns), 1)
    stats = jnp.zeros((count, columns), F32)
    for h in range(heads):
        logit = scratch[pl.ds(h, count, stride=heads), :]
        logit_ref[h] = logit
        logit = logit + padding
        peak = jnp.max(logit, axis=1, keepdims=True)
        e = jnp.exp(logit - peak).astype(BF16)
        e_ref[h] = e
        total = jnp.sum(e.astype(F32), axis=1, keepdims=True)
        for t, part in enumerate(split3(peak)):
            stats = jnp.where(lane == t * heads + h, part, stats)
        for t, part in enumerate(split3(total)):
            stats = jnp.where(lane == (t + 3) * heads + h, part, stats)
    stats = stats.astype(BF16)
    e_ref[heads] = stats
    stat_ref[...] = stats


def joined_thirds(stats, heads):
    lanes = stats.shape[1]
    return (
        stats
        + pltpu.roll(stats, lanes - heads, 1)
        + pltpu.roll(stats, lanes - 2 * heads, 1)
    )


def probs_kernel(R, heads, *refs):
    exps, far, (probs, scales) = refs[:R], refs[R : 2 * R], refs[2 * R :]
    columns = exps[0].shape[2]
    near = [joined_thirds(e[heads].astype(F32), heads) for e in exps]
    everything = near + [joined_thirds(s[...].astype(F32), heads) for s in far]
    peak = functools.reduce(jnp.maximum, everything)
    total = 0.0
    for s in everything:
        total = total + jnp.exp(s - peak) * pltpu.roll(s, s.shape[1] - 3 * heads, 1)
    for b in range(R):
        scale = jnp.exp(near[b] - peak) / total
        scales[b] = scale
        for h in range(heads):
            weight = exps[b][h].astype(F32) * scale[:, h : h + 1]
            probs[h, :, b * columns : (b + 1) * columns] = weight.astype(BF16)


def quad(refs, q, rows, lanes):
    per = max(lanes // refs[0].shape[-1], 1)
    return jnp.concatenate([refs[q * per + g][rows] for g in range(per)], axis=1)


def work_kernel(dims, heads, mine, other, *refs):
    Z, R, C, rows, parts, width = dims
    n = mine.shape[0]
    messages, refs = refs[:n], refs[n:]
    probs, value_ref, gate_ref, output_ref, *refs = refs
    values, mixed_grad, keep, send, partial, gathered, gates, grads, turned = refs
    columns = probs.shape[2] // R
    lanes, step = value_ref.shape[0], value_ref.shape[1] // heads
    quads = n * width // lanes
    per = n // quads
    here, _, _ = rows_place(dims)

    @pl.when(here)
    def _():
        gathered[...] = mine[...]

    @pl.when(jnp.logical_not(here))
    def _():
        gathered[...] = other[...]

    planes = [gathered.at[a] for a in range(n)]
    for q in range(quads):
        at = slice(q * step, (q + 1) * step)
        gate = jax.nn.sigmoid(dot(quad(planes, q, slice(0, rows), lanes), gate_ref[...]))
        grad = dot(quad(planes, q, slice(rows, 2 * rows), lanes), output_ref[...])
        product = (gate * grad).astype(BF16)
        gates[q] = gate
        grads[q] = grad
        tokens = dot(quad(messages, q, slice(0, R * columns), lanes), value_ref[...]).astype(BF16)
        for h in range(heads):
            mixed_grad[h, :, at] = product[:, h * step : (h + 1) * step]
            values[h, :, at] = tokens[:, h * step : (h + 1) * step]
    for h in range(heads):
        sums = dot_tn(probs[h], mixed_grad[h]).astype(BF16)
        for q in range(quads):
            turned[q, :, h * step : (h + 1) * step] = sums[:, q * step : (q + 1) * step]
    for q in range(quads):
        sums = dot_nt(turned[q], value_ref[...])
        for g in range(per):
            partial[q * per + g] = sums[:, g * width : (g + 1) * width]
    for q in range(quads):
        at = slice(q * step, (q + 1) * step)
        gate, grad = gates[q], grads[q]
        mixed = jnp.concatenate([dot(probs[h], values[h, :, at]) for h in range(heads)], axis=1)
        gated = mixed * gate
        gate_grad = (grad * gated * (1.0 - gate)).astype(BF16)
        update = dot_nt(gated.astype(BF16), output_ref[...])
        through = dot_nt(gate_grad, gate_ref[...])
        for g in range(per):
            for low, value in ((0, update), (rows, through)):
                value = value[:, g * width : (g + 1) * width]
                keep[q * per + g, low : low + rows] = value
                send[q * per + g, low : low + rows] = value.astype(BF16)


def finish_kernel(dims, keep, received, partial, *messages):
    Z, R, C, rows, parts, width = dims
    n, tall, _ = partial.shape
    here, block, part = rows_place(dims)
    at = pl.multiple_of(block * (tall // R) + part * rows, rows)
    for a, message in enumerate(messages):
        message[0:tall] = partial[a].astype(BF16)

        @pl.when(here)
        def _():
            both = keep[a] + received[a].astype(F32)
            message[tall:] = both[0:rows].astype(BF16)
            message[pl.ds(at, rows)] = (partial[a, pl.ds(at, rows)] + both[rows:]).astype(BF16)


def scores_kernel(R, heads, count, *refs):
    mixed_grads, refs = refs[:count], refs[count:]
    values, refs = refs[:count], refs[count:]
    scales, *refs = refs
    exps, refs = refs[:R], refs[R:]
    own_scores, total_ref, *messages = refs
    rows, columns = exps[0].shape[1:]
    lane = iota((rows, columns), 1)
    sums = jnp.zeros((rows, columns), F32)
    for h in range(heads):
        scores = sum(dot_nt(g[h], v[h]) for g, v in zip(mixed_grads, values))
        total = 0.0
        for b in range(R):
            part = scores[:, b * columns : (b + 1) * columns]
            if b == 0:
                own_scores[h] = part
            else:
                part = part.astype(BF16)
                messages[b - 1][h] = part
                part = part.astype(F32)
            weight = exps[b][h].astype(F32) * scales[b][:, h : h + 1]
            total = total + jnp.sum(weight * part, axis=1, keepdims=True)
        for t, part in enumerate(split3(total)):
            sums = jnp.where(lane == t * heads + h, part, sums)
    sums = sums.astype(BF16)
    total_ref[...] = sums
    for message in messages:
        message[heads] = sums


def pair_back_kernel(R, heads, x_ref, logit_ref, mean_ref, inverse_ref, e_ref, scale_ref, own_ref, back_ref, *refs):
    received, refs = refs[: R - 1], refs[R - 1 :]
    totals, refs = refs[: R + 1], refs[R + 1 :]
    out_ref, scratch = refs
    count, columns, width = x_ref.shape
    total = sum(t[...].astype(F32) for t in totals) + sum(m[heads].astype(F32) for m in received)
    total = joined_thirds(total, heads)
    scale = scale_ref[0]
    inverse = inverse_ref[...]
    cross = 0.0
    for h in range(heads):
        scores = own_ref[h]
        for m in received:
            scores = scores + m[h].astype(F32)
        prob = e_ref[h].astype(F32) * scale[:, h : h + 1]
        grad = prob * (scores - total[:, h : h + 1])
        cross = cross + grad * logit_ref[h]
        scaled = grad * inverse
        high = scaled.astype(BF16).astype(F32)
        scratch[pl.ds(h, count, stride=SLOTS), :] = high
        scratch[pl.ds(heads + h, count, stride=SLOTS), :] = high
        scratch[pl.ds(2 * heads + h, count, stride=SLOTS), :] = scaled - high
    factor = inverse * inverse * cross * (1.0 / width)
    rest = list(split3(factor * mean_ref[...])) + list(split3(factor))
    rest += [jnp.zeros_like(factor)] * (SLOTS - 3 * heads - len(rest))
    for t, part in enumerate(rest):
        scratch[pl.ds(3 * heads + t, count, stride=SLOTS), :] = part
    back = back_ref[...]
    for group in range(count // GROUP):
        tile = scratch[group * GROUP * SLOTS : (group + 1) * GROUP * SLOTS]
        product = dot(jnp.transpose(tile).astype(BF16), back)
        for g in range(GROUP):
            i = group * GROUP + g
            plain = product[:, 2 * g * width : (2 * g + 1) * width]
            slope = product[:, (2 * g + 1) * width : (2 * g + 2) * width]
            out_ref[i] = (plain - slope * x_ref[i].astype(F32)).astype(BF16)


def fold_kernel(dims, *refs):
    Z, R, C, rows, parts, width = dims
    messages, shares = refs[:Z], refs[Z:]
    columns = shares[0].shape[0] // 2
    z, x, c = place_of(dims)
    for b, share in enumerate(shares):
        at = slice(b * columns, (b + 1) * columns)
        share[0:columns] = sum(m[at].astype(F32) for m in messages).astype(BF16)
        for part in range(parts):
            plane = ((x ^ b) * C + c) * parts + part
            for a, message in enumerate(messages):

                @pl.when(plane ^ z == a)
                def _():
                    share[columns + part * rows : columns + (part + 1) * rows] = message[R * columns :]


def last_kernel(dims, seq_mask_ref, x_ref, gain_ref, token_ref, *refs):
    Z, R, C, rows, parts, width = dims
    shares, refs = refs[:R], refs[R:]
    update_ref, grad_ref, updates, through = refs
    channels, columns = x_ref.shape[1:]
    x = place_of(dims)[1]
    for b, share in enumerate(shares):
        at = pl.multiple_of((x ^ b) * width, width)
        through[:, pl.ds(at, width)] = share[0:columns].astype(F32)
        updates[:, pl.ds(at, width)] = share[columns:].astype(F32)

    mean_matrix = averaging(channels)
    live = column(token_ref[...].astype(F32), 2 * channels)
    gain = jnp.concatenate([gain_ref[...].astype(F32)] * 2, axis=1)
    second_half = iota(live.shape, 1) >= channels
    for pair in range(x_ref.shape[0] // 2):
        at = slice(pair * 2 * channels, (pair + 1) * 2 * channels)
        grad = through[:, at] * gain
        scaled, inverse = normalized(side_by_side(x_ref, pair, channels), mean_matrix)
        grad = inverse * (
            grad - average(grad, mean_matrix) - scaled * average(grad * scaled, mean_matrix)
        )
        grad = jnp.transpose(grad).astype(BF16)
        keep = jnp.where(second_half, seq_mask_ref[2 * pair + 1], seq_mask_ref[2 * pair]).astype(F32)
        update = jnp.transpose(updates[:, at] * keep * live).astype(BF16)
        for s in range(2):
            at = slice(s * channels, (s + 1) * channels)
            grad_ref[2 * pair + s] = grad[at]
            update_ref[2 * pair + s] = update[at]


def shards(
    Z, R, C,
    alignment_input, pair_features, update_cotangent, alignment_norm_gain, pair_norm_gain,
    value_matrix, gate_matrix, output_matrix, head_bias_matrix, sequence_mask, token_padding_mask,
):
    sequences, columns, channels = alignment_input.shape
    rows, _, pair_width = pair_features.shape
    heads = head_bias_matrix.shape[1]
    hidden = value_matrix.shape[1]
    depth = hidden // heads
    parts = columns // rows
    width = sequences // R * channels
    lanes = QUAD * channels
    step = QUAD * depth
    dims = (Z, R, C, rows, parts, width)
    slim = (Z, R, C, parts) == (4, 2, 2, 1)
    everyone = ("seq", "res", "sub")

    def exchange(value, dz=0, dx=0, dc=0):
        at = lambda z, x, c: (z * R + x) * C + c
        places = [(z, x, c) for z in range(Z) for x in range(R) for c in range(C)]
        return lax.ppermute(value, everyone, [(at(z, x, c), at(z ^ dz, x ^ dx, c ^ dc)) for z, x, c in places])

    in_hbm = lambda value: pltpu.with_memory_space_constraint(value, pltpu.HBM)

    gain = in_hbm(alignment_norm_gain.reshape(1, channels))
    by_channel = lambda value: jnp.swapaxes(value, 1, 2)
    alignment_turned = in_hbm(by_channel(alignment_input))
    token_row = in_hbm(token_padding_mask.reshape(1, columns))
    seq_mask = sequence_mask
    pair_input = in_hbm(pair_features)
    share = shape((2 * columns, width), BF16)

    held = call(
        functools.partial(first_kernel, dims),
        [share] * R,
        "first",
        scalars=1,
        operands=(seq_mask, alignment_turned, in_hbm(by_channel(update_cotangent)), gain, token_row),
    )
    held = [held[0]] + [exchange(m, dx=b) for b, m in enumerate(held) if b]
    tall = R * columns + (rows if slim else R * columns)
    packed = call(
        functools.partial(pack_kernel, dims, slim),
        [shape((tall, width), BF16)] * (2 if slim else 1),
        "pack",
        operands=held,
    )
    if slim:
        near, far = packed
        arrived = {0: near, 2: exchange(far, dz=2), 1: exchange(near, dz=1)}
        arrived[3] = exchange(arrived[2], dz=1)
    else:
        arrived, stride = {0: packed[0]}, Z // 2
        while stride:
            arrived |= {a ^ stride: exchange(m, dz=stride) for a, m in arrived.items()}
            stride //= 2

    spread_value, spread_gate, spread_output, moments, squares, centers, back = call(
        functools.partial(weights_kernel, depth),
        [shape((lanes, hidden * QUAD), BF16)] * 3
        + [shape((GROUP * SLOTS, GROUP * pair_width), BF16)] * 2
        + [shape((heads, pair_width), F32), shape((GROUP * SLOTS, 2 * GROUP * pair_width), BF16)],
        "weights",
        operands=(
            in_hbm(value_matrix), in_hbm(gate_matrix), in_hbm(output_matrix.T), in_hbm(head_bias_matrix.T),
            in_hbm(pair_norm_gain.reshape(1, pair_width)),
        ),
    )

    block = min(32, rows)
    steps = rows // block
    whole = pl.BlockSpec(memory_space=pltpu.VMEM)
    by_row = lambda *tail: pl.BlockSpec((block, *tail), lambda i: (i,) + (0,) * len(tail))
    by_middle = lambda lead: pl.BlockSpec((lead, block, columns), lambda i: (0, i, 0))
    exps, stats, logits, means, inverses = call(
        functools.partial(pair_kernel, heads),
        [
            shape((heads + 1, rows, columns), BF16),
            shape((rows, columns), BF16),
            shape((heads, rows, columns), F32),
            shape((rows, columns), F32),
            shape((rows, columns), F32),
        ],
        "pair",
        operands=(pair_input, moments, squares, centers, token_row),
        scratch=[pltpu.VMEM((block * heads, columns), F32)],
        grid=(steps,),
        in_specs=[by_row(columns, pair_width)] + [whole] * 3 + [pl.BlockSpec((1, columns), lambda i: (0, 0))],
        out_specs=[by_middle(heads + 1), by_row(columns), by_middle(heads), by_row(columns), by_row(columns)],
    )
    exps = [exps] + [exchange(exps, dx=b) for b in range(1, R)]
    far = [exchange(stats, dx=b, dc=1) for b in range(R)]
    probs, scales = call(
        functools.partial(probs_kernel, R, heads),
        [shape((heads, rows, R * columns), BF16), shape((R, rows, columns), F32)],
        "probs",
        operands=(*exps, *far),
    )

    values, mixed_grads, outgoing = [], [], {}
    for phase in [(0, 1, 2), (3,)] if slim else [tuple(range(Z))]:
        n = len(phase)
        quads = n * width // lanes
        messages = [arrived[a] for a in phase]
        (picked,) = call(
            functools.partial(pick_kernel, dims, slim),
            [shape((n, 2 * rows, width), BF16)],
            "pick",
            operands=messages,
        )
        value, mixed_grad, keep, send, partial = call(
            functools.partial(work_kernel, dims, heads),
            [
                shape((heads, R * columns, quads * step), BF16),
                shape((heads, rows, quads * step), BF16),
                shape((n, 2 * rows, width), F32),
                shape((n, 2 * rows, width), BF16),
                shape((n, R * columns, width), F32),
            ],
            "work",
            operands=(
                picked, exchange(picked, dc=1), *messages, probs, spread_value, spread_gate, spread_output,
            ),
            scratch=[
                pltpu.VMEM((n, 2 * rows, width), BF16),
                pltpu.VMEM((quads, rows, heads * step), F32),
                pltpu.VMEM((quads, rows, heads * step), F32),
                pltpu.VMEM((quads, R * columns, heads * step), BF16),
            ],
        )
        values.append(value)
        mixed_grads.append(mixed_grad)
        finished = call(
            functools.partial(finish_kernel, dims),
            [shape((R * columns + rows, width), BF16)] * n,
            "finish",
            operands=(keep, exchange(send, dc=1), partial),
        )
        outgoing |= dict(zip(phase, finished))
    collected = [exchange(outgoing[a], dz=a) if a else outgoing[a] for a in range(Z)]

    own_scores, own_total, *scores = call(
        functools.partial(scores_kernel, R, heads, len(values)),
        [shape((heads, rows, columns), F32), shape((rows, columns), BF16)]
        + [shape((heads + 1, rows, columns), BF16)] * (R - 1),
        "scores",
        operands=(*mixed_grads, *values, scales, *exps),
    )
    scores = [exchange(m, dx=b) for b, m in enumerate(scores, 1)]
    totals = [own_total] + [exchange(own_total, dx=b, dc=1) for b in range(R)]

    (pair_gradient,) = call(
        functools.partial(pair_back_kernel, R, heads),
        [shape(pair_features.shape, BF16)],
        "pair_back",
        operands=(
            pair_input, logits, means, inverses, exps[0], scales, own_scores, back, *scores, *totals,
        ),
        scratch=[pltpu.VMEM((block * SLOTS, columns), F32)],
        grid=(steps,),
        in_specs=[
            by_row(columns, pair_width), by_middle(heads), by_row(columns), by_row(columns),
            by_middle(heads + 1), by_middle(1), by_middle(heads), whole,
        ]
        + [by_middle(heads + 1)] * (R - 1)
        + [by_row(columns)] * (R + 1),
        out_specs=[by_row(columns, pair_width)],
    )
    shares = call(
        functools.partial(fold_kernel, dims), [share] * R, "fold", operands=collected
    )
    shares = [shares[0]] + [exchange(m, dx=b) for b, m in enumerate(shares) if b]
    alignment_update, alignment_gradient = call(
        functools.partial(last_kernel, dims),
        [shape(alignment_turned.shape, BF16)] * 2,
        "last",
        scalars=1,
        operands=(seq_mask, alignment_turned, gain, token_row, *shares),
        scratch=[pltpu.VMEM((columns, R * width), F32)] * 2,
    )
    return by_channel(alignment_update), by_channel(alignment_gradient), pair_gradient


def solution(mesh):
    split = P(("groups", "seq"), ("res", "sub"), None)
    sizes = (mesh.shape["seq"], mesh.shape["res"], mesh.shape["sub"])
    return jax.shard_map(
        functools.partial(shards, *sizes),
        mesh=mesh,
        in_specs=(split, split, split, P(), P(), P(), P(), P(), P())
        + (P(("groups", "seq")), P(("groups", "res", "sub"))),
        out_specs=(split, split, split),
        check_vma=False,
    )
```

time: 98.5 us -> 69.1 us (0.70)
  starting transfers between devices: 39.3 us -> 17.6 us
  waiting for transfers between devices: 2.05 us -> 22.3 us
  Pallas kernels: 42.5 us -> 27.4 us
  local copies, waits for them, and re-layouts: 11.1 us -> 0.66 us
  other arithmetic: 1.94 us -> 0 us
    ppermute x13 -> x18, waiting for transfers between devices: 2.05 us -> 22.3 us  [exchange(): lax.ppermute(value, everyone, [(at(z, x, c), at(z ^ dz, x ^ dx, c ^ dc))...]
    pallas_call x9 -> x15, Pallas kernels: 42.5 us -> 27.4 us  [call(): pl.pallas_call(kernel, out_shape=out_shape, in_specs=in_specs, out_specs=...]
    all_to_all x2 -> x0, starting transfers between devices: 14.9 us -> none  [the longest x1 7.53 us: shards(): collected = lax.all_to_all(partial, ('seq', 'res'), 0, 0, tiled=True)]
    unnamed x42 -> x4, local copies, waits for them, and re-layouts: 10.3 us -> 0.66 us
    ppermute x13 -> x18, starting transfers between devices: 24.4 us -> 17.6 us  [exchange(): lax.ppermute(value, everyone, [(at(z, x, c), at(z ^ dz, x ^ dx, c ^ dc))...]
    reshape x1 -> x0, other arithmetic: 1.29 us -> none  [shards(): gain2 = jnp.concatenate([alignment_norm_gain] * 2).reshape(1, 2 * channels)]
  transfers between devices with their start and end apart: 15 -> 18, of which waited for: 5 -> 8; matrix products, arithmetic and copies ran while one was open for 1% -> 0% of each run, Pallas kernels for 36% -> 34%
where the time goes in v2:
time: 69.1 us; the launch traced here: 68.8 us
  Pallas kernels  27.4 us (40%)
  waiting for transfers between devices  22.3 us (32%)
  starting transfers between devices  17.6 us (25%)
  between operations  0.78 us (1%)
    pallas_call x15, Pallas kernels, call(): pl.pallas_call(kernel, out_shape=out_shape, in_specs=in_specs, out_specs=...  27.4 us
    ppermute x18, waiting for transfers between devices, exchange(): lax.ppermute(value, everyone, [(at(z, x, c), at(z ^ dz, x ^ dx, c ^ dc))...  22.3 us
    ppermute x18, starting transfers between devices, exchange(): lax.ppermute(value, everyone, [(at(z, x, c), at(z ^ dz, x ^ dx, c ^ dc))...  17.6 us
  transfers between devices with their start and end apart: 18, of which 8 were waited for; matrix products, arithmetic and copies ran while one was open for 0% of the time, Pallas kernels for 34%

profile of v2, /device:TPU:0, one launch (start us, length us, event | category | flops | bytes accessed | tf_op | source)
XLA Modules:
  0.0 68.8 jit_solution(15027384426576641202)
XLA Ops:
  0.6 0.0 copy-start
  0.6 0.6 copy-done
  1.3 1.6 %first.1 = (bf16[256,256]{1,0:T(8,128)(2,1)S(1)}, bf16[256,256]{1,0:T(8,128)(2,1)S(1)}) custom-call(s32[8]{0:T(128)S(1)} %copy-done, bf16[8,64,128]{2,1,0:T(8,128)(2,1)} %bitcast.10, bf16[8,64,128]{2,1,0:T(8,128)(2,1)} %bitcast.9, bf16[1,64]{1,0:T(2,128)(2,1)} %bitcast.15, s32[1,128]{1,0:T(1,128)} %bitcast.17), custom_call_target="tpu_custom_call" | custom-call | flops 4499999744 | tf_op jit(solution)/shard_map/first/pallas_call | solution.py:60
  2.9 3.0 %collective-permute-start = (bf16[256,256]{1,0:T(8,128)(2,1)S(1)}, bf16[256,256]{1,0:T(8,128)(2,1)S(1)}, u32[]{:S(2)}, u32[]{:S(2)}) collective-permute-start(bf16[256,256]{1,0:T(8,128)(2,1)S(1)} %get-tuple-element.42), channel_id=1, source_target_pairs={{0,2},{1,3},{2,0},{3,1},{4,6},{5,7},{6,4},{7,5},{8,10},{9,11},{10,... | collective-permute-start | bytes 393224 | tf_op jit(solution)/shard_map/ppermute | solution.py:515
  5.9 1.3 %weights.1 = (bf16[256,1024]{1,0:T(8,128)(2,1)S(1)}, bf16[256,1024]{1,0:T(8,128)(2,1)S(1)}, bf16[256,1024]{1,0:T(8,128)(2,1)S(1)}, bf16[128,512]{1,0:T(8,128)(2,...) custom-call(bf16[64,256]{1,0:T(8,128)(2,1)} %value_ref.1, ...), custom_call_target="tpu_custom_call" | custom-call | flops 3900000000 | tf_op jit(solution)/shard_map/weights/pallas_call | solution.py:60
  7.2 2.2 %collective-permute-done.refs_1_ = bf16[256,256]{1,0:T(8,128)(2,1)S(1)} collective-permute-done((bf16[256,256]{1,0:T(8,128)(2,1)S(1)}, bf16[256,256]{1,0:T(8,128)(2,1)S(1)}, u32[]{:S(2)}, u32[]{:S(2)}) %collective-permute-start) | collective-permute-done | bytes 131104 | tf_op jit(solution)/shard_map/ppermute | solution.py:515
  9.4 1.9 %collective-permute-start.1 = (bf16[384,256]{1,0:T(8,128)(2,1)S(1)}, bf16[384,256]{1,0:T(8,128)(2,1)S(1)}, u32[]{:S(2)}, u32[]{:S(2)}) collective-permute-start(bf16[384,256]{1,0:T(8,128)(2,1)S(1)} %get-tuple-element.43.refs_0_), channel_id=1, source_target_pairs={{0,4},{1,5},{2,6},{3,7},{4,0},{5,1},{6,2},{7,3},{8,12},{9,13},{10,... | collective-permute-start | bytes 589832 | tf_op jit(solution)/shard_map/ppermute | solution.py:515
  11.3 2.6 %collective-permute-start.2 = (bf16[384,256]{1,0:T(8,128)(2,1)S(1)}, bf16[384,256]{1,0:T(8,128)(2,1)S(1)}, u32[]{:S(2)}, u32[]{:S(2)}) collective-permute-start(bf16[384,256]{1,0:T(8,128)(2,1)S(1)} %get-tuple-element.44), channel_id=1, source_target_pairs={{0,8},{1,9},{2,10},{3,11},{4,12},{5,13},{6,14},{7,15},{8,0},{9,1},... | collective-permute-start | bytes 589832 | tf_op jit(solution)/shard_map/ppermute | solution.py:515
  13.9 6.5 %pair.1 = (bf16[9,128,128]{2,1,0:T(8,128)(2,1)S(1)}, bf16[128,128]{1,0:T(8,128)(2,1)S(1)}, f32[8,128,128]{2,1,0:T(8,128)S(1)}, f32[128,128]{1,0:T(8,128)S(1)}, f32[128,128]{1,0:T(8,128)S(1)}) custom-call(bf16[128,128,128]{2,1,0:T(8,128)(2,1)} %x_ref.3, bf16[128,512]{1,0:T(8,128)(2,1)S(1)} %get-tuple-element.45.moments, ...), custom_call_target="tpu_custom_call" | custom-call | flops 19499999232 | tf_op jit(solution)/shard_map/pair/pallas_call | solution.py:60
  20.4 1.6 %collective-permute-start.4 = (bf16[9,128,128]{2,1,0:T(8,128)(2,1)S(1)}, bf16[9,128,128]{2,1,0:T(8,128)(2,1)S(1)}, u32[]{:S(2)}, u32[]{:S(2)}) collective-permute-start(bf16[9,128,128]{2,1,0:T(8,128)(2,1)S(1)} %get-tuple-element.48.refs_0_.refs_5_.e_ref), channel_id=1, source_target_pairs={{0,2},{1,3},{2,0},{3,1},{4,6},{5,7},{6,4},{7,5},{8,10},{9,11},{10,... | collective-permute-start | bytes 884744 | tf_op jit(solution)/shard_map/ppermute | solution.py:515
  22.0 0.0 collective-permute-done.1.refs_1_
  22.0 0.0 collective-permute-done.2.refs_2_
  22.0 0.1 collective-permute-start.3
  22.1 0.5 collective-permute-start.5
  22.6 1.1 %collective-permute-start.6 = (bf16[128,128]{1,0:T(8,128)(2,1)S(1)}, bf16[128,128]{1,0:T(8,128)(2,1)S(1)}, u32[]{:S(2)}, u32[]{:S(2)}) collective-permute-start(bf16[128,128]{1,0:T(8,128)(2,1)S(1)} %get-tuple-element.49), channel_id=1, source_target_pairs={{0,3},{1,2},{2,1},{3,0},{4,7},{5,6},{6,5},{7,4},{8,11},{9,10},{10,... | collective-permute-start | bytes 98312 | tf_op jit(solution)/shard_map/ppermute | solution.py:515
  23.7 0.4 collective-permute-start.10
  24.2 0.0 collective-permute-done.5.refs_2_
  24.2 3.4 %collective-permute-done.6.refs_3_ = bf16[128,128]{1,0:T(8,128)(2,1)S(1)} collective-permute-done((bf16[128,128]{1,0:T(8,128)(2,1)S(1)}, bf16[128,128]{1,0:T(8,128)(2,1)S(1)}, u32[]{:S(2)}, u32[]{:S(2)}) %collective-permute-start.6) | collective-permute-done | bytes 32800 | tf_op jit(solution)/shard_map/ppermute | solution.py:515
  27.5 0.6 collective-permute-done.4.refs_1_.refs_6_
  28.2 0.6 probs.1
  28.8 2.2 %collective-permute-done.10.refs_0_ = bf16[384,256]{1,0:T(8,128)(2,1)S(1)} collective-permute-done((bf16[384,256]{1,0:T(8,128)(2,1)S(1)}, bf16[384,256]{1,0:T(8,128)(2,1)S(1)}, u32[]{:S(2)}, u32[]{:S(2)}) %collective-permute-start.10) | collective-permute-done | bytes 196640 | tf_op jit(solution)/shard_map/ppermute | solution.py:515
  31.0 0.1 collective-permute-start.11
  31.1 0.0 collective-permute-done.3.other
  31.1 3.5 %work.2 = (bf16[8,256,384]{2,1,0:T(8,128)(2,1)S(1)}, bf16[8,128,384]{2,1,0:T(8,128)(2,1)S(1)}, f32[3,256,256]{2,1,0:T(8,128)S(1)}, bf16[3,256,256]{2,1,0:T(8,128)(2,1)S(1)}, f32[3,256,256]{2,1,0:T(8,128)S(1)}) custom-call(bf16[3,256,256]{2,1,0:T(8,128)(2,1)S(1)} %pick.2.mine, bf16[3,256,256]{2,1,0:T(8,128)(2,1)S(1)} %collective-permute-done.3.other, ...), custom_call_target="tpu_custom_call" | custom-call | flops 12000000000 | tf_op jit(solution)/shard_map/work/pallas_call | solution.py:60
  34.6 0.5 collective-permute-start.7
  35.1 0.0 collective-permute-done.11.other
  35.1 1.2 %work.3 = (bf16[8,256,128]{2,1,0:T(8,128)(2,1)S(1)}, bf16[8,128,128]{2,1,0:T(8,128)(2,1)S(1)}, f32[1,256,256]{2,1,0:T(8,128)S(1)}, bf16[1,256,256]{2,1,0:T(8,128)(2,1)S(1)}, f32[1,256,256]{2,1,0:T(8,128)S(1)}) custom-call(bf16[1,256,256]{2,1,0:T(8,128)(2,1)S(1)} %pick.3.mine, bf16[1,256,256]{2,1,0:T(8,128)(2,1)S(1)} %collective-permute-done.11.other, ...), custom_call_target="tpu_custom_call" | custom-call | flops 12000000000 | tf_op jit(solution)/shard_map/work/pallas_call | solution.py:60
  36.3 0.1 collective-permute-start.12
  36.4 1.3 %collective-permute-done.12.received = bf16[1,256,256]{2,1,0:T(8,128)(2,1)S(1)} collective-permute-done((bf16[1,256,256]{2,1,0:T(8,128)(2,1)S(1)}, bf16[1,256,256]{2,1,0:T(8,128)(2,1)S(1)}, u32[]{:S(2)}, u32[]{:S(2)}) %collective-permute-start.12) | collective-permute-done | bytes 131104 | tf_op jit(solution)/shard_map/ppermute | solution.py:515
  37.8 2.5 %collective-permute-start.13 = (bf16[384,256]{1,0:T(8,128)(2,1)S(1)}, bf16[384,256]{1,0:T(8,128)(2,1)S(1)}, u32[]{:S(2)}, u32[]{:S(2)}) collective-permute-start(bf16[384,256]{1,0:T(8,128)(2,1)S(1)} %finish.3), channel_id=1, source_target_pairs={{0,12},{1,13},{2,14},{3,15},{4,8},{5,9},{6,10},{7,11},{8,4},{9,5},... | collective-permute-start | bytes 589832 | tf_op jit(solution)/shard_map/ppermute | solution.py:515
  40.3 0.0 collective-permute-done.7.received
  40.3 0.1 finish.2
  40.4 0.1 collective-permute-start.8
  40.5 1.8 %collective-permute-start.9 = (bf16[384,256]{1,0:T(8,128)(2,1)S(1)}, bf16[384,256]{1,0:T(8,128)(2,1)S(1)}, u32[]{:S(2)}, u32[]{:S(2)}) collective-permute-start(bf16[384,256]{1,0:T(8,128)(2,1)S(1)} %get-tuple-element.59), channel_id=1, source_target_pairs={{0,8},{1,9},{2,10},{3,11},{4,12},{5,13},{6,14},{7,15},{8,0},{9,1},... | collective-permute-start | bytes 589832 | tf_op jit(solution)/shard_map/ppermute | solution.py:515
  42.3 1.8 %scores.1 = (f32[8,128,128]{2,1,0:T(8,128)S(1)}, bf16[128,128]{1,0:T(8,128)(2,1)S(1)}, bf16[9,128,128]{2,1,0:T(8,128)(2,1)S(1)}) custom-call(bf16[8,128,384]{2,1,0:T(8,128)(2,1)S(1)} %get-tuple-element.71.refs_0_, bf16[8,128,128]{2,1,0:T(8,128)(2,1)S(1)} %get-tuple-element.72.refs_1_, bf16[8,256,384]{2,1,0:T(8,128)(2,1)S(1)} %get-tuple-element.73.refs_2_, ...), custom_call_target="tpu_custom_call" | custom-call | flops 4499999744 | tf_op jit(solution)/shard_map/scores/pallas_call | solution.py:60
  44.1 0.7 collective-permute-start.15
  44.8 0.0 collective-permute-start.16
  44.8 2.7 %collective-permute-done.13.refs_3_ = bf16[384,256]{1,0:T(8,128)(2,1)S(1)} collective-permute-done((bf16[384,256]{1,0:T(8,128)(2,1)S(1)}, bf16[384,256]{1,0:T(8,128)(2,1)S(1)}, u32[]{:S(2)}, u32[]{:S(2)}) %collective-permute-start.13) | collective-permute-done | bytes 196640 | tf_op jit(solution)/shard_map/ppermute | solution.py:515
  47.5 0.0 collective-permute-start.17
  47.5 5.5 %collective-permute-done.8.refs_1_ = bf16[384,256]{1,0:T(8,128)(2,1)S(1)} collective-permute-done((bf16[384,256]{1,0:T(8,128)(2,1)S(1)}, bf16[384,256]{1,0:T(8,128)(2,1)S(1)}, u32[]{:S(2)}, u32[]{:S(2)}) %collective-permute-start.8) | collective-permute-done | bytes 196640 | tf_op jit(solution)/shard_map/ppermute | solution.py:515
  53.0 4.4 %collective-permute-done.9.refs_2_ = bf16[384,256]{1,0:T(8,128)(2,1)S(1)} collective-permute-done((bf16[384,256]{1,0:T(8,128)(2,1)S(1)}, bf16[384,256]{1,0:T(8,128)(2,1)S(1)}, u32[]{:S(2)}, u32[]{:S(2)}) %collective-permute-start.9) | collective-permute-done | bytes 196640 | tf_op jit(solution)/shard_map/ppermute | solution.py:515
  57.3 0.1 fold.1
  57.4 0.7 collective-permute-start.14
  58.1 0.0 collective-permute-done.16.refs_2_
  58.1 0.0 collective-permute-done.17.refs_3_
  58.1 0.0 collective-permute-done.15.refs_0_
  58.1 0.0 copy-start.1
  58.1 8.0 %pair_back.1 = bf16[128,128,128]{2,1,0:T(8,128)(2,1)} custom-call(bf16[128,128,128]{2,1,0:T(8,128)(2,1)} %x_ref.3, f32[8,128,128]{2,1,0:T(8,128)S(1)} %get-tuple-element.67.logit_ref, f32[128,128]{1,0:T(8,128)S(1)} %get-tuple-element.68.mean_ref, f32[128,128]{1,0:T(8,128)S(1)} %get-tuple-element.69.inverse_ref, ...), custom_call_target="tpu_custom_call" | custom-call | flops 24000000000 | tf_op jit(solution)/shard_map/pair_back/pallas_call | solution.py:60
  66.1 0.0 collective-permute-done.14.refs_1_
  66.1 0.0 copy-done.1
  66.1 2.7 %last.1 = (bf16[8,64,128]{2,1,0:T(8,128)(2,1)}, bf16[8,64,128]{2,1,0:T(8,128)(2,1)}) custom-call(s32[8]{0:T(128)S(1)} %copy-done.1, bf16[8,64,128]{2,1,0:T(8,128)(2,1)} %bitcast.11, bf16[1,64]{1,0:T(2,128)(2,1)} %bitcast.16, s32[1,128]{1,0:T(1,128)} %bitcast.19, bf16[256,256]{1,0:T(8,128)(2,1)S(1)} %get-tuple-element.63.refs_0_, ...), custom_call_target="tpu_custom_call" | custom-call | flops 8099999744 | tf_op jit(solution)/shard_map/last/pallas_call | solution.py:60
  (4 shorter events, 0.1 us)
Async XLA Ops:
  0.6 0.7 copy-start
  2.9 6.5 %collective-permute-start = (bf16[256,256]{1,0:T(8,128)(2,1)S(1)}, bf16[256,256]{1,0:T(8,128)(2,1)S(1)}, u32[]{:S(2)}, u32[]{:S(2)}) collective-permute-start(bf16[256,256]{1,0:T(8,128)(2,1)S(1)} %get-tuple-element.42), channel_id=1, source_target_pairs={{0,2},{1,3},{2,0},{3,1},{4,6},{5,7},{6,4},{7,5},{8,10},{9,11},{10,... | collective-permute-start | bytes 393224 | tf_op jit(solution)/shard_map/ppermute | solution.py:515
  9.4 12.6 %collective-permute-start.1 = (bf16[384,256]{1,0:T(8,128)(2,1)S(1)}, bf16[384,256]{1,0:T(8,128)(2,1)S(1)}, u32[]{:S(2)}, u32[]{:S(2)}) collective-permute-start(bf16[384,256]{1,0:T(8,128)(2,1)S(1)} %get-tuple-element.43.refs_0_), channel_id=1, source_target_pairs={{0,4},{1,5},{2,6},{3,7},{4,0},{5,1},{6,2},{7,3},{8,12},{9,13},{10,... | collective-permute-start | bytes 589832 | tf_op jit(solution)/shard_map/ppermute | solution.py:515
  11.3 10.7 %collective-permute-start.2 = (bf16[384,256]{1,0:T(8,128)(2,1)S(1)}, bf16[384,256]{1,0:T(8,128)(2,1)S(1)}, u32[]{:S(2)}, u32[]{:S(2)}) collective-permute-start(bf16[384,256]{1,0:T(8,128)(2,1)S(1)} %get-tuple-element.44), channel_id=1, source_target_pairs={{0,8},{1,9},{2,10},{3,11},{4,12},{5,13},{6,14},{7,15},{8,0},{9,1},... | collective-permute-start | bytes 589832 | tf_op jit(solution)/shard_map/ppermute | solution.py:515
  20.4 7.7 %collective-permute-start.4 = (bf16[9,128,128]{2,1,0:T(8,128)(2,1)S(1)}, bf16[9,128,128]{2,1,0:T(8,128)(2,1)S(1)}, u32[]{:S(2)}, u32[]{:S(2)}) collective-permute-start(bf16[9,128,128]{2,1,0:T(8,128)(2,1)S(1)} %get-tuple-element.48.refs_0_.refs_5_.e_ref), channel_id=1, source_target_pairs={{0,2},{1,3},{2,0},{3,1},{4,6},{5,7},{6,4},{7,5},{8,10},{9,11},{10,... | collective-permute-start | bytes 884744 | tf_op jit(solution)/shard_map/ppermute | solution.py:515
  22.0 9.0 %collective-permute-start.3 = (bf16[3,256,256]{2,1,0:T(8,128)(2,1)S(1)}, bf16[3,256,256]{2,1,0:T(8,128)(2,1)S(1)}, u32[]{:S(2)}, u32[]{:S(2)}) collective-permute-start(bf16[3,256,256]{2,1,0:T(8,128)(2,1)S(1)} %pick.2.mine), channel_id=1, source_target_pairs={{0,1},{1,0},{2,3},{3,2},{4,5},{5,4},{6,7},{7,6},{8,9},{9,8},{10,11... | collective-permute-start | bytes 1179656 | tf_op jit(solution)/shard_map/ppermute | solution.py:515
  22.1 2.0 %collective-permute-start.5 = (bf16[128,128]{1,0:T(8,128)(2,1)S(1)}, bf16[128,128]{1,0:T(8,128)(2,1)S(1)}, u32[]{:S(2)}, u32[]{:S(2)}) collective-permute-start(bf16[128,128]{1,0:T(8,128)(2,1)S(1)} %get-tuple-element.49), channel_id=1, source_target_pairs={{0,1},{1,0},{2,3},{3,2},{4,5},{5,4},{6,7},{7,6},{8,9},{9,8},{10,11... | collective-permute-start | bytes 98312 | tf_op jit(solution)/shard_map/ppermute | solution.py:515
  22.6 4.9 %collective-permute-start.6 = (bf16[128,128]{1,0:T(8,128)(2,1)S(1)}, bf16[128,128]{1,0:T(8,128)(2,1)S(1)}, u32[]{:S(2)}, u32[]{:S(2)}) collective-permute-start(bf16[128,128]{1,0:T(8,128)(2,1)S(1)} %get-tuple-element.49), channel_id=1, source_target_pairs={{0,3},{1,2},{2,1},{3,0},{4,7},{5,6},{6,5},{7,4},{8,11},{9,10},{10,... | collective-permute-start | bytes 98312 | tf_op jit(solution)/shard_map/ppermute | solution.py:515
  23.7 7.3 %collective-permute-start.10 = (bf16[384,256]{1,0:T(8,128)(2,1)S(1)}, bf16[384,256]{1,0:T(8,128)(2,1)S(1)}, u32[]{:S(2)}, u32[]{:S(2)}) collective-permute-start(bf16[384,256]{1,0:T(8,128)(2,1)S(1)} %collective-permute-done.2.refs_2_), channel_id=1, source_target_pairs={{0,4},{1,5},{2,6},{3,7},{4,0},{5,1},{6,2},{7,3},{8,12},{9,13},{10,... | collective-permute-start | bytes 589832 | tf_op jit(solution)/shard_map/ppermute | solution.py:515
  31.0 4.1 %collective-permute-start.11 = (bf16[1,256,256]{2,1,0:T(8,128)(2,1)S(1)}, bf16[1,256,256]{2,1,0:T(8,128)(2,1)S(1)}, u32[]{:S(2)}, u32[]{:S(2)}) collective-permute-start(bf16[1,256,256]{2,1,0:T(8,128)(2,1)S(1)} %pick.3.mine), channel_id=1, source_target_pairs={{0,1},{1,0},{2,3},{3,2},{4,5},{5,4},{6,7},{7,6},{8,9},{9,8},{10,11... | collective-permute-start | bytes 393224 | tf_op jit(solution)/shard_map/ppermute | solution.py:515
  34.6 5.7 %collective-permute-start.7 = (bf16[3,256,256]{2,1,0:T(8,128)(2,1)S(1)}, bf16[3,256,256]{2,1,0:T(8,128)(2,1)S(1)}, u32[]{:S(2)}, u32[]{:S(2)}) collective-permute-start(bf16[3,256,256]{2,1,0:T(8,128)(2,1)S(1)} %get-tuple-element.55), channel_id=1, source_target_pairs={{0,1},{1,0},{2,3},{3,2},{4,5},{5,4},{6,7},{7,6},{8,9},{9,8},{10,11... | collective-permute-start | bytes 1179656 | tf_op jit(solution)/shard_map/ppermute | solution.py:515
  36.3 1.4 %collective-permute-start.12 = (bf16[1,256,256]{2,1,0:T(8,128)(2,1)S(1)}, bf16[1,256,256]{2,1,0:T(8,128)(2,1)S(1)}, u32[]{:S(2)}, u32[]{:S(2)}) collective-permute-start(bf16[1,256,256]{2,1,0:T(8,128)(2,1)S(1)} %get-tuple-element.61), channel_id=1, source_target_pairs={{0,1},{1,0},{2,3},{3,2},{4,5},{5,4},{6,7},{7,6},{8,9},{9,8},{10,11... | collective-permute-start | bytes 393224 | tf_op jit(solution)/shard_map/ppermute | solution.py:515
  37.8 9.7 %collective-permute-start.13 = (bf16[384,256]{1,0:T(8,128)(2,1)S(1)}, bf16[384,256]{1,0:T(8,128)(2,1)S(1)}, u32[]{:S(2)}, u32[]{:S(2)}) collective-permute-start(bf16[384,256]{1,0:T(8,128)(2,1)S(1)} %finish.3), channel_id=1, source_target_pairs={{0,12},{1,13},{2,14},{3,15},{4,8},{5,9},{6,10},{7,11},{8,4},{9,5},... | collective-permute-start | bytes 589832 | tf_op jit(solution)/shard_map/ppermute | solution.py:515
  40.4 12.5 %collective-permute-start.8 = (bf16[384,256]{1,0:T(8,128)(2,1)S(1)}, bf16[384,256]{1,0:T(8,128)(2,1)S(1)}, u32[]{:S(2)}, u32[]{:S(2)}) collective-permute-start(bf16[384,256]{1,0:T(8,128)(2,1)S(1)} %get-tuple-element.58), channel_id=1, source_target_pairs={{0,4},{1,5},{2,6},{3,7},{4,0},{5,1},{6,2},{7,3},{8,12},{9,13},{10,... | collective-permute-start | bytes 589832 | tf_op jit(solution)/shard_map/ppermute | solution.py:515
  40.5 16.8 %collective-permute-start.9 = (bf16[384,256]{1,0:T(8,128)(2,1)S(1)}, bf16[384,256]{1,0:T(8,128)(2,1)S(1)}, u32[]{:S(2)}, u32[]{:S(2)}) collective-permute-start(bf16[384,256]{1,0:T(8,128)(2,1)S(1)} %get-tuple-element.59), channel_id=1, source_target_pairs={{0,8},{1,9},{2,10},{3,11},{4,12},{5,13},{6,14},{7,15},{8,0},{9,1},... | collective-permute-start | bytes 589832 | tf_op jit(solution)/shard_map/ppermute | solution.py:515
  44.1 14.0 %collective-permute-start.15 = (bf16[9,128,128]{2,1,0:T(8,128)(2,1)S(1)}, bf16[9,128,128]{2,1,0:T(8,128)(2,1)S(1)}, u32[]{:S(2)}, u32[]{:S(2)}) collective-permute-start(bf16[9,128,128]{2,1,0:T(8,128)(2,1)S(1)} %get-tuple-element.77), channel_id=1, source_target_pairs={{0,2},{1,3},{2,0},{3,1},{4,6},{5,7},{6,4},{7,5},{8,10},{9,11},{10,... | collective-permute-start | bytes 884744 | tf_op jit(solution)/shard_map/ppermute | solution.py:515
  44.8 13.3 %collective-permute-start.16 = (bf16[128,128]{1,0:T(8,128)(2,1)S(1)}, bf16[128,128]{1,0:T(8,128)(2,1)S(1)}, u32[]{:S(2)}, u32[]{:S(2)}) collective-permute-start(bf16[128,128]{1,0:T(8,128)(2,1)S(1)} %get-tuple-element.78.refs_1_), channel_id=1, source_target_pairs={{0,1},{1,0},{2,3},{3,2},{4,5},{5,4},{6,7},{7,6},{8,9},{9,8},{10,11... | collective-permute-start | bytes 98312 | tf_op jit(solution)/shard_map/ppermute | solution.py:515
  47.5 10.6 %collective-permute-start.17 = (bf16[128,128]{1,0:T(8,128)(2,1)S(1)}, bf16[128,128]{1,0:T(8,128)(2,1)S(1)}, u32[]{:S(2)}, u32[]{:S(2)}) collective-permute-start(bf16[128,128]{1,0:T(8,128)(2,1)S(1)} %get-tuple-element.78.refs_1_), channel_id=1, source_target_pairs={{0,3},{1,2},{2,1},{3,0},{4,7},{5,6},{6,5},{7,4},{8,11},{9,10},{10,... | collective-permute-start | bytes 98312 | tf_op jit(solution)/shard_map/ppermute | solution.py:515
  57.4 8.7 %collective-permute-start.14 = (bf16[256,256]{1,0:T(8,128)(2,1)S(1)}, bf16[256,256]{1,0:T(8,128)(2,1)S(1)}, u32[]{:S(2)}, u32[]{:S(2)}) collective-permute-start(bf16[256,256]{1,0:T(8,128)(2,1)S(1)} %get-tuple-element.64), channel_id=1, source_target_pairs={{0,2},{1,3},{2,0},{3,1},{4,6},{5,7},{6,4},{7,5},{8,10},{9,11},{10,... | collective-permute-start | bytes 393224 | tf_op jit(solution)/shard_map/ppermute | solution.py:515
  58.1 8.0 %copy-start.1 = (s32[8]{0:T(128)S(1)}, s32[8]{0:T(128)}, u32[]{:S(2)}) copy-start(s32[8]{0:T(128)} %seq_mask_ref.3) | copy-start | bytes 100

commit v3 on v2

--- a/solution.py
+++ b/solution.py
@@ -13,10 +13,7 @@
 QUAD = 4
 GROUP = 4
 SLOTS = 32
-COST = dict(
-    first=1.5, pack=0.4, weights=1.3, pair=6.5, pick=0.4, probs=0.8, work=4.0, scores=1.5, finish=0.6,
-    pair_back=8.0, fold=0.6, last=2.7,
-)
+COST = dict(first=1.5, pack=0.1, weights=1.3, pair=5, attach=0, pick=1, probs=0, work=0.0, scores=0.0, finish=0, pair_back=0, gather=5, fold=0, last=0)
 VMEM = 20 * 1024 * 1024
 
 
@@ -48,26 +45,25 @@
     return high, (value - high.astype(F32)).astype(BF16)
 
 
-def call(kernel, out_shape, name, scratch=(), flops=None, scalars=0, operands=(), grid=None, in_specs=None, out_specs=None):
+def call(kernel, out_shape, name, operands, scratch=(), after=(), grid=None, out_specs=None, into=None):
     whole = pl.BlockSpec(memory_space=pltpu.VMEM)
-    if in_specs is None:
-        in_specs = [pl.BlockSpec(memory_space=pltpu.SMEM)] * scalars + [whole] * (len(operands) - scalars)
-        out_specs = [whole] * len(out_shape)
+    count = len(operands)
+    body = lambda *refs: kernel(*refs[:count], *refs[count + len(after) :])
     extra = {} if grid is None else {"grid": grid}
-    moved = sum(o.size * o.dtype.itemsize for o in operands) + sum(
-        o.size * o.dtype.itemsize for o in out_shape
-    )
+    if into is not None:
+        extra["input_output_aliases"] = {count + len(after): 0}
+        after = [*after, into]
     return pl.pallas_call(
-        kernel,
+        body,
         out_shape=out_shape,
-        in_specs=in_specs,
-        out_specs=out_specs,
+        in_specs=[whole] * count + [pl.BlockSpec(memory_space=pl.ANY)] * len(after),
+        out_specs=out_specs or [whole] * len(out_shape),
         scratch_shapes=list(scratch),
         compiler_params=pltpu.CompilerParams(vmem_limit_bytes=VMEM),
         cost_estimate=pl.CostEstimate(flops=int(COST[name] * 3e9), bytes_accessed=0, transcendentals=0),
         name=name,
         **extra,
-    )(*operands)
+    )(*operands, *after)
 
 
 def shape(dims, dtype):
@@ -114,11 +110,7 @@
     moments[...] = diagonal(slots)
     squares[...] = diagonal(square_slots)
     high, middle, _ = split3(scaled - total * (1.0 / width))
-    left = jnp.concatenate([high, middle, high, jnp.where(row < 3, 1.0, 0.0)], axis=0)
-    right = jnp.concatenate(
-        [jnp.zeros((3 * heads, width), F32), jnp.where((row >= 3) & (row < 6), 1.0, 0.0)], axis=0
-    )
-    back[...] = diagonal(jnp.concatenate([left, right], axis=1))
+    back[...] = diagonal(jnp.concatenate([high, middle, high, jnp.where(row < 3, 1.0, 0.0)], axis=0))
 
 
 def side_by_side(ref, pair, channels):
@@ -157,19 +149,28 @@
     return c == lax.rem(block, C), x ^ (block // C), lax.rem(z, parts)
 
 
-def first_kernel(dims, seq_mask_ref, x_ref, u_ref, gain_ref, token_ref, *shares):
+def first_kernel(dims, seq_mask_ref, x_ref, u_ref, gain_ref, token_ref, scaled_out, inverse_out, alive_out, gain_out, *shares):
     Z, R, C, rows, parts, width = dims
     channels, columns = x_ref.shape[1:]
     mean_matrix = averaging(channels)
     live = column(token_ref[...].astype(F32), 2 * channels)
+    seq_mask = seq_mask_ref[...].astype(F32)
     gain = jnp.concatenate([gain_ref[...].astype(F32)] * 2, axis=1)
-    second_half = iota(live.shape, 1) >= channels
+    second_half = iota((1, 2 * channels), 1) >= channels
     normed, masked = [], []
     for pair in range(x_ref.shape[0] // 2):
-        scaled, _ = normalized(side_by_side(x_ref, pair, channels), mean_matrix)
+        at = slice(pair * 2 * channels, (pair + 1) * 2 * channels)
+        scaled, inverse = normalized(side_by_side(x_ref, pair, channels), mean_matrix)
+        scaled_out[:, at] = scaled
+        inverse_out[:, at] = inverse
         normed.append((scaled * gain).astype(BF16))
-        keep = jnp.where(second_half, seq_mask_ref[2 * pair + 1], seq_mask_ref[2 * pair]).astype(F32)
-        masked.append((side_by_side(u_ref, pair, channels) * keep * live).astype(BF16))
+        keep = jnp.where(
+            second_half, seq_mask[:, 2 * pair + 1 : 2 * pair + 2], seq_mask[:, 2 * pair : 2 * pair + 1]
+        )
+        alive = keep * live
+        alive_out[:, at] = alive
+        masked.append((side_by_side(u_ref, pair, channels) * alive).astype(BF16))
+    gain_out[...] = jnp.broadcast_to(gain, gain_out.shape)
     both = jnp.concatenate(
         [jnp.concatenate(normed, axis=1), jnp.concatenate(masked, axis=1)], axis=0
     )
@@ -202,9 +203,11 @@
             messages[0][(R + b) * columns : (R + b + 1) * columns] = held[b][columns:]
 
 
-def pick_kernel(dims, slim, *refs):
+def pick_kernel(dims, slim, count, *refs):
     Z, R, C, rows, parts, width = dims
-    messages, picked = refs[:-1], refs[-1]
+    messages, picked, relayed = refs[:count], refs[count], refs[count + 1 :]
+    for source, target in zip(messages, relayed):
+        target[...] = source[...]
     columns = messages[0].shape[0] // (R + 1 if slim else 2 * R)
     _, block, part = rows_place(dims)
     at = pl.multiple_of(block * columns + part * rows, rows)
@@ -213,65 +216,76 @@
         picked[n, rows : 2 * rows] = message[R * columns :] if slim else message[pl.ds(R * columns + at, rows)]
 
 
-def pair_kernel(heads, x_ref, moments, squares, centers, token_ref, e_ref, stat_ref, logit_ref, mean_ref, inverse_ref, scratch):
-    count, columns, width = x_ref.shape
-    groups = count // GROUP
-    x = x_ref[...].reshape(groups, GROUP, columns, width)
-    parts, highs, lows = [], [], []
-    for g in range(GROUP):
-        part = x[:, g].reshape(groups * columns, width)
-        value = part.astype(F32)
-        high, low = split2(value * value)
-        parts.append(part)
-        highs.append(high)
-        lows.append(low)
-    both = squares[...]
-    product = (
-        dot_nt(jnp.concatenate(parts, axis=1), moments[...])
-        + dot_nt(jnp.concatenate(highs, axis=1), both)
-        + dot_nt(jnp.concatenate(lows, axis=1), both)
-    )
+def pair_kernel(heads, block, x_ref, moments, squares, centers, token_ref, *refs):
+    e_upper, e_lower, stat_ref, logit_ref, mean_ref, inverse_ref, scratch = refs
+    rows, columns, width = x_ref.shape
+    cut = e_upper.shape[1]
+    groups = block // GROUP
     padding = 1000000000.0 * (token_ref[...].astype(F32) - 1.0)
-    center = centers[...]
-    for group in range(groups):
-        turned = jnp.transpose(product[group * columns : (group + 1) * columns])
+    lane = iota((rows, columns), 1)
+
+    def step(index, carry):
+        low = pl.multiple_of(index * block, block)
+        x = x_ref[pl.ds(low, block)].reshape(groups, GROUP, columns, width)
+        parts, highs, lows = [], [], []
         for g in range(GROUP):
-            i = group * GROUP + g
-            base = g * SLOTS
-            raw = (
-                turned[base : base + heads]
-                + turned[base + heads : base + 2 * heads]
-                + turned[base + 2 * heads : base + 3 * heads]
-            )
-            total = turned[base + 3 * heads : base + 3 * heads + 1]
-            square = turned[base + 3 * heads + 4 : base + 3 * heads + 5]
-            mean = total * (1.0 / width)
-            upper = total.astype(BF16).astype(F32)
-            lower = total - upper
-            spread_sum = (square - upper * upper * (1.0 / width)) - (
-                2.0 * upper * lower + lower * lower
-            ) * (1.0 / width)
-            inverse = lax.rsqrt(jnp.maximum(spread_sum, 0.0) * (1.0 / width) + EPS)
-            scratch[i * heads : (i + 1) * heads] = inverse * (raw - mean * center)
-            mean_ref[i : i + 1] = mean
-            inverse_ref[i : i + 1] = inverse
-    lane = iota((count, columns), 1)
-    stats = jnp.zeros((count, columns), F32)
+            part = x[:, g].reshape(groups * columns, width)
+            value = part.astype(F32)
+            high, rest = split2(value * value)
+            parts.append(part)
+            highs.append(high)
+            lows.append(rest)
+        product = dot_nt(
+            jnp.concatenate(parts + highs + lows, axis=1),
+            jnp.concatenate([moments[...], squares[...], squares[...]], axis=1),
+        )
+        center = centers[...]
+        for group in range(groups):
+            turned = jnp.transpose(product[group * columns : (group + 1) * columns])
+            for g in range(GROUP):
+                i = group * GROUP + g
+                base = g * SLOTS
+                raw = (
+                    turned[base : base + heads]
+                    + turned[base + heads : base + 2 * heads]
+                    + turned[base + 2 * heads : base + 3 * heads]
+                )
+                total = turned[base + 3 * heads : base + 3 * heads + 1]
+                square = turned[base + 3 * heads + 4 : base + 3 * heads + 5]
+                mean = total * (1.0 / width)
+                upper = total.astype(BF16).astype(F32)
+                lower = total - upper
+                spread_sum = (square - upper * upper * (1.0 / width)) - (
+                    2.0 * upper * lower + lower * lower
+                ) * (1.0 / width)
+                inverse = lax.rsqrt(jnp.maximum(spread_sum, 0.0) * (1.0 / width) + EPS)
+                scratch[pl.ds(pl.multiple_of((low + i) * heads, heads), heads)] = inverse * (raw - mean * center)
+                mean_ref[pl.ds(low + i, 1)] = mean
+                inverse_ref[pl.ds(low + i, 1)] = inverse
+        return carry
+
+    lax.fori_loop(0, rows // block, step, 0, unroll=True)
+    stats = jnp.zeros((rows, columns), F32)
+    ones = jnp.ones((columns, columns), BF16)
     for h in range(heads):
-        logit = scratch[pl.ds(h, count, stride=heads), :]
+        logit = scratch[pl.ds(h, rows, stride=heads), :]
         logit_ref[h] = logit
         logit = logit + padding
         peak = jnp.max(logit, axis=1, keepdims=True)
         e = jnp.exp(logit - peak).astype(BF16)
-        e_ref[h] = e
-        total = jnp.sum(e.astype(F32), axis=1, keepdims=True)
-        for t, part in enumerate(split3(peak)):
-            stats = jnp.where(lane == t * heads + h, part, stats)
-        for t, part in enumerate(split3(total)):
-            stats = jnp.where(lane == (t + 3) * heads + h, part, stats)
-    stats = stats.astype(BF16)
-    e_ref[heads] = stats
-    stat_ref[...] = stats
+        e_upper[h] = e[:cut]
+        e_lower[h] = e[cut:]
+        stats = jnp.where(lane == h, peak, stats)
+        stats = jnp.where(lane == 3 * heads + h, dot(e, ones), stats)
+    high, middle, rest = split3(stats)
+    stats = high + pltpu.roll(middle, heads, 1) + pltpu.roll(rest, 2 * heads, 1)
+    stat_ref[...] = stats.astype(BF16)
+
+
+def thirds(value, heads):
+    lane = iota(value.shape, 1)
+    high, middle, low = split3(jnp.where(lane < heads, value, 0.0))
+    return high + pltpu.roll(middle, heads, 1) + pltpu.roll(low, 2 * heads, 1)
 
 
 def joined_thirds(stats, heads):
@@ -283,11 +297,31 @@
     )
 
 
+def attach_kernel(heads, e_ref, own_ref, other_ref, message):
+    size = e_ref.shape[1]
+    message[0:heads] = e_ref[...]
+    at = heads
+    for ref in (own_ref, other_ref):
+        for low in range(0, ref.shape[0], size):
+            message[at] = ref[low : low + size]
+            at += 1
+
+
+def attached(message, heads, rows):
+    count = rows // message.shape[1]
+    return [
+        jnp.concatenate([message[at + n] for n in range(count)], axis=0).astype(F32)
+        for at in (heads, heads + count)
+    ]
+
+
 def probs_kernel(R, heads, *refs):
-    exps, far, (probs, scales) = refs[:R], refs[R : 2 * R], refs[2 * R :]
-    columns = exps[0].shape[2]
-    near = [joined_thirds(e[heads].astype(F32), heads) for e in exps]
-    everything = near + [joined_thirds(s[...].astype(F32), heads) for s in far]
+    exps, (probs, scales) = refs[: 2 * R], refs[2 * R :]
+    rows, columns = scales.shape[1:]
+    exps = [exps[2 * b : 2 * b + 2] for b in range(R)]
+    stats = [[joined_thirds(s, heads) for s in attached(lower, heads, rows)] for _, lower in exps]
+    near = [pair[0] for pair in stats]
+    everything = near + [pair[1] for pair in stats]
     peak = functools.reduce(jnp.maximum, everything)
     total = 0.0
     for s in everything:
@@ -296,8 +330,12 @@
         scale = jnp.exp(near[b] - peak) / total
         scales[b] = scale
         for h in range(heads):
-            weight = exps[b][h].astype(F32) * scale[:, h : h + 1]
-            probs[h, :, b * columns : (b + 1) * columns] = weight.astype(BF16)
+            low = 0
+            for e in exps[b]:
+                at = slice(low, low + e.shape[1])
+                low += e.shape[1]
+                weight = e[h].astype(F32) * scale[at, h : h + 1]
+                probs[h, at, b * columns : (b + 1) * columns] = weight.astype(BF16)
 
 
 def quad(refs, q, rows, lanes):
@@ -379,9 +417,10 @@
     mixed_grads, refs = refs[:count], refs[count:]
     values, refs = refs[:count], refs[count:]
     scales, *refs = refs
-    exps, refs = refs[:R], refs[R:]
+    exps, refs = refs[: 2 * R], refs[2 * R :]
     own_scores, total_ref, *messages = refs
-    rows, columns = exps[0].shape[1:]
+    half = heads // 2
+    rows, columns = total_ref.shape
     lane = iota((rows, columns), 1)
     sums = jnp.zeros((rows, columns), F32)
     for h in range(heads):
@@ -393,64 +432,86 @@
                 own_scores[h] = part
             else:
                 part = part.astype(BF16)
-                messages[b - 1][h] = part
+                messages[2 * b - 2 + h // half][h % half] = part
                 part = part.astype(F32)
-            weight = exps[b][h].astype(F32) * scales[b][:, h : h + 1]
+            weight = jnp.concatenate([e[h] for e in exps[2 * b : 2 * b + 2]], axis=0)
+            weight = weight.astype(F32) * scales[b][:, h : h + 1]
             total = total + jnp.sum(weight * part, axis=1, keepdims=True)
         for t, part in enumerate(split3(total)):
             sums = jnp.where(lane == t * heads + h, part, sums)
-    sums = sums.astype(BF16)
-    total_ref[...] = sums
-    for message in messages:
-        message[heads] = sums
-
-
-def pair_back_kernel(R, heads, x_ref, logit_ref, mean_ref, inverse_ref, e_ref, scale_ref, own_ref, back_ref, *refs):
-    received, refs = refs[: R - 1], refs[R - 1 :]
-    totals, refs = refs[: R + 1], refs[R + 1 :]
-    out_ref, scratch = refs
-    count, columns, width = x_ref.shape
-    total = sum(t[...].astype(F32) for t in totals) + sum(m[heads].astype(F32) for m in received)
+    total_ref[...] = sums.astype(BF16)
+
+
+def attach_total_kernel(heads, scores_ref, own_ref, other_ref, message):
+    count = scores_ref.shape[0]
+    message[0:count] = scores_ref[...]
+    total = sum(joined_thirds(ref[...].astype(F32), heads) for ref in (own_ref, other_ref))
+    message[count] = thirds(total, heads).astype(BF16)
+
+
+def pair_back_kernel(R, heads, first, x_ref, e_ref, logit_ref, mean_ref, inverse_ref, scale_ref, own_ref, back_ref, *refs):
+    own_total, received, refs = refs[0], refs[1 : 2 * R - 1], refs[2 * R - 1 :]
+    firsts, seconds, half = received[::2], received[1::2], heads // 2
+    out_ref, done_ref, scratch, turned, rounded = refs
+    count, columns, width = out_ref.shape
+    here = pl.ds(pl.multiple_of(pl.program_id(0) * count, count), count)
+    low = pl.multiple_of(first + pl.program_id(0) * count, count)
+    at = pl.ds(low, count)
+    done_ref[...] = jnp.zeros_like(done_ref)
+    total = sum(m[half, at].astype(F32) for m in (own_total, *seconds))
     total = joined_thirds(total, heads)
-    scale = scale_ref[0]
-    inverse = inverse_ref[...]
+    scale = scale_ref[0, at]
+    inverse = inverse_ref[at]
     cross = 0.0
     for h in range(heads):
-        scores = own_ref[h]
-        for m in received:
-            scores = scores + m[h].astype(F32)
-        prob = e_ref[h].astype(F32) * scale[:, h : h + 1]
+        scores = own_ref[h, at]
+        for m in (firsts, seconds)[h // half]:
+            scores = scores + m[h % half, at].astype(F32)
+        prob = e_ref[h, here].astype(F32) * scale[:, h : h + 1]
         grad = prob * (scores - total[:, h : h + 1])
-        cross = cross + grad * logit_ref[h]
+        cross = cross + grad * logit_ref[h, at]
         scaled = grad * inverse
         high = scaled.astype(BF16).astype(F32)
         scratch[pl.ds(h, count, stride=SLOTS), :] = high
         scratch[pl.ds(heads + h, count, stride=SLOTS), :] = high
         scratch[pl.ds(2 * heads + h, count, stride=SLOTS), :] = scaled - high
     factor = inverse * inverse * cross * (1.0 / width)
-    rest = list(split3(factor * mean_ref[...])) + list(split3(factor))
+    rest = [*split3(factor * mean_ref[at]), factor]
     rest += [jnp.zeros_like(factor)] * (SLOTS - 3 * heads - len(rest))
     for t, part in enumerate(rest):
         scratch[pl.ds(3 * heads + t, count, stride=SLOTS), :] = part
-    back = back_ref[...]
-    for group in range(count // GROUP):
-        tile = scratch[group * GROUP * SLOTS : (group + 1) * GROUP * SLOTS]
-        product = dot(jnp.transpose(tile).astype(BF16), back)
-        for g in range(GROUP):
-            i = group * GROUP + g
-            plain = product[:, 2 * g * width : (2 * g + 1) * width]
-            slope = product[:, (2 * g + 1) * width : (2 * g + 2) * width]
-            out_ref[i] = (plain - slope * x_ref[i].astype(F32)).astype(BF16)
-
-
-def fold_kernel(dims, *refs):
+    groups = count // GROUP
+    for group in range(groups):
+        rows = slice(group * columns, (group + 1) * columns)
+        tile = jnp.transpose(scratch[group * GROUP * SLOTS : (group + 1) * GROUP * SLOTS])
+        turned[rows] = tile
+        rounded[rows] = tile.astype(BF16)
+    for g in range(0, GROUP, 2):
+        product = dot(rounded[...], back_ref[:, g * width : (g + 2) * width])
+        for group in range(groups):
+            rows = slice(group * columns, (group + 1) * columns)
+            for s in range(2):
+                i = group * GROUP + g + s
+                lane = (g + s) * SLOTS + 3 * heads + 3
+                slope = turned[rows, lane : lane + 1] * x_ref[low + i].astype(F32)
+                out_ref[i] = (product[rows, s * width : (s + 1) * width] - slope).astype(BF16)
+
+
+def gather_kernel(one, other, total):
+    at = slice(0, total.shape[0])
+    total[...] = one[at].astype(F32) + other[at].astype(F32)
+
+
+def fold_kernel(dims, sums, *refs):
     Z, R, C, rows, parts, width = dims
-    messages, shares = refs[:Z], refs[Z:]
+    messages, refs = refs[:Z], refs[Z:]
+    early, shares = refs[:-R], refs[-R:]
     columns = shares[0].shape[0] // 2
     z, x, c = place_of(dims)
     for b, share in enumerate(shares):
         at = slice(b * columns, (b + 1) * columns)
-        share[0:columns] = sum(m[at].astype(F32) for m in messages).astype(BF16)
+        total = sum(m[at].astype(F32) for a, m in enumerate(messages) if a not in sums)
+        share[0:columns] = sum((m[at] for m in early), total).astype(BF16)
         for part in range(parts):
             plane = ((x ^ b) * C + c) * parts + part
             for a, message in enumerate(messages):
@@ -460,31 +521,27 @@
                     share[columns + part * rows : columns + (part + 1) * rows] = message[R * columns :]
 
 
-def last_kernel(dims, seq_mask_ref, x_ref, gain_ref, token_ref, *refs):
+def last_kernel(dims, scaled_ref, inverse_ref, alive_ref, gain_ref, *refs):
     Z, R, C, rows, parts, width = dims
     shares, refs = refs[:R], refs[R:]
     update_ref, grad_ref, updates, through = refs
-    channels, columns = x_ref.shape[1:]
+    channels, columns = grad_ref.shape[1:]
     x = place_of(dims)[1]
     for b, share in enumerate(shares):
         at = pl.multiple_of((x ^ b) * width, width)
         through[:, pl.ds(at, width)] = share[0:columns].astype(F32)
         updates[:, pl.ds(at, width)] = share[columns:].astype(F32)
-
     mean_matrix = averaging(channels)
-    live = column(token_ref[...].astype(F32), 2 * channels)
-    gain = jnp.concatenate([gain_ref[...].astype(F32)] * 2, axis=1)
-    second_half = iota(live.shape, 1) >= channels
-    for pair in range(x_ref.shape[0] // 2):
+    gain = gain_ref[0:1]
+    for pair in range(grad_ref.shape[0] // 2):
         at = slice(pair * 2 * channels, (pair + 1) * 2 * channels)
+        scaled = scaled_ref[:, at]
         grad = through[:, at] * gain
-        scaled, inverse = normalized(side_by_side(x_ref, pair, channels), mean_matrix)
-        grad = inverse * (
+        grad = inverse_ref[:, at] * (
             grad - average(grad, mean_matrix) - scaled * average(grad * scaled, mean_matrix)
         )
         grad = jnp.transpose(grad).astype(BF16)
-        keep = jnp.where(second_half, seq_mask_ref[2 * pair + 1], seq_mask_ref[2 * pair]).astype(F32)
-        update = jnp.transpose(updates[:, at] * keep * live).astype(BF16)
+        update = jnp.transpose(updates[:, at] * alive_ref[:, at]).astype(BF16)
         for s in range(2):
             at = slice(s * channels, (s + 1) * channels)
             grad_ref[2 * pair + s] = grad[at]
@@ -520,15 +577,14 @@
     by_channel = lambda value: jnp.swapaxes(value, 1, 2)
     alignment_turned = in_hbm(by_channel(alignment_input))
     token_row = in_hbm(token_padding_mask.reshape(1, columns))
-    seq_mask = sequence_mask
-    pair_input = in_hbm(pair_features)
+    seq_mask = in_hbm(sequence_mask.reshape(1, sequences))
     share = shape((2 * columns, width), BF16)
 
-    held = call(
+    kept = shape((columns, sequences * channels), F32)
+    scaled, inverse, alive, wide_gain, *held = call(
         functools.partial(first_kernel, dims),
-        [share] * R,
+        [kept] * 3 + [shape((8, 2 * channels), F32)] + [share] * R,
         "first",
-        scalars=1,
         operands=(seq_mask, alignment_turned, in_hbm(by_channel(update_cotangent)), gain, token_row),
     )
     held = [held[0]] + [exchange(m, dx=b) for b, m in enumerate(held) if b]
@@ -540,9 +596,8 @@
         operands=held,
     )
     if slim:
-        near, far = packed
-        arrived = {0: near, 2: exchange(far, dz=2), 1: exchange(near, dz=1)}
-        arrived[3] = exchange(arrived[2], dz=1)
+        near, away = packed
+        arrived = {0: near, 2: exchange(away, dz=2), 1: exchange(near, dz=1)}
     else:
         arrived, stride = {0: packed[0]}, Z // 2
         while stride:
@@ -553,7 +608,7 @@
         functools.partial(weights_kernel, depth),
         [shape((lanes, hidden * QUAD), BF16)] * 3
         + [shape((GROUP * SLOTS, GROUP * pair_width), BF16)] * 2
-        + [shape((heads, pair_width), F32), shape((GROUP * SLOTS, 2 * GROUP * pair_width), BF16)],
+        + [shape((heads, pair_width), F32), shape((GROUP * SLOTS, GROUP * pair_width), BF16)],
         "weights",
         operands=(
             in_hbm(value_matrix), in_hbm(gate_matrix), in_hbm(output_matrix.T), in_hbm(head_bias_matrix.T),
@@ -561,47 +616,57 @@
         ),
     )
 
-    block = min(32, rows)
-    steps = rows // block
-    whole = pl.BlockSpec(memory_space=pltpu.VMEM)
-    by_row = lambda *tail: pl.BlockSpec((block, *tail), lambda i: (i,) + (0,) * len(tail))
-    by_middle = lambda lead: pl.BlockSpec((lead, block, columns), lambda i: (0, i, 0))
-    exps, stats, logits, means, inverses = call(
-        functools.partial(pair_kernel, heads),
-        [
-            shape((heads + 1, rows, columns), BF16),
+    block = rows // 4
+    cuts = ((0, 3 * block), (3 * block, block))
+    upper, lower, stats, logits, means, inverses = call(
+        functools.partial(pair_kernel, heads, block),
+        [shape((heads, size, columns), BF16) for _, size in cuts]
+        + [
             shape((rows, columns), BF16),
             shape((heads, rows, columns), F32),
             shape((rows, columns), F32),
             shape((rows, columns), F32),
         ],
         "pair",
-        operands=(pair_input, moments, squares, centers, token_row),
-        scratch=[pltpu.VMEM((block * heads, columns), F32)],
-        grid=(steps,),
-        in_specs=[by_row(columns, pair_width)] + [whole] * 3 + [pl.BlockSpec((1, columns), lambda i: (0, 0))],
-        out_specs=[by_middle(heads + 1), by_row(columns), by_middle(heads), by_row(columns), by_row(columns)],
-    )
-    exps = [exps] + [exchange(exps, dx=b) for b in range(1, R)]
-    far = [exchange(stats, dx=b, dc=1) for b in range(R)]
+        operands=(pair_features, moments, squares, centers, token_row),
+        scratch=[pltpu.VMEM((rows * heads, columns), F32)],
+    )
+    (lower,) = call(
+        functools.partial(attach_kernel, heads),
+        [shape((heads + 2 * rows // lower.shape[1], *lower.shape[1:]), BF16)],
+        "attach",
+        operands=(lower, stats, exchange(stats, dc=1)),
+    )
+    exps = [upper, lower]
+    exps = exps + [exchange(e, dx=b) for b in range(1, R) for e in exps]
+    phases = [(2,), (3,), (1, 0)] if slim else [tuple(range(Z))]
+
+    def pick(phase, relays=0, after=()):
+        return call(
+            functools.partial(pick_kernel, dims, slim, len(phase)),
+            [shape((len(phase), 2 * rows, width), BF16)] + [shape((tall, width), BF16)] * relays,
+            "pick",
+            after=after,
+            operands=[arrived[a] for a in phase],
+        )
+
+    first_picked, *relayed = pick(phases[0], relays=int(slim), after=[lower])
+    if slim:
+        arrived[3] = exchange(relayed[0], dz=1)
     probs, scales = call(
         functools.partial(probs_kernel, R, heads),
         [shape((heads, rows, R * columns), BF16), shape((R, rows, columns), F32)],
         "probs",
-        operands=(*exps, *far),
+        operands=exps,
+        after=[first_picked],
     )
 
     values, mixed_grads, outgoing = [], [], {}
-    for phase in [(0, 1, 2), (3,)] if slim else [tuple(range(Z))]:
+    for phase in phases:
         n = len(phase)
         quads = n * width // lanes
         messages = [arrived[a] for a in phase]
-        (picked,) = call(
-            functools.partial(pick_kernel, dims, slim),
-            [shape((n, 2 * rows, width), BF16)],
-            "pick",
-            operands=messages,
-        )
+        picked = first_picked if phase == phases[0] else pick(phase, after=[probs])[0]
         value, mixed_grad, keep, send, partial = call(
             functools.partial(work_kernel, dims, heads),
             [
@@ -612,6 +677,7 @@
                 shape((n, R * columns, width), F32),
             ],
             "work",
+            after=[outgoing[2]] if slim and 3 in phase else [],
             operands=(
                 picked, exchange(picked, dc=1), *messages, probs, spread_value, spread_gate, spread_output,
             ),
@@ -636,40 +702,68 @@
     own_scores, own_total, *scores = call(
         functools.partial(scores_kernel, R, heads, len(values)),
         [shape((heads, rows, columns), F32), shape((rows, columns), BF16)]
-        + [shape((heads + 1, rows, columns), BF16)] * (R - 1),
+        + [shape((heads // 2, rows, columns), BF16)] * (2 * R - 2),
         "scores",
         operands=(*mixed_grads, *values, scales, *exps),
     )
-    scores = [exchange(m, dx=b) for b, m in enumerate(scores, 1)]
-    totals = [own_total] + [exchange(own_total, dx=b, dc=1) for b in range(R)]
-
-    (pair_gradient,) = call(
-        functools.partial(pair_back_kernel, R, heads),
-        [shape(pair_features.shape, BF16)],
-        "pair_back",
-        operands=(
-            pair_input, logits, means, inverses, exps[0], scales, own_scores, back, *scores, *totals,
-        ),
-        scratch=[pltpu.VMEM((block * SLOTS, columns), F32)],
-        grid=(steps,),
-        in_specs=[
-            by_row(columns, pair_width), by_middle(heads), by_row(columns), by_row(columns),
-            by_middle(heads + 1), by_middle(1), by_middle(heads), whole,
-        ]
-        + [by_middle(heads + 1)] * (R - 1)
-        + [by_row(columns)] * (R + 1),
-        out_specs=[by_row(columns, pair_width)],
-    )
+    other_total = exchange(own_total, dc=1)
+    received = []
+    for b in range(1, R):
+        upper, lower = scores[2 * b - 2 : 2 * b]
+        (lower,) = call(
+            functools.partial(attach_total_kernel, heads),
+            [shape((heads // 2 + 1, rows, columns), BF16)],
+            "attach",
+            operands=(lower, own_total, other_total),
+        )
+        received += [exchange(upper, dx=b), exchange(lower, dx=b)]
+    received = [lower, *received]
+
+    def pair_back(index, into=None, after=()):
+        first, part_rows = cuts[index]
+        return call(
+            functools.partial(pair_back_kernel, R, heads, first),
+            [shape(pair_features.shape, BF16), shape((8, 128), F32)],
+            "pair_back",
+            operands=(pair_features, exps[index], logits, means, inverses, scales, own_scores, back, *received),
+            scratch=[
+                pltpu.VMEM((block * SLOTS, columns), F32),
+                pltpu.VMEM((block // GROUP * columns, GROUP * SLOTS), F32),
+                pltpu.VMEM((block // GROUP * columns, GROUP * SLOTS), BF16),
+            ],
+            grid=(part_rows // block,),
+            out_specs=[
+                pl.BlockSpec((block, columns, pair_width), lambda i: (first // block + i, 0, 0)),
+                pl.BlockSpec((8, 128), lambda i: (0, 0)),
+            ],
+            into=into,
+            after=after,
+        )
+
+    sums, early = (), []
+    if slim:
+        sums = (0, 2)
+        early = call(
+            gather_kernel,
+            [shape((R * columns, width), F32)],
+            "gather",
+            operands=[collected[a] for a in sums],
+        )
+    pair_gradient, done = pair_back(0, after=early)
     shares = call(
-        functools.partial(fold_kernel, dims), [share] * R, "fold", operands=collected
-    )
+        functools.partial(fold_kernel, dims, sums),
+        [share] * R,
+        "fold",
+        operands=(*collected, *early),
+        after=[done],
+    )
+    pair_gradient, _ = pair_back(1, into=pair_gradient, after=[shares[0]])
     shares = [shares[0]] + [exchange(m, dx=b) for b, m in enumerate(shares) if b]
     alignment_update, alignment_gradient = call(
         functools.partial(last_kernel, dims),
         [shape(alignment_turned.shape, BF16)] * 2,
         "last",
-        scalars=1,
-        operands=(seq_mask, alignment_turned, gain, token_row, *shares),
+        operands=(scaled, inverse, alive, wide_gain, *shares),
         scratch=[pltpu.VMEM((columns, R * width), F32)] * 2,
     )
     return by_channel(alignment_update), by_channel(alignment_gradient), pair_gradient

time: 69.1 us -> 62 us (0.90)
  waiting for transfers between devices: 22.3 us -> 16.7 us
  Pallas kernels: 27.4 us -> 24.5 us
  starting transfers between devices: 17.6 us -> 19.9 us
    ppermute x18 -> x20, waiting for transfers between devices: 22.3 us -> 16.7 us  [exchange(): lax.ppermute(value, everyone, [(at(z, x, c), at(z ^ dz, x ^ dx, c ^ dc))...]
    pallas_call x15 -> x22, Pallas kernels: 27.4 us -> 24.5 us  [call(): pl.pallas_call(body, out_shape=out_shape, in_specs=[whole] * count + [pl....]
    ppermute x18 -> x20, starting transfers between devices: 17.6 us -> 19.9 us  [exchange(): lax.ppermute(value, everyone, [(at(z, x, c), at(z ^ dz, x ^ dx, c ^ dc))...]
  transfers between devices with their start and end apart: 18 -> 20, of which waited for: 8 -> 5; matrix products, arithmetic and copies ran while one was open for 0% -> 0% of each run, Pallas kernels for 34% -> 35%
where the time goes in v3:
time: 62 us; the launch traced here: 61.9 us
  Pallas kernels  24.5 us (40%)
  starting transfers between devices  19.9 us (32%)
  waiting for transfers between devices  16.7 us (27%)
  between operations  0.85 us (1%)
    pallas_call x22, Pallas kernels, call(): pl.pallas_call(body, out_shape=out_shape, in_specs=[whole] * count + [pl....  24.5 us
    ppermute x20, starting transfers between devices, exchange(): lax.ppermute(value, everyone, [(at(z, x, c), at(z ^ dz, x ^ dx, c ^ dc))...  19.9 us
    ppermute x20, waiting for transfers between devices, exchange(): lax.ppermute(value, everyone, [(at(z, x, c), at(z ^ dz, x ^ dx, c ^ dc))...  16.7 us
  transfers between devices with their start and end apart: 20, of which 5 were waited for; matrix products, arithmetic and copies ran while one was open for 0% of the time, Pallas kernels for 35%

profile of v3, /device:TPU:0, one launch (start us, length us, event | category | flops | bytes accessed | tf_op | source)
XLA Modules:
  0.0 61.9 jit_solution(6473666731989544666)
XLA Ops:
  0.6 1.6 %first.1 = (f32[128,512]{1,0:T(8,128)S(1)}, f32[128,512]{1,0:T(8,128)S(1)}, f32[128,512]{1,0:T(8,128)S(1)}, f32[8,128]{1,0:T(8,128)S(1)}, bf16[256,256]{1,0:T(8,128)(2,1)S(1)}, /*index=5*/bf16[256,256]{1,0:T(8,128)(2,1)S(1)}) custom-call(s32[1,8]{1,0:T(1,128)} %bitcast.16, bf16[8,64,128]{2,1,0:T(8,128)(2,1)} %bitcast.10, bf16[8,64,128]{2,1,0:T(8,128)(2,1)} %bitcast.11, ...), custom_call_target="tpu_custom_call" | custom-call | flops 4499999744 | tf_op jit(solution)/shard_map/first/pallas_call | solution.py:56
  2.2 3.0 %collective-permute-start = (bf16[256,256]{1,0:T(8,128)(2,1)S(1)}, bf16[256,256]{1,0:T(8,128)(2,1)S(1)}, u32[]{:S(2)}, u32[]{:S(2)}) collective-permute-start(bf16[256,256]{1,0:T(8,128)(2,1)S(1)} %get-tuple-element.61), channel_id=1, source_target_pairs={{0,2},{1,3},{2,0},{3,1},{4,6},{5,7},{6,4},{7,5},{8,10},{9,11},{10,... | collective-permute-start | bytes 393224 | tf_op jit(solution)/shard_map/ppermute | solution.py:572
  5.2 0.0 copy-start
  5.2 1.4 %weights.1 = (bf16[256,1024]{1,0:T(8,128)(2,1)S(1)}, bf16[256,1024]{1,0:T(8,128)(2,1)S(1)}, bf16[256,1024]{1,0:T(8,128)(2,1)S(1)}, bf16[128,512]{1,0:T(8,128)(2,...) custom-call(bf16[64,256]{1,0:T(8,128)(2,1)} %refs_0_.4, ...), custom_call_target="tpu_custom_call" | custom-call | flops 3900000000 | tf_op jit(solution)/shard_map/weights/pallas_call | solution.py:56
  6.7 2.1 %collective-permute-done.refs_1_ = bf16[256,256]{1,0:T(8,128)(2,1)S(1)} collective-permute-done((bf16[256,256]{1,0:T(8,128)(2,1)S(1)}, bf16[256,256]{1,0:T(8,128)(2,1)S(1)}, u32[]{:S(2)}, u32[]{:S(2)}) %collective-permute-start) | collective-permute-done | bytes 131104 | tf_op jit(solution)/shard_map/ppermute | solution.py:572
  8.8 2.9 %collective-permute-start.5 = (bf16[384,256]{1,0:T(8,128)(2,1)S(1)}, bf16[384,256]{1,0:T(8,128)(2,1)S(1)}, u32[]{:S(2)}, u32[]{:S(2)}) collective-permute-start(bf16[384,256]{1,0:T(8,128)(2,1)S(1)} %get-tuple-element.69), channel_id=1, source_target_pairs={{0,8},{1,9},{2,10},{3,11},{4,12},{5,13},{6,14},{7,15},{8,0},{9,1},... | collective-permute-start | bytes 589832 | tf_op jit(solution)/shard_map/ppermute | solution.py:572
  11.7 0.0 copy-done
  11.7 4.7 %pair.1 = (bf16[8,96,128]{2,1,0:T(8,128)(2,1)S(1)}, bf16[8,32,128]{2,1,0:T(8,128)(2,1)S(1)}, bf16[128,128]{1,0:T(8,128)(2,1)S(1)}, f32[8,128,128]{2,1,0:T(8,128)...) custom-call(bf16[128,128,128]{2,1,0:T(8,128)(2,1)S(1)} %copy-done, bf16[128,512]{1,0:T(8,128)(2,1)S(1)} %get-tuple-element.63.refs_1_, ...), custom_call_target="tpu_custom_call" | custom-call | flops 15000000512 | tf_op jit(solution)/shard_map/pair/pallas_call | solution.py:56
  16.4 0.1 collective-permute-start.2
  16.5 1.6 %collective-permute-start.3 = (bf16[8,96,128]{2,1,0:T(8,128)(2,1)S(1)}, bf16[8,96,128]{2,1,0:T(8,128)(2,1)S(1)}, u32[]{:S(2)}, u32[]{:S(2)}) collective-permute-start(bf16[8,96,128]{2,1,0:T(8,128)(2,1)S(1)} %get-tuple-element.66.refs_0_.refs_7_.refs_1_), channel_id=1, source_target_pairs={{0,2},{1,3},{2,0},{3,1},{4,6},{5,7},{6,4},{7,5},{8,10},{9,11},{10,... | collective-permute-start | bytes 589832 | tf_op jit(solution)/shard_map/ppermute | solution.py:572
  18.0 0.0 collective-permute-done.2.refs_2_
  18.0 1.2 %collective-permute-start.4 = (bf16[16,32,128]{2,1,0:T(8,128)(2,1)S(1)}, bf16[16,32,128]{2,1,0:T(8,128)(2,1)S(1)}, u32[]{:S(2)}, u32[]{:S(2)}) collective-permute-start(bf16[16,32,128]{2,1,0:T(8,128)(2,1)S(1)} %attach.2.refs_1_.refs_8_), channel_id=1, source_target_pairs={{0,2},{1,3},{2,0},{3,1},{4,6},{5,7},{6,4},{7,5},{8,10},{9,11},{10,... | collective-permute-start | bytes 393224 | tf_op jit(solution)/shard_map/ppermute | solution.py:572
  19.2 1.6 %collective-permute-start.1 = (bf16[384,256]{1,0:T(8,128)(2,1)S(1)}, bf16[384,256]{1,0:T(8,128)(2,1)S(1)}, u32[]{:S(2)}, u32[]{:S(2)}) collective-permute-start(bf16[384,256]{1,0:T(8,128)(2,1)S(1)} %get-tuple-element.62.refs_1_.refs_3_), channel_id=1, source_target_pairs={{0,4},{1,5},{2,6},{3,7},{4,0},{5,1},{6,2},{7,3},{8,12},{9,13},{10,... | collective-permute-start | bytes 589832 | tf_op jit(solution)/shard_map/ppermute | solution.py:572
  20.8 0.0 collective-permute-done.5.refs_0_.refs_2_
  20.8 0.1 collective-permute-start.9
  20.9 0.5 collective-permute-start.12
  21.4 5.2 %collective-permute-done.4.refs_3_.refs_10_ = bf16[16,32,128]{2,1,0:T(8,128)(2,1)S(1)} collective-permute-done((bf16[16,32,128]{2,1,0:T(8,128)(2,1)S(1)}, bf16[16,32,128]{2,1,0:T(8,128)(2,1)S(1)}, u32[]{:S(2)}, u32[]{:S(2)}) %collective-permute-start.4) | collective-permute-done | bytes 131104 | tf_op jit(solution)/shard_map/ppermute | solution.py:572
  26.6 0.0 collective-permute-done.3.refs_2_.refs_9_
  26.6 0.6 probs.1
  27.2 0.0 collective-permute-done.1.refs_0_.refs_2_
  27.2 0.1 collective-permute-start.6
  27.3 0.0 collective-permute-done.9.refs_1_
  27.3 1.3 %work.4 = (bf16[8,256,128]{2,1,0:T(8,128)(2,1)S(1)}, bf16[8,128,128]{2,1,0:T(8,128)(2,1)S(1)}, f32[1,256,256]{2,1,0:T(8,128)S(1)}, bf16[1,256,256]{2,1,0:T(8,128)(2,1)S(1)}, f32[1,256,256]{2,1,0:T(8,128)S(1)}) custom-call(bf16[1,256,256]{2,1,0:T(8,128)(2,1)S(1)} %get-tuple-element.70.refs_4_.refs_0_, ...), custom_call_target="tpu_custom_call" | custom-call | tf_op jit(solution)/shard_map/work/pallas_call | solution.py:56
  28.6 0.5 collective-permute-start.10
  29.1 1.0 %collective-permute-done.12.refs_0_.refs_2_ = bf16[384,256]{1,0:T(8,128)(2,1)S(1)} collective-permute-done((bf16[384,256]{1,0:T(8,128)(2,1)S(1)}, bf16[384,256]{1,0:T(8,128)(2,1)S(1)}, u32[]{:S(2)}, u32[]{:S(2)}) %collective-permute-start.12) | collective-permute-done | bytes 196640 | tf_op jit(solution)/shard_map/ppermute | solution.py:572
  30.1 0.1 collective-permute-start.13
  30.2 0.0 collective-permute-done.6.refs_1_
  30.2 2.4 %work.3 = (bf16[8,256,256]{2,1,0:T(8,128)(2,1)S(1)}, bf16[8,128,256]{2,1,0:T(8,128)(2,1)S(1)}, f32[2,256,256]{2,1,0:T(8,128)S(1)}, bf16[2,256,256]{2,1,0:T(8,128)(2,1)S(1)}, f32[2,256,256]{2,1,0:T(8,128)S(1)}) custom-call(bf16[2,256,256]{2,1,0:T(8,128)(2,1)S(1)} %pick.4.refs_0_, bf16[2,256,256]{2,1,0:T(8,128)(2,1)S(1)} %collective-permute-done.6.refs_1_, ...), custom_call_target="tpu_custom_call" | custom-call | tf_op jit(solution)/shard_map/work/pallas_call | solution.py:56
  32.6 0.5 collective-permute-start.7
  33.2 0.0 collective-permute-done.10.refs_1_
  33.2 0.4 collective-permute-start.11
  33.6 0.0 collective-permute-done.13.refs_1_
  33.6 1.2 %work.5 = (bf16[8,256,128]{2,1,0:T(8,128)(2,1)S(1)}, bf16[8,128,128]{2,1,0:T(8,128)(2,1)S(1)}, f32[1,256,256]{2,1,0:T(8,128)S(1)}, bf16[1,256,256]{2,1,0:T(8,128)(2,1)S(1)}, f32[1,256,256]{2,1,0:T(8,128)S(1)}) custom-call(bf16[1,256,256]{2,1,0:T(8,128)(2,1)S(1)} %pick.5.refs_0_, bf16[1,256,256]{2,1,0:T(8,128)(2,1)S(1)} %collective-permute-done.13.refs_1_, ...), custom_call_target="tpu_custom_call" | custom-call | tf_op jit(solution)/shard_map/work/pallas_call | solution.py:56
  34.9 0.1 collective-permute-start.14
  35.0 1.8 %scores.1 = (f32[8,128,128]{2,1,0:T(8,128)S(1)}, bf16[128,128]{1,0:T(8,128)(2,1)S(1)}, bf16[4,128,128]{2,1,0:T(8,128)(2,1)S(1)}, bf16[4,128,128]{2,1,0:T(8,128)(2,1)S(1)}) custom-call(bf16[8,128,128]{2,1,0:T(8,128)(2,1)S(1)} %get-tuple-element.91.refs_0_, bf16[8,128,128]{2,1,0:T(8,128)(2,1)S(1)} %get-tuple-element.92.refs_1_, ...), custom_call_target="tpu_custom_call" | custom-call | tf_op jit(solution)/shard_map/scores/pallas_call | solution.py:56
  36.8 0.6 collective-permute-start.16
  37.3 1.0 %collective-permute-start.17 = (bf16[4,128,128]{2,1,0:T(8,128)(2,1)S(1)}, bf16[4,128,128]{2,1,0:T(8,128)(2,1)S(1)}, u32[]{:S(2)}, u32[]{:S(2)}) collective-permute-start(bf16[4,128,128]{2,1,0:T(8,128)(2,1)S(1)} %get-tuple-element.101), channel_id=1, source_target_pairs={{0,2},{1,3},{2,0},{3,1},{4,6},{5,7},{6,4},{7,5},{8,10},{9,11},{10,... | collective-permute-start | bytes 393224 | tf_op jit(solution)/shard_map/ppermute | solution.py:572
  38.3 0.0 collective-permute-done.16.refs_2_
  38.3 0.2 attach.3.refs_8_
  38.5 1.1 %collective-permute-start.18 = (bf16[5,128,128]{2,1,0:T(8,128)(2,1)S(1)}, bf16[5,128,128]{2,1,0:T(8,128)(2,1)S(1)}, u32[]{:S(2)}, u32[]{:S(2)}) collective-permute-start(bf16[5,128,128]{2,1,0:T(8,128)(2,1)S(1)} %attach.3.refs_8_), channel_id=1, source_target_pairs={{0,2},{1,3},{2,0},{3,1},{4,6},{5,7},{6,4},{7,5},{8,10},{9,11},{10,... | collective-permute-start | bytes 491528 | tf_op jit(solution)/shard_map/ppermute | solution.py:572
  39.6 0.0 collective-permute-done.14.refs_1_
  39.7 3.6 %collective-permute-start.15 = (bf16[384,256]{1,0:T(8,128)(2,1)S(1)}, bf16[384,256]{1,0:T(8,128)(2,1)S(1)}, u32[]{:S(2)}, u32[]{:S(2)}) collective-permute-start(bf16[384,256]{1,0:T(8,128)(2,1)S(1)} %finish.5), channel_id=1, source_target_pairs={{0,12},{1,13},{2,14},{3,15},{4,8},{5,9},{6,10},{7,11},{8,4},{9,5},... | collective-permute-start | bytes 589832 | tf_op jit(solution)/shard_map/ppermute | solution.py:572
  43.3 0.0 collective-permute-done.7.refs_1_
  43.3 0.3 finish.3
  43.6 0.1 collective-permute-start.8
  43.6 6.8 %collective-permute-done.11.refs_1_.refs_2_ = bf16[384,256]{1,0:T(8,128)(2,1)S(1)} collective-permute-done((bf16[384,256]{1,0:T(8,128)(2,1)S(1)}, bf16[384,256]{1,0:T(8,128)(2,1)S(1)}, u32[]{:S(2)}, u32[]{:S(2)}) %collective-permute-start.11) | collective-permute-done | bytes 196640 | tf_op jit(solution)/shard_map/ppermute | solution.py:572
  50.4 0.0 collective-permute-done.17.refs_9_
  50.5 0.0 collective-permute-done.18.refs_10_
  50.5 5.2 %pair_back.2 = (bf16[128,128,128]{2,1,0:T(8,128)(2,1)}, f32[8,128]{1,0:T(8,128)S(1)}) custom-call(bf16[128,128,128]{2,1,0:T(8,128)(2,1)S(1)} %copy-done, bf16[8,96,128]{2,1,0:T(8,128)(2,1)S(1)} %get-tuple-element.66.refs_0_.refs_7_.refs_1_, f32[8,128,128]{2,1,0:T(8,128)S(1)} %get-tuple-element.87.refs_2_, f32[128,128]{1,0:T(8,128)S(1)} %get-tuple-element.88.refs_3_, ...), custom_call_target="tpu_custom_call" | custom-call | tf_op jit(solution)/shard_map/pair_back/pallas_call | solution.py:56
  55.7 0.0 collective-permute-done.15.refs_3_
  55.7 0.0 collective-permute-done.8.refs_1_
  55.7 0.1 fold.1
  55.7 1.0 %collective-permute-start.19 = (bf16[256,256]{1,0:T(8,128)(2,1)S(1)}, bf16[256,256]{1,0:T(8,128)(2,1)S(1)}, u32[]{:S(2)}, u32[]{:S(2)}) collective-permute-start(bf16[256,256]{1,0:T(8,128)(2,1)S(1)} %get-tuple-element.104), channel_id=1, source_target_pairs={{0,2},{1,3},{2,0},{3,1},{4,6},{5,7},{6,4},{7,5},{8,10},{9,11},{10,... | collective-permute-start | bytes 393224 | tf_op jit(solution)/shard_map/ppermute | solution.py:572
  56.7 2.4 %pair_back.3 = (bf16[128,128,128]{2,1,0:T(8,128)(2,1)}, f32[8,128]{1,0:T(8,128)}) custom-call(bf16[128,128,128]{2,1,0:T(8,128)(2,1)S(1)} %copy-done, bf16[16,32,128]{2,1,0:T(8,128)(2,1)S(1)} %attach.2.refs_1_.refs_8_, f32[8,128,128]{2,1,0:T(8,128)S(1)} %get-tuple-element.87.refs_2_, ...), custom_call_target="tpu_custom_call", output_to_operand_aliasing={{0}: (12, {})} | custom-call | tf_op jit(solution)/shard_map/pair_back/pallas_call | solution.py:56
  59.1 1.7 %collective-permute-done.19.refs_5_ = bf16[256,256]{1,0:T(8,128)(2,1)S(1)} collective-permute-done((bf16[256,256]{1,0:T(8,128)(2,1)S(1)}, bf16[256,256]{1,0:T(8,128)(2,1)S(1)}, u32[]{:S(2)}, u32[]{:S(2)}) %collective-permute-start.19) | collective-permute-done | bytes 131104 | tf_op jit(solution)/shard_map/ppermute | solution.py:572
  60.8 1.1 %last.1 = (bf16[8,64,128]{2,1,0:T(8,128)(2,1)}, bf16[8,64,128]{2,1,0:T(8,128)(2,1)}) custom-call(f32[128,512]{1,0:T(8,128)S(1)} %get-tuple-element.56.refs_0_, f32[128,512]{1,0:T(8,128)S(1)} %get-tuple-element.57.refs_1_, f32[128,512]{1,0:T(8,128)S(1)} %get-tuple-element.58.refs_2_, f32[8,128]{1,0:T(8,128)S(1)} %get-tuple-element.59.refs_3_, ...), custom_call_target="tpu_custom_call" | custom-call | tf_op jit(solution)/shard_map/last/pallas_call | solution.py:56
  (8 shorter events, 0.2 us)
Async XLA Ops:
  2.2 6.5 %collective-permute-start = (bf16[256,256]{1,0:T(8,128)(2,1)S(1)}, bf16[256,256]{1,0:T(8,128)(2,1)S(1)}, u32[]{:S(2)}, u32[]{:S(2)}) collective-permute-start(bf16[256,256]{1,0:T(8,128)(2,1)S(1)} %get-tuple-element.61), channel_id=1, source_target_pairs={{0,2},{1,3},{2,0},{3,1},{4,6},{5,7},{6,4},{7,5},{8,10},{9,11},{10,... | collective-permute-start | bytes 393224 | tf_op jit(solution)/shard_map/ppermute | solution.py:572
  5.2 6.4 %copy-start = (bf16[128,128,128]{2,1,0:T(8,128)(2,1)S(1)}, bf16[128,128,128]{2,1,0:T(8,128)(2,1)}, u32[]{:S(2)}) copy-start(bf16[128,128,128]{2,1,0:T(8,128)(2,1)} %refs_0_.7) | copy-start | bytes 12582916
  8.8 12.0 %collective-permute-start.5 = (bf16[384,256]{1,0:T(8,128)(2,1)S(1)}, bf16[384,256]{1,0:T(8,128)(2,1)S(1)}, u32[]{:S(2)}, u32[]{:S(2)}) collective-permute-start(bf16[384,256]{1,0:T(8,128)(2,1)S(1)} %get-tuple-element.69), channel_id=1, source_target_pairs={{0,8},{1,9},{2,10},{3,11},{4,12},{5,13},{6,14},{7,15},{8,0},{9,1},... | collective-permute-start | bytes 589832 | tf_op jit(solution)/shard_map/ppermute | solution.py:572
  16.4 1.6 %collective-permute-start.2 = (bf16[128,128]{1,0:T(8,128)(2,1)S(1)}, bf16[128,128]{1,0:T(8,128)(2,1)S(1)}, u32[]{:S(2)}, u32[]{:S(2)}) collective-permute-start(bf16[128,128]{1,0:T(8,128)(2,1)S(1)} %get-tuple-element.68.refs_1_), channel_id=1, source_target_pairs={{0,1},{1,0},{2,3},{3,2},{4,5},{5,4},{6,7},{7,6},{8,9},{9,8},{10,11... | collective-permute-start | bytes 98312 | tf_op jit(solution)/shard_map/ppermute | solution.py:572
  16.5 10.1 %collective-permute-start.3 = (bf16[8,96,128]{2,1,0:T(8,128)(2,1)S(1)}, bf16[8,96,128]{2,1,0:T(8,128)(2,1)S(1)}, u32[]{:S(2)}, u32[]{:S(2)}) collective-permute-start(bf16[8,96,128]{2,1,0:T(8,128)(2,1)S(1)} %get-tuple-element.66.refs_0_.refs_7_.refs_1_), channel_id=1, source_target_pairs={{0,2},{1,3},{2,0},{3,1},{4,6},{5,7},{6,4},{7,5},{8,10},{9,11},{10,... | collective-permute-start | bytes 589832 | tf_op jit(solution)/shard_map/ppermute | solution.py:572
  18.0 8.6 %collective-permute-start.4 = (bf16[16,32,128]{2,1,0:T(8,128)(2,1)S(1)}, bf16[16,32,128]{2,1,0:T(8,128)(2,1)S(1)}, u32[]{:S(2)}, u32[]{:S(2)}) collective-permute-start(bf16[16,32,128]{2,1,0:T(8,128)(2,1)S(1)} %attach.2.refs_1_.refs_8_), channel_id=1, source_target_pairs={{0,2},{1,3},{2,0},{3,1},{4,6},{5,7},{6,4},{7,5},{8,10},{9,11},{10,... | collective-permute-start | bytes 393224 | tf_op jit(solution)/shard_map/ppermute | solution.py:572
  19.2 8.0 %collective-permute-start.1 = (bf16[384,256]{1,0:T(8,128)(2,1)S(1)}, bf16[384,256]{1,0:T(8,128)(2,1)S(1)}, u32[]{:S(2)}, u32[]{:S(2)}) collective-permute-start(bf16[384,256]{1,0:T(8,128)(2,1)S(1)} %get-tuple-element.62.refs_1_.refs_3_), channel_id=1, source_target_pairs={{0,4},{1,5},{2,6},{3,7},{4,0},{5,1},{6,2},{7,3},{8,12},{9,13},{10,... | collective-permute-start | bytes 589832 | tf_op jit(solution)/shard_map/ppermute | solution.py:572
  20.8 6.5 %collective-permute-start.9 = (bf16[1,256,256]{2,1,0:T(8,128)(2,1)S(1)}, bf16[1,256,256]{2,1,0:T(8,128)(2,1)S(1)}, u32[]{:S(2)}, u32[]{:S(2)}) collective-permute-start(bf16[1,256,256]{2,1,0:T(8,128)(2,1)S(1)} %get-tuple-element.70.refs_4_.refs_0_), channel_id=1, source_target_pairs={{0,1},{1,0},{2,3},{3,2},{4,5},{5,4},{6,7},{7,6},{8,9},{9,8},{10,11... | collective-permute-start | bytes 393224 | tf_op jit(solution)/shard_map/ppermute | solution.py:572
  20.9 9.2 %collective-permute-start.12 = (bf16[384,256]{1,0:T(8,128)(2,1)S(1)}, bf16[384,256]{1,0:T(8,128)(2,1)S(1)}, u32[]{:S(2)}, u32[]{:S(2)}) collective-permute-start(bf16[384,256]{1,0:T(8,128)(2,1)S(1)} %get-tuple-element.83), channel_id=1, source_target_pairs={{0,4},{1,5},{2,6},{3,7},{4,0},{5,1},{6,2},{7,3},{8,12},{9,13},{10,... | collective-permute-start | bytes 589832 | tf_op jit(solution)/shard_map/ppermute | solution.py:572
  27.2 3.0 %collective-permute-start.6 = (bf16[2,256,256]{2,1,0:T(8,128)(2,1)S(1)}, bf16[2,256,256]{2,1,0:T(8,128)(2,1)S(1)}, u32[]{:S(2)}, u32[]{:S(2)}) collective-permute-start(bf16[2,256,256]{2,1,0:T(8,128)(2,1)S(1)} %pick.4.refs_0_), channel_id=1, source_target_pairs={{0,1},{1,0},{2,3},{3,2},{4,5},{5,4},{6,7},{7,6},{8,9},{9,8},{10,11... | collective-permute-start | bytes 786440 | tf_op jit(solution)/shard_map/ppermute | solution.py:572
  28.6 4.6 %collective-permute-start.10 = (bf16[1,256,256]{2,1,0:T(8,128)(2,1)S(1)}, bf16[1,256,256]{2,1,0:T(8,128)(2,1)S(1)}, u32[]{:S(2)}, u32[]{:S(2)}) collective-permute-start(bf16[1,256,256]{2,1,0:T(8,128)(2,1)S(1)} %get-tuple-element.81), channel_id=1, source_target_pairs={{0,1},{1,0},{2,3},{3,2},{4,5},{5,4},{6,7},{7,6},{8,9},{9,8},{10,11... | collective-permute-start | bytes 393224 | tf_op jit(solution)/shard_map/ppermute | solution.py:572
  30.1 3.5 %collective-permute-start.13 = (bf16[1,256,256]{2,1,0:T(8,128)(2,1)S(1)}, bf16[1,256,256]{2,1,0:T(8,128)(2,1)S(1)}, u32[]{:S(2)}, u32[]{:S(2)}) collective-permute-start(bf16[1,256,256]{2,1,0:T(8,128)(2,1)S(1)} %pick.5.refs_0_), channel_id=1, source_target_pairs={{0,1},{1,0},{2,3},{3,2},{4,5},{5,4},{6,7},{7,6},{8,9},{9,8},{10,11... | collective-permute-start | bytes 393224 | tf_op jit(solution)/shard_map/ppermute | solution.py:572
  32.6 10.6 %collective-permute-start.7 = (bf16[2,256,256]{2,1,0:T(8,128)(2,1)S(1)}, bf16[2,256,256]{2,1,0:T(8,128)(2,1)S(1)}, u32[]{:S(2)}, u32[]{:S(2)}) collective-permute-start(bf16[2,256,256]{2,1,0:T(8,128)(2,1)S(1)} %get-tuple-element.76), channel_id=1, source_target_pairs={{0,1},{1,0},{2,3},{3,2},{4,5},{5,4},{6,7},{7,6},{8,9},{9,8},{10,11... | collective-permute-start | bytes 786440 | tf_op jit(solution)/shard_map/ppermute | solution.py:572
  33.2 17.2 %collective-permute-start.11 = (bf16[384,256]{1,0:T(8,128)(2,1)S(1)}, bf16[384,256]{1,0:T(8,128)(2,1)S(1)}, u32[]{:S(2)}, u32[]{:S(2)}) collective-permute-start(bf16[384,256]{1,0:T(8,128)(2,1)S(1)} %finish.4.refs_7_), channel_id=1, source_target_pairs={{0,8},{1,9},{2,10},{3,11},{4,12},{5,13},{6,14},{7,15},{8,0},{9,1},... | collective-permute-start | bytes 589832 | tf_op jit(solution)/shard_map/ppermute | solution.py:572
  34.9 4.7 %collective-permute-start.14 = (bf16[1,256,256]{2,1,0:T(8,128)(2,1)S(1)}, bf16[1,256,256]{2,1,0:T(8,128)(2,1)S(1)}, u32[]{:S(2)}, u32[]{:S(2)}) collective-permute-start(bf16[1,256,256]{2,1,0:T(8,128)(2,1)S(1)} %get-tuple-element.85), channel_id=1, source_target_pairs={{0,1},{1,0},{2,3},{3,2},{4,5},{5,4},{6,7},{7,6},{8,9},{9,8},{10,11... | collective-permute-start | bytes 393224 | tf_op jit(solution)/shard_map/ppermute | solution.py:572
  36.8 1.5 %collective-permute-start.16 = (bf16[128,128]{1,0:T(8,128)(2,1)S(1)}, bf16[128,128]{1,0:T(8,128)(2,1)S(1)}, u32[]{:S(2)}, u32[]{:S(2)}) collective-permute-start(bf16[128,128]{1,0:T(8,128)(2,1)S(1)} %get-tuple-element.100.refs_1_), channel_id=1, source_target_pairs={{0,1},{1,0},{2,3},{3,2},{4,5},{5,4},{6,7},{7,6},{8,9},{9,8},{10,11... | collective-permute-start | bytes 98312 | tf_op jit(solution)/shard_map/ppermute | solution.py:572
  37.3 13.1 %collective-permute-start.17 = (bf16[4,128,128]{2,1,0:T(8,128)(2,1)S(1)}, bf16[4,128,128]{2,1,0:T(8,128)(2,1)S(1)}, u32[]{:S(2)}, u32[]{:S(2)}) collective-permute-start(bf16[4,128,128]{2,1,0:T(8,128)(2,1)S(1)} %get-tuple-element.101), channel_id=1, source_target_pairs={{0,2},{1,3},{2,0},{3,1},{4,6},{5,7},{6,4},{7,5},{8,10},{9,11},{10,... | collective-permute-start | bytes 393224 | tf_op jit(solution)/shard_map/ppermute | solution.py:572
  38.5 12.0 %collective-permute-start.18 = (bf16[5,128,128]{2,1,0:T(8,128)(2,1)S(1)}, bf16[5,128,128]{2,1,0:T(8,128)(2,1)S(1)}, u32[]{:S(2)}, u32[]{:S(2)}) collective-permute-start(bf16[5,128,128]{2,1,0:T(8,128)(2,1)S(1)} %attach.3.refs_8_), channel_id=1, source_target_pairs={{0,2},{1,3},{2,0},{3,1},{4,6},{5,7},{6,4},{7,5},{8,10},{9,11},{10,... | collective-permute-start | bytes 491528 | tf_op jit(solution)/shard_map/ppermute | solution.py:572
  39.7 16.0 %collective-permute-start.15 = (bf16[384,256]{1,0:T(8,128)(2,1)S(1)}, bf16[384,256]{1,0:T(8,128)(2,1)S(1)}, u32[]{:S(2)}, u32[]{:S(2)}) collective-permute-start(bf16[384,256]{1,0:T(8,128)(2,1)S(1)} %finish.5), channel_id=1, source_target_pairs={{0,12},{1,13},{2,14},{3,15},{4,8},{5,9},{6,10},{7,11},{8,4},{9,5},... | collective-permute-start | bytes 589832 | tf_op jit(solution)/shard_map/ppermute | solution.py:572
  43.6 12.1 %collective-permute-start.8 = (bf16[384,256]{1,0:T(8,128)(2,1)S(1)}, bf16[384,256]{1,0:T(8,128)(2,1)S(1)}, u32[]{:S(2)}, u32[]{:S(2)}) collective-permute-start(bf16[384,256]{1,0:T(8,128)(2,1)S(1)} %get-tuple-element.79), channel_id=1, source_target_pairs={{0,4},{1,5},{2,6},{3,7},{4,0},{5,1},{6,2},{7,3},{8,12},{9,13},{10,... | collective-permute-start | bytes 589832 | tf_op jit(solution)/shard_map/ppermute | solution.py:572
  55.7 5.0 %collective-permute-start.19 = (bf16[256,256]{1,0:T(8,128)(2,1)S(1)}, bf16[256,256]{1,0:T(8,128)(2,1)S(1)}, u32[]{:S(2)}, u32[]{:S(2)}) collective-permute-start(bf16[256,256]{1,0:T(8,128)(2,1)S(1)} %get-tuple-element.104), channel_id=1, source_target_pairs={{0,2},{1,3},{2,0},{3,1},{4,6},{5,7},{6,4},{7,5},{8,10},{9,11},{10,... | collective-permute-start | bytes 393224 | tf_op jit(solution)/shard_map/ppermute | solution.py:572

commit v4 on v3

--- a/solution.py
+++ b/solution.py
@@ -13,7 +13,7 @@
 QUAD = 4
 GROUP = 4
 SLOTS = 32
-COST = dict(first=1.5, pack=0.1, weights=1.3, pair=5, attach=0, pick=1, probs=0, work=0.0, scores=0.0, finish=0, pair_back=0, gather=5, fold=0, last=0)
+COST = dict(first=1.5, pack=0.1, weights=1.3, pair=2.5, attach=0, pick=0, probs=0, prepare=0, work=0.0, scores=0.0, finish=0, pair_back=0, gather=5, settle=5, fold=0, last=0)
 VMEM = 20 * 1024 * 1024
 
 
@@ -216,17 +216,17 @@
         picked[n, rows : 2 * rows] = message[R * columns :] if slim else message[pl.ds(R * columns + at, rows)]
 
 
-def pair_kernel(heads, block, x_ref, moments, squares, centers, token_ref, *refs):
-    e_upper, e_lower, stat_ref, logit_ref, mean_ref, inverse_ref, scratch = refs
-    rows, columns, width = x_ref.shape
-    cut = e_upper.shape[1]
+def pair_kernel(heads, block, first, x_ref, moments, squares, centers, token_ref, *refs):
+    before, refs = refs[:-6], refs[-6:]
+    e_ref, stat_ref, logit_ref, mean_ref, inverse_ref, scratch = refs
+    rows, columns, width = e_ref.shape[1], *x_ref.shape[1:]
     groups = block // GROUP
     padding = 1000000000.0 * (token_ref[...].astype(F32) - 1.0)
     lane = iota((rows, columns), 1)
 
     def step(index, carry):
         low = pl.multiple_of(index * block, block)
-        x = x_ref[pl.ds(low, block)].reshape(groups, GROUP, columns, width)
+        x = x_ref[pl.ds(first + low, block)].reshape(groups, GROUP, columns, width)
         parts, highs, lows = [], [], []
         for g in range(GROUP):
             part = x[:, g].reshape(groups * columns, width)
@@ -273,13 +273,14 @@
         logit = logit + padding
         peak = jnp.max(logit, axis=1, keepdims=True)
         e = jnp.exp(logit - peak).astype(BF16)
-        e_upper[h] = e[:cut]
-        e_lower[h] = e[cut:]
+        e_ref[h] = e
         stats = jnp.where(lane == h, peak, stats)
         stats = jnp.where(lane == 3 * heads + h, dot(e, ones), stats)
     high, middle, rest = split3(stats)
     stats = high + pltpu.roll(middle, heads, 1) + pltpu.roll(rest, 2 * heads, 1)
-    stat_ref[...] = stats.astype(BF16)
+    stat_ref[first:] = stats.astype(BF16)
+    for ref in before:
+        stat_ref[0:first] = ref[...]
 
 
 def thirds(value, heads):
@@ -300,19 +301,15 @@
 def attach_kernel(heads, e_ref, own_ref, other_ref, message):
     size = e_ref.shape[1]
     message[0:heads] = e_ref[...]
-    at = heads
-    for ref in (own_ref, other_ref):
-        for low in range(0, ref.shape[0], size):
-            message[at] = ref[low : low + size]
-            at += 1
+    both = own_ref[...].astype(F32) + pltpu.roll(other_ref[...].astype(F32), own_ref.shape[1] // 2, 1)
+    for n in range(own_ref.shape[0] // size):
+        message[heads + n] = both[n * size : (n + 1) * size].astype(BF16)
 
 
 def attached(message, heads, rows):
-    count = rows // message.shape[1]
-    return [
-        jnp.concatenate([message[at + n] for n in range(count)], axis=0).astype(F32)
-        for at in (heads, heads + count)
-    ]
+    parts = [message[heads + n] for n in range(rows // message.shape[1])]
+    both = jnp.concatenate(parts, axis=0).astype(F32)
+    return [both, pltpu.roll(both, both.shape[1] // 2, 1)]
 
 
 def probs_kernel(R, heads, *refs):
@@ -343,16 +340,13 @@
     return jnp.concatenate([refs[q * per + g][rows] for g in range(per)], axis=1)
 
 
-def work_kernel(dims, heads, mine, other, *refs):
+def prepare_kernel(dims, heads, mine, other, *refs):
     Z, R, C, rows, parts, width = dims
     n = mine.shape[0]
     messages, refs = refs[:n], refs[n:]
-    probs, value_ref, gate_ref, output_ref, *refs = refs
-    values, mixed_grad, keep, send, partial, gathered, gates, grads, turned = refs
-    columns = probs.shape[2] // R
+    value_ref, gate_ref, output_ref, values, mixed_grad, gates, grads, gathered = refs
+    columns = values.shape[1] // R
     lanes, step = value_ref.shape[0], value_ref.shape[1] // heads
-    quads = n * width // lanes
-    per = n // quads
     here, _, _ = rows_place(dims)
 
     @pl.when(here)
@@ -364,7 +358,7 @@
         gathered[...] = other[...]
 
     planes = [gathered.at[a] for a in range(n)]
-    for q in range(quads):
+    for q in range(n * width // lanes):
         at = slice(q * step, (q + 1) * step)
         gate = jax.nn.sigmoid(dot(quad(planes, q, slice(0, rows), lanes), gate_ref[...]))
         grad = dot(quad(planes, q, slice(rows, 2 * rows), lanes), output_ref[...])
@@ -375,6 +369,15 @@
         for h in range(heads):
             mixed_grad[h, :, at] = product[:, h * step : (h + 1) * step]
             values[h, :, at] = tokens[:, h * step : (h + 1) * step]
+
+
+def work_kernel(dims, heads, values, mixed_grad, gates, grads, probs, value_ref, gate_ref, output_ref, *refs):
+    Z, R, C, rows, parts, width = dims
+    keep, send, partial, turned = refs
+    n = partial.shape[0]
+    step = value_ref.shape[1] // heads
+    quads = gates.shape[0]
+    per = n // quads
     for h in range(heads):
         sums = dot_tn(probs[h], mixed_grad[h]).astype(BF16)
         for q in range(quads):
@@ -424,7 +427,10 @@
     lane = iota((rows, columns), 1)
     sums = jnp.zeros((rows, columns), F32)
     for h in range(heads):
-        scores = sum(dot_nt(g[h], v[h]) for g, v in zip(mixed_grads, values))
+        scores = dot_nt(
+            jnp.concatenate([g[h] for g in mixed_grads], axis=1),
+            jnp.concatenate([v[h] for v in values], axis=1),
+        )
         total = 0.0
         for b in range(R):
             part = scores[:, b * columns : (b + 1) * columns]
@@ -461,7 +467,7 @@
     total = sum(m[half, at].astype(F32) for m in (own_total, *seconds))
     total = joined_thirds(total, heads)
     scale = scale_ref[0, at]
-    inverse = inverse_ref[at]
+    inverse = inverse_ref[here]
     cross = 0.0
     for h in range(heads):
         scores = own_ref[h, at]
@@ -469,14 +475,14 @@
             scores = scores + m[h % half, at].astype(F32)
         prob = e_ref[h, here].astype(F32) * scale[:, h : h + 1]
         grad = prob * (scores - total[:, h : h + 1])
-        cross = cross + grad * logit_ref[h, at]
+        cross = cross + grad * logit_ref[h, here]
         scaled = grad * inverse
         high = scaled.astype(BF16).astype(F32)
         scratch[pl.ds(h, count, stride=SLOTS), :] = high
         scratch[pl.ds(heads + h, count, stride=SLOTS), :] = high
         scratch[pl.ds(2 * heads + h, count, stride=SLOTS), :] = scaled - high
     factor = inverse * inverse * cross * (1.0 / width)
-    rest = [*split3(factor * mean_ref[at]), factor]
+    rest = [*split3(factor * mean_ref[here]), factor]
     rest += [jnp.zeros_like(factor)] * (SLOTS - 3 * heads - len(rest))
     for t, part in enumerate(rest):
         scratch[pl.ds(3 * heads + t, count, stride=SLOTS), :] = part
@@ -497,6 +503,10 @@
                 out_ref[i] = (product[rows, s * width : (s + 1) * width] - slope).astype(BF16)
 
 
+def settle_kernel(out):
+    out[...] = jnp.zeros_like(out)
+
+
 def gather_kernel(one, other, total):
     at = slice(0, total.shape[0])
     total[...] = one[at].astype(F32) + other[at].astype(F32)
@@ -587,22 +597,18 @@
         "first",
         operands=(seq_mask, alignment_turned, in_hbm(by_channel(update_cotangent)), gain, token_row),
     )
+    first_kept = held[0]
     held = [held[0]] + [exchange(m, dx=b) for b, m in enumerate(held) if b]
     tall = R * columns + (rows if slim else R * columns)
-    packed = call(
-        functools.partial(pack_kernel, dims, slim),
-        [shape((tall, width), BF16)] * (2 if slim else 1),
-        "pack",
-        operands=held,
-    )
-    if slim:
-        near, away = packed
-        arrived = {0: near, 2: exchange(away, dz=2), 1: exchange(near, dz=1)}
-    else:
-        arrived, stride = {0: packed[0]}, Z // 2
-        while stride:
-            arrived |= {a ^ stride: exchange(m, dz=stride) for a, m in arrived.items()}
-            stride //= 2
+
+    def pack(after):
+        return call(
+            functools.partial(pack_kernel, dims, slim),
+            [shape((tall, width), BF16)] * (2 if slim else 1),
+            "pack",
+            operands=held,
+            after=after,
+        )
 
     spread_value, spread_gate, spread_output, moments, squares, centers, back = call(
         functools.partial(weights_kernel, depth),
@@ -617,29 +623,48 @@
     )
 
     block = rows // 4
-    cuts = ((0, 3 * block), (3 * block, block))
-    upper, lower, stats, logits, means, inverses = call(
-        functools.partial(pair_kernel, heads, block),
-        [shape((heads, size, columns), BF16) for _, size in cuts]
-        + [
-            shape((rows, columns), BF16),
-            shape((heads, rows, columns), F32),
-            shape((rows, columns), F32),
-            shape((rows, columns), F32),
-        ],
-        "pair",
-        operands=(pair_features, moments, squares, centers, token_row),
-        scratch=[pltpu.VMEM((rows * heads, columns), F32)],
-    )
+    cuts = ((0, 2 * block), (2 * block, 2 * block))
+    def pair(index, before=(), after=()):
+        first, size = cuts[index]
+        return call(
+            functools.partial(pair_kernel, heads, block, first),
+            [
+                shape((heads, size, columns), BF16),
+                shape((first + size, columns), BF16),
+                shape((heads, size, columns), F32),
+                shape((size, columns), F32),
+                shape((size, columns), F32),
+            ],
+            "pair",
+            operands=(pair_features, moments, squares, centers, token_row, *before),
+            scratch=[pltpu.VMEM((size * heads, columns), F32)],
+            after=after,
+        )
+
+    upper, stats, *upper_kept = pair(0, after=[first_kept])
+    packed = pack(after=[stats])
+    if slim:
+        near, away = packed
+        arrived = {0: near, 2: exchange(away, dz=2), 1: exchange(near, dz=1)}
+    else:
+        arrived, stride = {0: packed[0]}, Z // 2
+        while stride:
+            arrived |= {a ^ stride: exchange(m, dz=stride) for a, m in arrived.items()}
+            stride //= 2
+    lower, stats, *lower_kept = pair(1, before=[stats], after=packed[:1])
+    forward = [(upper, *upper_kept), (lower, *lower_kept)]
+    uppers = [upper] + [exchange(upper, dx=b) for b in range(1, R)]
     (lower,) = call(
         functools.partial(attach_kernel, heads),
-        [shape((heads + 2 * rows // lower.shape[1], *lower.shape[1:]), BF16)],
+        [shape((heads + rows // lower.shape[1], *lower.shape[1:]), BF16)],
         "attach",
         operands=(lower, stats, exchange(stats, dc=1)),
-    )
-    exps = [upper, lower]
-    exps = exps + [exchange(e, dx=b) for b in range(1, R) for e in exps]
-    phases = [(2,), (3,), (1, 0)] if slim else [tuple(range(Z))]
+        after=uppers[1:],
+    )
+    lowers = [lower] + [exchange(lower, dx=b) for b in range(1, R)]
+    exps = [e for pair_of in zip(uppers, lowers) for e in pair_of]
+    phases = [(2,), (0,), (1,), (3,)] if slim else [tuple(range(Z))]
+    prepared, unfinished, outgoing = {}, {}, {}
 
     def pick(phase, relays=0, after=()):
         return call(
@@ -650,61 +675,86 @@
             operands=[arrived[a] for a in phase],
         )
 
-    first_picked, *relayed = pick(phases[0], relays=int(slim), after=[lower])
+    def prepare(phase, picked, after=()):
+        n = len(phase)
+        quads = n * width // lanes
+        prepared[phase] = call(
+            functools.partial(prepare_kernel, dims, heads),
+            [
+                shape((heads, R * columns, quads * step), BF16),
+                shape((heads, rows, quads * step), BF16),
+                shape((quads, rows, heads * step), F32),
+                shape((quads, rows, heads * step), F32),
+            ],
+            "prepare",
+            operands=(
+                picked, exchange(picked, dc=1), *[arrived[a] for a in phase],
+                spread_value, spread_gate, spread_output,
+            ),
+            scratch=[pltpu.VMEM((n, 2 * rows, width), BF16)],
+            after=after,
+        )
+
+    def work(phase, after=()):
+        n = len(phase)
+        keep, send, partial = call(
+            functools.partial(work_kernel, dims, heads),
+            [
+                shape((n, 2 * rows, width), F32),
+                shape((n, 2 * rows, width), BF16),
+                shape((n, R * columns, width), F32),
+            ],
+            "work",
+            operands=(*prepared[phase], probs, spread_value, spread_gate, spread_output),
+            scratch=[pltpu.VMEM((n * width // lanes, R * columns, heads * step), BF16)],
+            after=after,
+        )
+        unfinished[phase] = keep, exchange(send, dc=1), partial
+
+    def finish(phase, after=()):
+        finished = call(
+            functools.partial(finish_kernel, dims),
+            [shape((R * columns + rows, width), BF16)] * len(phase),
+            "finish",
+            operands=unfinished[phase],
+            after=after,
+        )
+        outgoing.update(zip(phase, finished))
+
+    early_phases = phases[:3]
+    first_picked, *relayed = pick(phases[0], relays=int(slim), after=[lower, *arrived.values()][:3 if slim else 1])
+    prepare(phases[0], first_picked)
     if slim:
         arrived[3] = exchange(relayed[0], dz=1)
+    for phase in early_phases[1:]:
+        prepare(phase, *pick(phase, after=[first_picked]))
     probs, scales = call(
         functools.partial(probs_kernel, R, heads),
         [shape((heads, rows, R * columns), BF16), shape((R, rows, columns), F32)],
         "probs",
         operands=exps,
-        after=[first_picked],
-    )
-
-    values, mixed_grads, outgoing = [], [], {}
-    for phase in phases:
-        n = len(phase)
-        quads = n * width // lanes
-        messages = [arrived[a] for a in phase]
-        picked = first_picked if phase == phases[0] else pick(phase, after=[probs])[0]
-        value, mixed_grad, keep, send, partial = call(
-            functools.partial(work_kernel, dims, heads),
-            [
-                shape((heads, R * columns, quads * step), BF16),
-                shape((heads, rows, quads * step), BF16),
-                shape((n, 2 * rows, width), F32),
-                shape((n, 2 * rows, width), BF16),
-                shape((n, R * columns, width), F32),
-            ],
-            "work",
-            after=[outgoing[2]] if slim and 3 in phase else [],
-            operands=(
-                picked, exchange(picked, dc=1), *messages, probs, spread_value, spread_gate, spread_output,
-            ),
-            scratch=[
-                pltpu.VMEM((n, 2 * rows, width), BF16),
-                pltpu.VMEM((quads, rows, heads * step), F32),
-                pltpu.VMEM((quads, rows, heads * step), F32),
-                pltpu.VMEM((quads, R * columns, heads * step), BF16),
-            ],
-        )
-        values.append(value)
-        mixed_grads.append(mixed_grad)
-        finished = call(
-            functools.partial(finish_kernel, dims),
-            [shape((R * columns + rows, width), BF16)] * n,
-            "finish",
-            operands=(keep, exchange(send, dc=1), partial),
-        )
-        outgoing |= dict(zip(phase, finished))
-    collected = [exchange(outgoing[a], dz=a) if a else outgoing[a] for a in range(Z)]
+        after=[prepared[phase][1] for phase in early_phases],
+    )
+
+    work(phases[0])
+    if slim:
+        work((1,))
+        finish((2,), after=[unfinished[(1,)][2]])
+        (picked,) = pick((3,), after=[outgoing[2]])
+        work((0,), after=[picked])
+        prepare((3,), picked, after=[unfinished[(0,)][2]])
+    else:
+        finish(phases[0])
 
     own_scores, own_total, *scores = call(
-        functools.partial(scores_kernel, R, heads, len(values)),
+        functools.partial(scores_kernel, R, heads, len(prepared)),
         [shape((heads, rows, columns), F32), shape((rows, columns), BF16)]
         + [shape((heads // 2, rows, columns), BF16)] * (2 * R - 2),
         "scores",
-        operands=(*mixed_grads, *values, scales, *exps),
+        after=[],
+        operands=(
+            *[p[1] for p in prepared.values()], *[p[0] for p in prepared.values()], scales, *exps,
+        ),
     )
     other_total = exchange(own_total, dc=1)
     received = []
@@ -717,7 +767,13 @@
             operands=(lower, own_total, other_total),
         )
         received += [exchange(upper, dx=b), exchange(lower, dx=b)]
+    if slim:
+        work((3,), after=[])
+        finish((3,))
+        finish((1,), after=[unfinished[(3,)][2]])
+        finish((0,))
     received = [lower, *received]
+    collected = [exchange(outgoing[a], dz=a) if a else outgoing[a] for a in range(Z)]
 
     def pair_back(index, into=None, after=()):
         first, part_rows = cuts[index]
@@ -725,7 +781,7 @@
             functools.partial(pair_back_kernel, R, heads, first),
             [shape(pair_features.shape, BF16), shape((8, 128), F32)],
             "pair_back",
-            operands=(pair_features, exps[index], logits, means, inverses, scales, own_scores, back, *received),
+            operands=(pair_features, *forward[index], scales, own_scores, back, *received),
             scratch=[
                 pltpu.VMEM((block * SLOTS, columns), F32),
                 pltpu.VMEM((block // GROUP * columns, GROUP * SLOTS), F32),
@@ -749,7 +805,8 @@
             "gather",
             operands=[collected[a] for a in sums],
         )
-    pair_gradient, done = pair_back(0, after=early)
+    settled = call(settle_kernel, [shape((8, 128), F32)], "settle", operands=[], after=received[1:])
+    pair_gradient, done = pair_back(0, after=[*settled, *early])
     shares = call(
         functools.partial(fold_kernel, dims, sums),
         [share] * R,

time: 62 us -> 58.1 us (0.937)
  waiting for transfers between devices: 16.7 us -> 7.22 us
  starting transfers between devices: 19.9 us -> 22.4 us
  Pallas kernels: 24.5 us -> 26.6 us
  local copies, waits for them, and re-layouts: 0.01 us -> 0.83 us
    ppermute x20 -> x22, waiting for transfers between devices: 16.7 us -> 7.22 us  [exchange(): lax.ppermute(value, everyone, [(at(z, x, c), at(z ^ dz, x ^ dx, c ^ dc))...]
    ppermute x20 -> x22, starting transfers between devices: 19.9 us -> 22.4 us  [exchange(): lax.ppermute(value, everyone, [(at(z, x, c), at(z ^ dz, x ^ dx, c ^ dc))...]
    pallas_call x22 -> x31, Pallas kernels: 24.5 us -> 26.6 us  [call(): pl.pallas_call(body, out_shape=out_shape, in_specs=[whole] * count + [pl....]
    unnamed x2, local copies, waits for them, and re-layouts: 0.01 us -> 0.83 us
  transfers between devices with their start and end apart: 20 -> 22, of which waited for: 5 -> 7; matrix products, arithmetic and copies ran while one was open for 0% -> 0% of each run, Pallas kernels for 35% -> 41%
where the time goes in v4:
time: 58.1 us; the launch traced here: 57.9 us
  Pallas kernels  26.6 us (46%)
  starting transfers between devices  22.4 us (39%)
  waiting for transfers between devices  7.22 us (12%)
  between operations  0.9 us (2%)
  local copies, waits for them, and re-layouts  0.83 us (1%)
    pallas_call x31, Pallas kernels, call(): pl.pallas_call(body, out_shape=out_shape, in_specs=[whole] * count + [pl....  26.6 us
    ppermute x22, starting transfers between devices, exchange(): lax.ppermute(value, everyone, [(at(z, x, c), at(z ^ dz, x ^ dx, c ^ dc))...  22.4 us
    ppermute x22, waiting for transfers between devices, exchange(): lax.ppermute(value, everyone, [(at(z, x, c), at(z ^ dz, x ^ dx, c ^ dc))...  7.22 us
  transfers between devices with their start and end apart: 22, of which 7 were waited for; matrix products, arithmetic and copies ran while one was open for 0% of the time, Pallas kernels for 41%

profile of v4, /device:TPU:0, one launch (start us, length us, event | category | flops | bytes accessed | tf_op | source)
XLA Modules:
  0.0 57.9 jit_solution(873703493799728277)
XLA Ops:
  0.6 1.6 %first.1 = (f32[128,512]{1,0:T(8,128)S(1)}, f32[128,512]{1,0:T(8,128)S(1)}, f32[128,512]{1,0:T(8,128)S(1)}, f32[8,128]{1,0:T(8,128)S(1)}, bf16[256,256]{1,0:T(8,128)(2,1)S(1)}, /*index=5*/bf16[256,256]{1,0:T(8,128)(2,1)S(1)}) custom-call(s32[1,8]{1,0:T(1,128)} %bitcast.16, bf16[8,64,128]{2,1,0:T(8,128)(2,1)} %bitcast.10, bf16[8,64,128]{2,1,0:T(8,128)(2,1)} %bitcast.11, ...), custom_call_target="tpu_custom_call" | custom-call | flops 4499999744 | tf_op jit(solution)/shard_map/first/pallas_call | solution.py:56
  2.2 3.0 %collective-permute-start = (bf16[256,256]{1,0:T(8,128)(2,1)S(1)}, bf16[256,256]{1,0:T(8,128)(2,1)S(1)}, u32[]{:S(2)}, u32[]{:S(2)}) collective-permute-start(bf16[256,256]{1,0:T(8,128)(2,1)S(1)} %get-tuple-element.76), channel_id=1, source_target_pairs={{0,2},{1,3},{2,0},{3,1},{4,6},{5,7},{6,4},{7,5},{8,10},{9,11},{10,... | collective-permute-start | bytes 393224 | tf_op jit(solution)/shard_map/ppermute | solution.py:582
  5.3 1.4 %weights.1 = (bf16[256,1024]{1,0:T(8,128)(2,1)S(1)}, bf16[256,1024]{1,0:T(8,128)(2,1)S(1)}, bf16[256,1024]{1,0:T(8,128)(2,1)S(1)}, bf16[128,512]{1,0:T(8,128)(2,...) custom-call(bf16[64,256]{1,0:T(8,128)(2,1)} %refs_0_.5, ...), custom_call_target="tpu_custom_call" | custom-call | flops 3900000000 | tf_op jit(solution)/shard_map/weights/pallas_call | solution.py:56
  6.7 0.8 %copy-done = bf16[128,128,128]{2,1,0:T(8,128)(2,1)S(1)} copy-done((bf16[128,128,128]{2,1,0:T(8,128)(2,1)S(1)}, bf16[128,128,128]{2,1,0:T(8,128)(2,1)}, u32[]{:S(2)}) %copy-start) | copy-done | bytes 4194328
  7.5 2.9 %pair.2 = (bf16[8,64,128]{2,1,0:T(8,128)(2,1)S(1)}, bf16[64,128]{1,0:T(8,128)(2,1)S(1)}, f32[8,64,128]{2,1,0:T(8,128)S(1)}, f32[64,128]{1,0:T(8,128)S(1)}, f32[64,128]{1,0:T(8,128)S(1)}) custom-call(bf16[128,128,128]{2,1,0:T(8,128)(2,1)S(1)} %copy-done, bf16[128,512]{1,0:T(8,128)(2,1)S(1)} %get-tuple-element.77.refs_1_, ...), custom_call_target="tpu_custom_call" | custom-call | flops 7500000256 | tf_op jit(solution)/shard_map/pair/pallas_call | solution.py:56
  10.4 0.1 collective-permute-start.3
  10.5 0.0 collective-permute-done.refs_1_
  10.6 3.2 %collective-permute-start.1 = (bf16[384,256]{1,0:T(8,128)(2,1)S(1)}, bf16[384,256]{1,0:T(8,128)(2,1)S(1)}, u32[]{:S(2)}, u32[]{:S(2)}) collective-permute-start(bf16[384,256]{1,0:T(8,128)(2,1)S(1)} %get-tuple-element.82), channel_id=1, source_target_pairs={{0,8},{1,9},{2,10},{3,11},{4,12},{5,13},{6,14},{7,15},{8,0},{9,1},... | collective-permute-start | bytes 589832 | tf_op jit(solution)/shard_map/ppermute | solution.py:582
  13.7 1.6 %collective-permute-start.7 = (bf16[384,256]{1,0:T(8,128)(2,1)S(1)}, bf16[384,256]{1,0:T(8,128)(2,1)S(1)}, u32[]{:S(2)}, u32[]{:S(2)}) collective-permute-start(bf16[384,256]{1,0:T(8,128)(2,1)S(1)} %get-tuple-element.81.refs_6_.refs_2_.refs_0_), channel_id=1, source_target_pairs={{0,4},{1,5},{2,6},{3,7},{4,0},{5,1},{6,2},{7,3},{8,12},{9,13},{10,... | collective-permute-start | bytes 589832 | tf_op jit(solution)/shard_map/ppermute | solution.py:582
  15.3 2.9 %pair.3 = (bf16[8,64,128]{2,1,0:T(8,128)(2,1)S(1)}, bf16[128,128]{1,0:T(8,128)(2,1)S(1)}, f32[8,64,128]{2,1,0:T(8,128)S(1)}, f32[64,128]{1,0:T(8,128)S(1)}, f32[64,128]{1,0:T(8,128)S(1)}) custom-call(bf16[128,128,128]{2,1,0:T(8,128)(2,1)S(1)} %copy-done, bf16[128,512]{1,0:T(8,128)(2,1)S(1)} %get-tuple-element.77.refs_1_, ...), custom_call_target="tpu_custom_call" | custom-call | flops 7500000256 | tf_op jit(solution)/shard_map/pair/pallas_call | solution.py:56
  18.3 0.1 collective-permute-start.2
  18.3 0.0 collective-permute-done.3.refs_3_.refs_2_.refs_11_
  18.3 1.2 %collective-permute-done.2.refs_2_ = bf16[128,128]{1,0:T(8,128)(2,1)S(1)} collective-permute-done((bf16[128,128]{1,0:T(8,128)(2,1)S(1)}, bf16[128,128]{1,0:T(8,128)(2,1)S(1)}, u32[]{:S(2)}, u32[]{:S(2)}) %collective-permute-start.2) | collective-permute-done | bytes 32800 | tf_op jit(solution)/shard_map/ppermute | solution.py:582
  19.5 0.1 attach.2.refs_1_.refs_10_
  19.6 1.6 %collective-permute-start.5 = (bf16[10,64,128]{2,1,0:T(8,128)(2,1)S(1)}, bf16[10,64,128]{2,1,0:T(8,128)(2,1)S(1)}, u32[]{:S(2)}, u32[]{:S(2)}) collective-permute-start(bf16[10,64,128]{2,1,0:T(8,128)(2,1)S(1)} %attach.2.refs_1_.refs_10_), channel_id=1, source_target_pairs={{0,2},{1,3},{2,0},{3,1},{4,6},{5,7},{6,4},{7,5},{8,10},{9,11},{10,... | collective-permute-start | bytes 491528 | tf_op jit(solution)/shard_map/ppermute | solution.py:582
  21.2 1.2 %collective-permute-done.1.refs_0_.refs_3_.refs_2_ = bf16[384,256]{1,0:T(8,128)(2,1)S(1)} collective-permute-done((bf16[384,256]{1,0:T(8,128)(2,1)S(1)}, bf16[384,256]{1,0:T(8,128)(2,1)S(1)}, u32[]{:S(2)}, u32[]{:S(2)}) %collective-permute-start.1) | collective-permute-done | bytes 196640 | tf_op jit(solution)/shard_map/ppermute | solution.py:582
  22.5 0.1 collective-permute-start.4
  22.5 0.5 collective-permute-start.6
  23.0 0.0 collective-permute-done.7.refs_0_.refs_2_
  23.1 0.1 collective-permute-start.8
  23.2 1.0 %collective-permute-start.9 = (bf16[384,256]{1,0:T(8,128)(2,1)S(1)}, bf16[384,256]{1,0:T(8,128)(2,1)S(1)}, u32[]{:S(2)}, u32[]{:S(2)}) collective-permute-start(bf16[384,256]{1,0:T(8,128)(2,1)S(1)} %get-tuple-element.97), channel_id=1, source_target_pairs={{0,4},{1,5},{2,6},{3,7},{4,0},{5,1},{6,2},{7,3},{8,12},{9,13},{10,... | collective-permute-start | bytes 589832 | tf_op jit(solution)/shard_map/ppermute | solution.py:582
  24.2 0.0 collective-permute-done.4.refs_1_
  24.2 0.5 prepare.4
  24.7 0.0 collective-permute-done.6.refs_1_
  24.7 0.5 prepare.5
  25.2 0.0 collective-permute-done.8.refs_1_
  25.2 0.5 prepare.6
  25.7 0.2 collective-permute-done.5.refs_3_.refs_12_
  25.9 0.6 %probs.1 = (bf16[8,128,256]{2,1,0:T(8,128)(2,1)S(1)}, f32[2,128,128]{2,1,0:T(8,128)S(1)}) custom-call(bf16[8,64,128]{2,1,0:T(8,128)(2,1)S(1)} %get-tuple-element.85.refs_0_.refs_9_.refs_1_, bf16[10,64,128]{2,1,0:T(8,128)(2,1)S(1)} %attach.2.refs_1_.refs_10_, bf16[8,64,128]{2,1,0:T(8,128)(2,1)S(1)} %collective-permute-done.3.refs_3_.refs_2_.refs_11_, ...), custom_call_target="tpu_custom_call" | custom-call | tf_op jit(solution)/shard_map/probs/pallas_call | solution.py:56
  26.6 1.0 %work.4 = (f32[1,256,256]{2,1,0:T(8,128)S(1)}, bf16[1,256,256]{2,1,0:T(8,128)(2,1)S(1)}, f32[1,256,256]{2,1,0:T(8,128)S(1)}) custom-call(bf16[8,256,128]{2,1,0:T(8,128)(2,1)S(1)} %get-tuple-element.98.refs_0_.refs_4_, bf16[8,128,128]{2,1,0:T(8,128)(2,1)S(1)} %get-tuple-element.94.refs_4_.refs_1_.refs_0_, f32[1,128,1024]{2,1,0:T(8,128)S(1)} %get-tuple-element.99.refs_2_, ...), custom_call_target="tpu_custom_call" | custom-call | tf_op jit(solution)/shard_map/work/pallas_call | solution.py:56
  27.5 0.1 collective-permute-start.10
  27.6 1.0 %work.5 = (f32[1,256,256]{2,1,0:T(8,128)S(1)}, bf16[1,256,256]{2,1,0:T(8,128)(2,1)S(1)}, f32[1,256,256]{2,1,0:T(8,128)S(1)}) custom-call(bf16[8,256,128]{2,1,0:T(8,128)(2,1)S(1)} %get-tuple-element.104.refs_0_.refs_6_, bf16[8,128,128]{2,1,0:T(8,128)(2,1)S(1)} %get-tuple-element.95.refs_6_.refs_1_.refs_2_, f32[1,128,1024]{2,1,0:T(8,128)S(1)} %get-tuple-element.105.refs_2_, ...), custom_call_target="tpu_custom_call" | custom-call | tf_op jit(solution)/shard_map/work/pallas_call | solution.py:56
  28.6 0.4 collective-permute-done.10.refs_1_
  29.0 2.8 %collective-permute-start.15 = (bf16[384,256]{1,0:T(8,128)(2,1)S(1)}, bf16[384,256]{1,0:T(8,128)(2,1)S(1)}, u32[]{:S(2)}, u32[]{:S(2)}) collective-permute-start(bf16[384,256]{1,0:T(8,128)(2,1)S(1)} %finish.4.refs_1_), channel_id=1, source_target_pairs={{0,8},{1,9},{2,10},{3,11},{4,12},{5,13},{6,14},{7,15},{8,0},{9,1},... | collective-permute-start | bytes 589832 | tf_op jit(solution)/shard_map/ppermute | solution.py:582
  31.8 0.0 collective-permute-done.9.refs_0_.refs_2_
  31.8 0.1 collective-permute-start.13
  31.9 0.5 collective-permute-start.12
  32.4 1.0 %work.6 = (f32[1,256,256]{2,1,0:T(8,128)S(1)}, bf16[1,256,256]{2,1,0:T(8,128)(2,1)S(1)}, f32[1,256,256]{2,1,0:T(8,128)S(1)}) custom-call(bf16[8,256,128]{2,1,0:T(8,128)(2,1)S(1)} %get-tuple-element.90.refs_0_.refs_5_, bf16[8,128,128]{2,1,0:T(8,128)(2,1)S(1)} %get-tuple-element.91.refs_5_.refs_1_, f32[1,128,1024]{2,1,0:T(8,128)S(1)} %get-tuple-element.92.refs_2_, ...), custom_call_target="tpu_custom_call" | custom-call | tf_op jit(solution)/shard_map/work/pallas_call | solution.py:56
  33.4 0.1 collective-permute-start.11
  33.5 0.0 collective-permute-done.13.refs_1_
  33.5 0.6 %prepare.7 = (bf16[8,256,128]{2,1,0:T(8,128)(2,1)S(1)}, bf16[8,128,128]{2,1,0:T(8,128)(2,1)S(1)}, f32[1,128,1024]{2,1,0:T(8,128)S(1)}, f32[1,128,1024]{2,1,0:T(8,128)S(1)}) custom-call(bf16[1,256,256]{2,1,0:T(8,128)(2,1)S(1)} %pick.7.refs_8_.refs_0_, bf16[1,256,256]{2,1,0:T(8,128)(2,1)S(1)} %collective-permute-done.13.refs_1_, ...), custom_call_target="tpu_custom_call" | custom-call | tf_op jit(solution)/shard_map/prepare/pallas_call | solution.py:56
  34.2 1.8 %scores.1 = (f32[8,128,128]{2,1,0:T(8,128)S(1)}, bf16[128,128]{1,0:T(8,128)(2,1)S(1)}, bf16[4,128,128]{2,1,0:T(8,128)(2,1)S(1)}, bf16[4,128,128]{2,1,0:T(8,128)(2,1)S(1)}) custom-call(bf16[8,128,128]{2,1,0:T(8,128)(2,1)S(1)} %get-tuple-element.94.refs_4_.refs_1_.refs_0_, bf16[8,128,128]{2,1,0:T(8,128)(2,1)S(1)} %get-tuple-element.91.refs_5_.refs_1_, ...), custom_call_target="tpu_custom_call" | custom-call | tf_op jit(solution)/shard_map/scores/pallas_call | solution.py:56
  36.0 0.5 collective-permute-start.18
  36.5 1.0 %work.7 = (f32[1,256,256]{2,1,0:T(8,128)S(1)}, bf16[1,256,256]{2,1,0:T(8,128)(2,1)S(1)}, f32[1,256,256]{2,1,0:T(8,128)S(1)}) custom-call(bf16[8,256,128]{2,1,0:T(8,128)(2,1)S(1)} %get-tuple-element.113.refs_0_.refs_7_, bf16[8,128,128]{2,1,0:T(8,128)(2,1)S(1)} %get-tuple-element.114.refs_1_.refs_3_, f32[1,128,1024]{2,1,0:T(8,128)S(1)} %get-tuple-element.115.refs_2_, ...), custom_call_target="tpu_custom_call" | custom-call | tf_op jit(solution)/shard_map/work/pallas_call | solution.py:56
  37.4 0.0 collective-permute-done.12.refs_1_
  37.5 0.1 finish.6
  37.5 0.7 %collective-permute-start.14 = (bf16[384,256]{1,0:T(8,128)(2,1)S(1)}, bf16[384,256]{1,0:T(8,128)(2,1)S(1)}, u32[]{:S(2)}, u32[]{:S(2)}) collective-permute-start(bf16[384,256]{1,0:T(8,128)(2,1)S(1)} %finish.6), channel_id=1, source_target_pairs={{0,4},{1,5},{2,6},{3,7},{4,0},{5,1},{6,2},{7,3},{8,12},{9,13},{10,... | collective-permute-start | bytes 589832 | tf_op jit(solution)/shard_map/ppermute | solution.py:582
  38.2 0.0 collective-permute-start.16
  38.2 0.0 collective-permute-done.11.refs_1_
  38.2 1.5 %collective-permute-start.19 = (bf16[4,128,128]{2,1,0:T(8,128)(2,1)S(1)}, bf16[4,128,128]{2,1,0:T(8,128)(2,1)S(1)}, u32[]{:S(2)}, u32[]{:S(2)}) collective-permute-start(bf16[4,128,128]{2,1,0:T(8,128)(2,1)S(1)} %get-tuple-element.128), channel_id=1, source_target_pairs={{0,2},{1,3},{2,0},{3,1},{4,6},{5,7},{6,4},{7,5},{8,10},{9,11},{10,... | collective-permute-start | bytes 393224 | tf_op jit(solution)/shard_map/ppermute | solution.py:582
  39.7 0.0 collective-permute-done.18.refs_2_
  39.8 0.2 attach.3.refs_8_
  40.0 0.6 %collective-permute-start.20 = (bf16[5,128,128]{2,1,0:T(8,128)(2,1)S(1)}, bf16[5,128,128]{2,1,0:T(8,128)(2,1)S(1)}, u32[]{:S(2)}, u32[]{:S(2)}) collective-permute-start(bf16[5,128,128]{2,1,0:T(8,128)(2,1)S(1)} %attach.3.refs_8_), channel_id=1, source_target_pairs={{0,2},{1,3},{2,0},{3,1},{4,6},{5,7},{6,4},{7,5},{8,10},{9,11},{10,... | collective-permute-start | bytes 491528 | tf_op jit(solution)/shard_map/ppermute | solution.py:582
  40.6 0.8 %collective-permute-done.15.refs_1_.refs_2_ = bf16[384,256]{1,0:T(8,128)(2,1)S(1)} collective-permute-done((bf16[384,256]{1,0:T(8,128)(2,1)S(1)}, bf16[384,256]{1,0:T(8,128)(2,1)S(1)}, u32[]{:S(2)}, u32[]{:S(2)}) %collective-permute-start.15) | collective-permute-done | bytes 196640 | tf_op jit(solution)/shard_map/ppermute | solution.py:582
  41.4 0.0 collective-permute-done.16.refs_1_
  41.5 2.8 %collective-permute-start.17 = (bf16[384,256]{1,0:T(8,128)(2,1)S(1)}, bf16[384,256]{1,0:T(8,128)(2,1)S(1)}, u32[]{:S(2)}, u32[]{:S(2)}) collective-permute-start(bf16[384,256]{1,0:T(8,128)(2,1)S(1)} %finish.7), channel_id=1, source_target_pairs={{0,12},{1,13},{2,14},{3,15},{4,8},{5,9},{6,10},{7,11},{8,4},{9,5},... | collective-permute-start | bytes 589832 | tf_op jit(solution)/shard_map/ppermute | solution.py:582
  44.2 0.3 collective-permute-done.19.refs_0_.refs_9_
  44.5 3.1 %collective-permute-done.20.refs_1_.refs_10_ = bf16[5,128,128]{2,1,0:T(8,128)(2,1)S(1)} collective-permute-done((bf16[5,128,128]{2,1,0:T(8,128)(2,1)S(1)}, bf16[5,128,128]{2,1,0:T(8,128)(2,1)S(1)}, u32[]{:S(2)}, u32[]{:S(2)}) %collective-permute-start.20) | collective-permute-done | bytes 163872 | tf_op jit(solution)/shard_map/ppermute | solution.py:582
  47.6 3.8 %pair_back.2 = (bf16[128,128,128]{2,1,0:T(8,128)(2,1)}, f32[8,128]{1,0:T(8,128)S(1)}) custom-call(bf16[128,128,128]{2,1,0:T(8,128)(2,1)S(1)} %copy-done, bf16[8,64,128]{2,1,0:T(8,128)(2,1)S(1)} %get-tuple-element.85.refs_0_.refs_9_.refs_1_, f32[8,64,128]{2,1,0:T(8,128)S(1)} %get-tuple-element.120.refs_2_, f32[64,128]{1,0:T(8,128)S(1)} %get-tuple-element.121.refs_3_, ...), custom_call_target="tpu_custom_call" | custom-call | tf_op jit(solution)/shard_map/pair_back/pallas_call | solution.py:56
  51.4 0.0 collective-permute-done.14.refs_1_
  51.4 0.1 fold.1
  51.5 1.6 %collective-permute-start.21 = (bf16[256,256]{1,0:T(8,128)(2,1)S(1)}, bf16[256,256]{1,0:T(8,128)(2,1)S(1)}, u32[]{:S(2)}, u32[]{:S(2)}) collective-permute-start(bf16[256,256]{1,0:T(8,128)(2,1)S(1)} %get-tuple-element.131), channel_id=1, source_target_pairs={{0,2},{1,3},{2,0},{3,1},{4,6},{5,7},{6,4},{7,5},{8,10},{9,11},{10,... | collective-permute-start | bytes 393224 | tf_op jit(solution)/shard_map/ppermute | solution.py:582
  53.0 3.8 %pair_back.3 = (bf16[128,128,128]{2,1,0:T(8,128)(2,1)}, f32[8,128]{1,0:T(8,128)}) custom-call(bf16[128,128,128]{2,1,0:T(8,128)(2,1)S(1)} %copy-done, bf16[8,64,128]{2,1,0:T(8,128)(2,1)S(1)} %get-tuple-element.83.refs_0_.refs_1_, f32[8,64,128]{2,1,0:T(8,128)S(1)} %get-tuple-element.134.refs_2_, ...), custom_call_target="tpu_custom_call", output_to_operand_aliasing={{0}: (12, {})} | custom-call | tf_op jit(solution)/shard_map/pair_back/pallas_call | solution.py:56
  56.8 1.1 %last.1 = (bf16[8,64,128]{2,1,0:T(8,128)(2,1)}, bf16[8,64,128]{2,1,0:T(8,128)(2,1)}) custom-call(f32[128,512]{1,0:T(8,128)S(1)} %get-tuple-element.71.refs_0_, f32[128,512]{1,0:T(8,128)S(1)} %get-tuple-element.72.refs_1_, f32[128,512]{1,0:T(8,128)S(1)} %get-tuple-element.73.refs_2_, f32[8,128]{1,0:T(8,128)S(1)} %get-tuple-element.74.refs_3_, ...), custom_call_target="tpu_custom_call" | custom-call | tf_op jit(solution)/shard_map/last/pallas_call | solution.py:56
  (13 shorter events, 0.3 us)
Async XLA Ops:
  2.2 8.3 %collective-permute-start = (bf16[256,256]{1,0:T(8,128)(2,1)S(1)}, bf16[256,256]{1,0:T(8,128)(2,1)S(1)}, u32[]{:S(2)}, u32[]{:S(2)}) collective-permute-start(bf16[256,256]{1,0:T(8,128)(2,1)S(1)} %get-tuple-element.76), channel_id=1, source_target_pairs={{0,2},{1,3},{2,0},{3,1},{4,6},{5,7},{6,4},{7,5},{8,10},{9,11},{10,... | collective-permute-start | bytes 393224 | tf_op jit(solution)/shard_map/ppermute | solution.py:582
  5.2 2.3 %copy-start = (bf16[128,128,128]{2,1,0:T(8,128)(2,1)S(1)}, bf16[128,128,128]{2,1,0:T(8,128)(2,1)}, u32[]{:S(2)}) copy-start(bf16[128,128,128]{2,1,0:T(8,128)(2,1)} %refs_0_.9) | copy-start | bytes 12582916
  10.4 7.9 %collective-permute-start.3 = (bf16[8,64,128]{2,1,0:T(8,128)(2,1)S(1)}, bf16[8,64,128]{2,1,0:T(8,128)(2,1)S(1)}, u32[]{:S(2)}, u32[]{:S(2)}) collective-permute-start(bf16[8,64,128]{2,1,0:T(8,128)(2,1)S(1)} %get-tuple-element.85.refs_0_.refs_9_.refs_1_), channel_id=1, source_target_pairs={{0,2},{1,3},{2,0},{3,1},{4,6},{5,7},{6,4},{7,5},{8,10},{9,11},{10,... | collective-permute-start | bytes 393224 | tf_op jit(solution)/shard_map/ppermute | solution.py:582
  10.6 11.8 %collective-permute-start.1 = (bf16[384,256]{1,0:T(8,128)(2,1)S(1)}, bf16[384,256]{1,0:T(8,128)(2,1)S(1)}, u32[]{:S(2)}, u32[]{:S(2)}) collective-permute-start(bf16[384,256]{1,0:T(8,128)(2,1)S(1)} %get-tuple-element.82), channel_id=1, source_target_pairs={{0,8},{1,9},{2,10},{3,11},{4,12},{5,13},{6,14},{7,15},{8,0},{9,1},... | collective-permute-start | bytes 589832 | tf_op jit(solution)/shard_map/ppermute | solution.py:582
  13.7 9.3 %collective-permute-start.7 = (bf16[384,256]{1,0:T(8,128)(2,1)S(1)}, bf16[384,256]{1,0:T(8,128)(2,1)S(1)}, u32[]{:S(2)}, u32[]{:S(2)}) collective-permute-start(bf16[384,256]{1,0:T(8,128)(2,1)S(1)} %get-tuple-element.81.refs_6_.refs_2_.refs_0_), channel_id=1, source_target_pairs={{0,4},{1,5},{2,6},{3,7},{4,0},{5,1},{6,2},{7,3},{8,12},{9,13},{10,... | collective-permute-start | bytes 589832 | tf_op jit(solution)/shard_map/ppermute | solution.py:582
  18.3 1.3 %collective-permute-start.2 = (bf16[128,128]{1,0:T(8,128)(2,1)S(1)}, bf16[128,128]{1,0:T(8,128)(2,1)S(1)}, u32[]{:S(2)}, u32[]{:S(2)}) collective-permute-start(bf16[128,128]{1,0:T(8,128)(2,1)S(1)} %get-tuple-element.84.refs_1_), channel_id=1, source_target_pairs={{0,1},{1,0},{2,3},{3,2},{4,5},{5,4},{6,7},{7,6},{8,9},{9,8},{10,11... | collective-permute-start | bytes 98312 | tf_op jit(solution)/shard_map/ppermute | solution.py:582
  19.6 6.3 %collective-permute-start.5 = (bf16[10,64,128]{2,1,0:T(8,128)(2,1)S(1)}, bf16[10,64,128]{2,1,0:T(8,128)(2,1)S(1)}, u32[]{:S(2)}, u32[]{:S(2)}) collective-permute-start(bf16[10,64,128]{2,1,0:T(8,128)(2,1)S(1)} %attach.2.refs_1_.refs_10_), channel_id=1, source_target_pairs={{0,2},{1,3},{2,0},{3,1},{4,6},{5,7},{6,4},{7,5},{8,10},{9,11},{10,... | collective-permute-start | bytes 491528 | tf_op jit(solution)/shard_map/ppermute | solution.py:582
  22.5 1.8 %collective-permute-start.4 = (bf16[1,256,256]{2,1,0:T(8,128)(2,1)S(1)}, bf16[1,256,256]{2,1,0:T(8,128)(2,1)S(1)}, u32[]{:S(2)}, u32[]{:S(2)}) collective-permute-start(bf16[1,256,256]{2,1,0:T(8,128)(2,1)S(1)} %pick.5.refs_0_), channel_id=1, source_target_pairs={{0,1},{1,0},{2,3},{3,2},{4,5},{5,4},{6,7},{7,6},{8,9},{9,8},{10,11... | collective-permute-start | bytes 393224 | tf_op jit(solution)/shard_map/ppermute | solution.py:582
  22.5 2.2 %collective-permute-start.6 = (bf16[1,256,256]{2,1,0:T(8,128)(2,1)S(1)}, bf16[1,256,256]{2,1,0:T(8,128)(2,1)S(1)}, u32[]{:S(2)}, u32[]{:S(2)}) collective-permute-start(bf16[1,256,256]{2,1,0:T(8,128)(2,1)S(1)} %get-tuple-element.86.refs_1_.refs_0_), channel_id=1, source_target_pairs={{0,1},{1,0},{2,3},{3,2},{4,5},{5,4},{6,7},{7,6},{8,9},{9,8},{10,11... | collective-permute-start | bytes 393224 | tf_op jit(solution)/shard_map/ppermute | solution.py:582
  23.1 2.1 %collective-permute-start.8 = (bf16[1,256,256]{2,1,0:T(8,128)(2,1)S(1)}, bf16[1,256,256]{2,1,0:T(8,128)(2,1)S(1)}, u32[]{:S(2)}, u32[]{:S(2)}) collective-permute-start(bf16[1,256,256]{2,1,0:T(8,128)(2,1)S(1)} %pick.6.refs_0_), channel_id=1, source_target_pairs={{0,1},{1,0},{2,3},{3,2},{4,5},{5,4},{6,7},{7,6},{8,9},{9,8},{10,11... | collective-permute-start | bytes 393224 | tf_op jit(solution)/shard_map/ppermute | solution.py:582
  23.2 8.6 %collective-permute-start.9 = (bf16[384,256]{1,0:T(8,128)(2,1)S(1)}, bf16[384,256]{1,0:T(8,128)(2,1)S(1)}, u32[]{:S(2)}, u32[]{:S(2)}) collective-permute-start(bf16[384,256]{1,0:T(8,128)(2,1)S(1)} %get-tuple-element.97), channel_id=1, source_target_pairs={{0,4},{1,5},{2,6},{3,7},{4,0},{5,1},{6,2},{7,3},{8,12},{9,13},{10,... | collective-permute-start | bytes 589832 | tf_op jit(solution)/shard_map/ppermute | solution.py:582
  27.5 1.4 %collective-permute-start.10 = (bf16[1,256,256]{2,1,0:T(8,128)(2,1)S(1)}, bf16[1,256,256]{2,1,0:T(8,128)(2,1)S(1)}, u32[]{:S(2)}, u32[]{:S(2)}) collective-permute-start(bf16[1,256,256]{2,1,0:T(8,128)(2,1)S(1)} %get-tuple-element.102), channel_id=1, source_target_pairs={{0,1},{1,0},{2,3},{3,2},{4,5},{5,4},{6,7},{7,6},{8,9},{9,8},{10,11... | collective-permute-start | bytes 393224 | tf_op jit(solution)/shard_map/ppermute | solution.py:582
  29.0 12.4 %collective-permute-start.15 = (bf16[384,256]{1,0:T(8,128)(2,1)S(1)}, bf16[384,256]{1,0:T(8,128)(2,1)S(1)}, u32[]{:S(2)}, u32[]{:S(2)}) collective-permute-start(bf16[384,256]{1,0:T(8,128)(2,1)S(1)} %finish.4.refs_1_), channel_id=1, source_target_pairs={{0,8},{1,9},{2,10},{3,11},{4,12},{5,13},{6,14},{7,15},{8,0},{9,1},... | collective-permute-start | bytes 589832 | tf_op jit(solution)/shard_map/ppermute | solution.py:582
  31.8 1.7 %collective-permute-start.13 = (bf16[1,256,256]{2,1,0:T(8,128)(2,1)S(1)}, bf16[1,256,256]{2,1,0:T(8,128)(2,1)S(1)}, u32[]{:S(2)}, u32[]{:S(2)}) collective-permute-start(bf16[1,256,256]{2,1,0:T(8,128)(2,1)S(1)} %pick.7.refs_8_.refs_0_), channel_id=1, source_target_pairs={{0,1},{1,0},{2,3},{3,2},{4,5},{5,4},{6,7},{7,6},{8,9},{9,8},{10,11... | collective-permute-start | bytes 393224 | tf_op jit(solution)/shard_map/ppermute | solution.py:582
  31.9 5.5 %collective-permute-start.12 = (bf16[1,256,256]{2,1,0:T(8,128)(2,1)S(1)}, bf16[1,256,256]{2,1,0:T(8,128)(2,1)S(1)}, u32[]{:S(2)}, u32[]{:S(2)}) collective-permute-start(bf16[1,256,256]{2,1,0:T(8,128)(2,1)S(1)} %get-tuple-element.112), channel_id=1, source_target_pairs={{0,1},{1,0},{2,3},{3,2},{4,5},{5,4},{6,7},{7,6},{8,9},{9,8},{10,11... | collective-permute-start | bytes 393224 | tf_op jit(solution)/shard_map/ppermute | solution.py:582
  33.4 4.8 %collective-permute-start.11 = (bf16[1,256,256]{2,1,0:T(8,128)(2,1)S(1)}, bf16[1,256,256]{2,1,0:T(8,128)(2,1)S(1)}, u32[]{:S(2)}, u32[]{:S(2)}) collective-permute-start(bf16[1,256,256]{2,1,0:T(8,128)(2,1)S(1)} %get-tuple-element.109), channel_id=1, source_target_pairs={{0,1},{1,0},{2,3},{3,2},{4,5},{5,4},{6,7},{7,6},{8,9},{9,8},{10,11... | collective-permute-start | bytes 393224 | tf_op jit(solution)/shard_map/ppermute | solution.py:582
  36.0 3.8 %collective-permute-start.18 = (bf16[128,128]{1,0:T(8,128)(2,1)S(1)}, bf16[128,128]{1,0:T(8,128)(2,1)S(1)}, u32[]{:S(2)}, u32[]{:S(2)}) collective-permute-start(bf16[128,128]{1,0:T(8,128)(2,1)S(1)} %get-tuple-element.127.refs_1_), channel_id=1, source_target_pairs={{0,1},{1,0},{2,3},{3,2},{4,5},{5,4},{6,7},{7,6},{8,9},{9,8},{10,11... | collective-permute-start | bytes 98312 | tf_op jit(solution)/shard_map/ppermute | solution.py:582
  37.5 13.9 %collective-permute-start.14 = (bf16[384,256]{1,0:T(8,128)(2,1)S(1)}, bf16[384,256]{1,0:T(8,128)(2,1)S(1)}, u32[]{:S(2)}, u32[]{:S(2)}) collective-permute-start(bf16[384,256]{1,0:T(8,128)(2,1)S(1)} %finish.6), channel_id=1, source_target_pairs={{0,4},{1,5},{2,6},{3,7},{4,0},{5,1},{6,2},{7,3},{8,12},{9,13},{10,... | collective-permute-start | bytes 589832 | tf_op jit(solution)/shard_map/ppermute | solution.py:582
  38.2 3.2 %collective-permute-start.16 = (bf16[1,256,256]{2,1,0:T(8,128)(2,1)S(1)}, bf16[1,256,256]{2,1,0:T(8,128)(2,1)S(1)}, u32[]{:S(2)}, u32[]{:S(2)}) collective-permute-start(bf16[1,256,256]{2,1,0:T(8,128)(2,1)S(1)} %get-tuple-element.119), channel_id=1, source_target_pairs={{0,1},{1,0},{2,3},{3,2},{4,5},{5,4},{6,7},{7,6},{8,9},{9,8},{10,11... | collective-permute-start | bytes 393224 | tf_op jit(solution)/shard_map/ppermute | solution.py:582
  38.2 6.3 %collective-permute-start.19 = (bf16[4,128,128]{2,1,0:T(8,128)(2,1)S(1)}, bf16[4,128,128]{2,1,0:T(8,128)(2,1)S(1)}, u32[]{:S(2)}, u32[]{:S(2)}) collective-permute-start(bf16[4,128,128]{2,1,0:T(8,128)(2,1)S(1)} %get-tuple-element.128), channel_id=1, source_target_pairs={{0,2},{1,3},{2,0},{3,1},{4,6},{5,7},{6,4},{7,5},{8,10},{9,11},{10,... | collective-permute-start | bytes 393224 | tf_op jit(solution)/shard_map/ppermute | solution.py:582
  40.0 7.7 %collective-permute-start.20 = (bf16[5,128,128]{2,1,0:T(8,128)(2,1)S(1)}, bf16[5,128,128]{2,1,0:T(8,128)(2,1)S(1)}, u32[]{:S(2)}, u32[]{:S(2)}) collective-permute-start(bf16[5,128,128]{2,1,0:T(8,128)(2,1)S(1)} %attach.3.refs_8_), channel_id=1, source_target_pairs={{0,2},{1,3},{2,0},{3,1},{4,6},{5,7},{6,4},{7,5},{8,10},{9,11},{10,... | collective-permute-start | bytes 491528 | tf_op jit(solution)/shard_map/ppermute | solution.py:582
  41.5 9.9 %collective-permute-start.17 = (bf16[384,256]{1,0:T(8,128)(2,1)S(1)}, bf16[384,256]{1,0:T(8,128)(2,1)S(1)}, u32[]{:S(2)}, u32[]{:S(2)}) collective-permute-start(bf16[384,256]{1,0:T(8,128)(2,1)S(1)} %finish.7), channel_id=1, source_target_pairs={{0,12},{1,13},{2,14},{3,15},{4,8},{5,9},{6,10},{7,11},{8,4},{9,5},... | collective-permute-start | bytes 589832 | tf_op jit(solution)/shard_map/ppermute | solution.py:582
  51.5 5.3 %collective-permute-start.21 = (bf16[256,256]{1,0:T(8,128)(2,1)S(1)}, bf16[256,256]{1,0:T(8,128)(2,1)S(1)}, u32[]{:S(2)}, u32[]{:S(2)}) collective-permute-start(bf16[256,256]{1,0:T(8,128)(2,1)S(1)} %get-tuple-element.131), channel_id=1, source_target_pairs={{0,2},{1,3},{2,0},{3,1},{4,6},{5,7},{6,4},{7,5},{8,10},{9,11},{10,... | collective-permute-start | bytes 393224 | tf_op jit(solution)/shard_map/ppermute | solution.py:582

commit v5 on v4

--- a/solution.py
+++ b/solution.py
@@ -13,6 +13,8 @@
 QUAD = 4
 GROUP = 4
 SLOTS = 32
+BACK_SLOTS = 16
+BACK_GROUP = 8
 COST = dict(first=1.5, pack=0.1, weights=1.3, pair=2.5, attach=0, pick=0, probs=0, prepare=0, work=0.0, scores=0.0, finish=0, pair_back=0, gather=5, settle=5, fold=0, last=0)
 VMEM = 20 * 1024 * 1024
 
@@ -102,15 +104,18 @@
     )
 
     def diagonal(tile):
-        tall = jnp.concatenate([tile] * GROUP, axis=0)
-        full = jnp.concatenate([tall] * GROUP, axis=1)
+        copies = GROUP * SLOTS // tile.shape[0]
+        tall = jnp.concatenate([tile] * copies, axis=0)
+        full = jnp.concatenate([tall] * copies, axis=1)
         row, col = iota(full.shape, 0), iota(full.shape, 1)
-        return jnp.where(row // SLOTS == col // tile.shape[1], full, 0.0).astype(BF16)
+        return jnp.where(row // tile.shape[0] == col // tile.shape[1], full, 0.0).astype(BF16)
 
     moments[...] = diagonal(slots)
     squares[...] = diagonal(square_slots)
-    high, middle, _ = split3(scaled - total * (1.0 / width))
-    back[...] = diagonal(jnp.concatenate([high, middle, high, jnp.where(row < 3, 1.0, 0.0)], axis=0))
+    row = iota((BACK_SLOTS - heads, width), 0)
+    back[...] = diagonal(
+        jnp.concatenate([scaled - total * (1.0 / width), jnp.where(row < 3, 1.0, 0.0)], axis=0)
+    )
 
 
 def side_by_side(ref, pair, channels):
@@ -476,29 +481,26 @@
         prob = e_ref[h, here].astype(F32) * scale[:, h : h + 1]
         grad = prob * (scores - total[:, h : h + 1])
         cross = cross + grad * logit_ref[h, here]
-        scaled = grad * inverse
-        high = scaled.astype(BF16).astype(F32)
-        scratch[pl.ds(h, count, stride=SLOTS), :] = high
-        scratch[pl.ds(heads + h, count, stride=SLOTS), :] = high
-        scratch[pl.ds(2 * heads + h, count, stride=SLOTS), :] = scaled - high
+        scratch[pl.ds(h, count, stride=BACK_SLOTS), :] = grad * inverse
     factor = inverse * inverse * cross * (1.0 / width)
     rest = [*split3(factor * mean_ref[here]), factor]
-    rest += [jnp.zeros_like(factor)] * (SLOTS - 3 * heads - len(rest))
+    rest += [jnp.zeros_like(factor)] * (BACK_SLOTS - heads - len(rest))
     for t, part in enumerate(rest):
-        scratch[pl.ds(3 * heads + t, count, stride=SLOTS), :] = part
-    groups = count // GROUP
+        scratch[pl.ds(heads + t, count, stride=BACK_SLOTS), :] = part
+    groups = count // BACK_GROUP
+    size = BACK_GROUP * BACK_SLOTS
     for group in range(groups):
         rows = slice(group * columns, (group + 1) * columns)
-        tile = jnp.transpose(scratch[group * GROUP * SLOTS : (group + 1) * GROUP * SLOTS])
+        tile = jnp.transpose(scratch[group * size : (group + 1) * size])
         turned[rows] = tile
         rounded[rows] = tile.astype(BF16)
-    for g in range(0, GROUP, 2):
+    for g in range(0, BACK_GROUP, 2):
         product = dot(rounded[...], back_ref[:, g * width : (g + 2) * width])
         for group in range(groups):
             rows = slice(group * columns, (group + 1) * columns)
             for s in range(2):
-                i = group * GROUP + g + s
-                lane = (g + s) * SLOTS + 3 * heads + 3
+                i = group * BACK_GROUP + g + s
+                lane = (g + s) * BACK_SLOTS + heads + 3
                 slope = turned[rows, lane : lane + 1] * x_ref[low + i].astype(F32)
                 out_ref[i] = (product[rows, s * width : (s + 1) * width] - slope).astype(BF16)
 
@@ -614,7 +616,7 @@
         functools.partial(weights_kernel, depth),
         [shape((lanes, hidden * QUAD), BF16)] * 3
         + [shape((GROUP * SLOTS, GROUP * pair_width), BF16)] * 2
-        + [shape((heads, pair_width), F32), shape((GROUP * SLOTS, GROUP * pair_width), BF16)],
+        + [shape((heads, pair_width), F32), shape((BACK_GROUP * BACK_SLOTS, BACK_GROUP * pair_width), BF16)],
         "weights",
         operands=(
             in_hbm(value_matrix), in_hbm(gate_matrix), in_hbm(output_matrix.T), in_hbm(head_bias_matrix.T),
@@ -733,7 +735,7 @@
         [shape((heads, rows, R * columns), BF16), shape((R, rows, columns), F32)],
         "probs",
         operands=exps,
-        after=[prepared[phase][1] for phase in early_phases],
+        after=[prepared[phase][1] for phase in early_phases[:2]],
     )
 
     work(phases[0])
@@ -783,9 +785,9 @@
             "pair_back",
             operands=(pair_features, *forward[index], scales, own_scores, back, *received),
             scratch=[
-                pltpu.VMEM((block * SLOTS, columns), F32),
-                pltpu.VMEM((block // GROUP * columns, GROUP * SLOTS), F32),
-                pltpu.VMEM((block // GROUP * columns, GROUP * SLOTS), BF16),
+                pltpu.VMEM((block * BACK_SLOTS, columns), F32),
+                pltpu.VMEM((block // BACK_GROUP * columns, BACK_GROUP * BACK_SLOTS), F32),
+                pltpu.VMEM((block // BACK_GROUP * columns, BACK_GROUP * BACK_SLOTS), BF16),
             ],
             grid=(part_rows // block,),
             out_specs=[

time: 58.1 us -> 57.1 us (0.983)
  Pallas kernels: 26.6 us -> 25.2 us
  waiting for transfers between devices: 7.22 us -> 8.55 us
  starting transfers between devices: 22.4 us -> 21.4 us
    ppermute x22, waiting for transfers between devices: 7.22 us -> 8.55 us  [exchange(): lax.ppermute(value, everyone, [(at(z, x, c), at(z ^ dz, x ^ dx, c ^ dc))...]
    pallas_call x31, Pallas kernels: 26.6 us -> 25.2 us  [call(): pl.pallas_call(body, out_shape=out_shape, in_specs=[whole] * count + [pl....]
    ppermute x22, starting transfers between devices: 22.4 us -> 21.4 us  [exchange(): lax.ppermute(value, everyone, [(at(z, x, c), at(z ^ dz, x ^ dx, c ^ dc))...]
  transfers between devices with their start and end apart: 22 -> 22, of which waited for: 7 -> 7; matrix products, arithmetic and copies ran while one was open for 0% -> 0% of each run, Pallas kernels for 41% -> 39%
where the time goes in v5:
time: 57.1 us; the launch traced here: 56.9 us
  Pallas kernels  25.2 us (44%)
  starting transfers between devices  21.4 us (37%)
  waiting for transfers between devices  8.55 us (15%)
  between operations  0.92 us (2%)
  local copies, waits for them, and re-layouts  0.83 us (1%)
    pallas_call x31, Pallas kernels, call(): pl.pallas_call(body, out_shape=out_shape, in_specs=[whole] * count + [pl....  25.2 us
    ppermute x22, starting transfers between devices, exchange(): lax.ppermute(value, everyone, [(at(z, x, c), at(z ^ dz, x ^ dx, c ^ dc))...  21.4 us
    ppermute x22, waiting for transfers between devices, exchange(): lax.ppermute(value, everyone, [(at(z, x, c), at(z ^ dz, x ^ dx, c ^ dc))...  8.55 us
  transfers between devices with their start and end apart: 22, of which 7 were waited for; matrix products, arithmetic and copies ran while one was open for 0% of the time, Pallas kernels for 39%

profile of v5, /device:TPU:0, one launch (start us, length us, event | category | flops | bytes accessed | tf_op | source)
XLA Modules:
  0.0 56.9 jit_solution(15174836728475054919)
XLA Ops:
  0.6 1.6 %first.1 = (f32[128,512]{1,0:T(8,128)S(1)}, f32[128,512]{1,0:T(8,128)S(1)}, f32[128,512]{1,0:T(8,128)S(1)}, f32[8,128]{1,0:T(8,128)S(1)}, bf16[256,256]{1,0:T(8,128)(2,1)S(1)}, /*index=5*/bf16[256,256]{1,0:T(8,128)(2,1)S(1)}) custom-call(s32[1,8]{1,0:T(1,128)} %bitcast.16, bf16[8,64,128]{2,1,0:T(8,128)(2,1)} %bitcast.10, bf16[8,64,128]{2,1,0:T(8,128)(2,1)} %bitcast.11, ...), custom_call_target="tpu_custom_call" | custom-call | flops 4499999744 | tf_op jit(solution)/shard_map/first/pallas_call | solution.py:58
  2.2 3.0 %collective-permute-start = (bf16[256,256]{1,0:T(8,128)(2,1)S(1)}, bf16[256,256]{1,0:T(8,128)(2,1)S(1)}, u32[]{:S(2)}, u32[]{:S(2)}) collective-permute-start(bf16[256,256]{1,0:T(8,128)(2,1)S(1)} %get-tuple-element.76), channel_id=1, source_target_pairs={{0,2},{1,3},{2,0},{3,1},{4,6},{5,7},{6,4},{7,5},{8,10},{9,11},{10,... | collective-permute-start | bytes 393224 | tf_op jit(solution)/shard_map/ppermute | solution.py:584
  5.3 1.4 %weights.1 = (bf16[256,1024]{1,0:T(8,128)(2,1)S(1)}, bf16[256,1024]{1,0:T(8,128)(2,1)S(1)}, bf16[256,1024]{1,0:T(8,128)(2,1)S(1)}, bf16[128,512]{1,0:T(8,128)(2,...) custom-call(bf16[64,256]{1,0:T(8,128)(2,1)} %refs_0_.5, ...), custom_call_target="tpu_custom_call" | custom-call | flops 3900000000 | tf_op jit(solution)/shard_map/weights/pallas_call | solution.py:58
  6.7 0.8 %copy-done = bf16[128,128,128]{2,1,0:T(8,128)(2,1)S(1)} copy-done((bf16[128,128,128]{2,1,0:T(8,128)(2,1)S(1)}, bf16[128,128,128]{2,1,0:T(8,128)(2,1)}, u32[]{:S(2)}) %copy-start) | copy-done | bytes 4194328
  7.5 2.9 %pair.2 = (bf16[8,64,128]{2,1,0:T(8,128)(2,1)S(1)}, bf16[64,128]{1,0:T(8,128)(2,1)S(1)}, f32[8,64,128]{2,1,0:T(8,128)S(1)}, f32[64,128]{1,0:T(8,128)S(1)}, f32[64,128]{1,0:T(8,128)S(1)}) custom-call(bf16[128,128,128]{2,1,0:T(8,128)(2,1)S(1)} %copy-done, bf16[128,512]{1,0:T(8,128)(2,1)S(1)} %get-tuple-element.77.refs_1_, ...), custom_call_target="tpu_custom_call" | custom-call | flops 7500000256 | tf_op jit(solution)/shard_map/pair/pallas_call | solution.py:58
  10.4 0.1 collective-permute-start.3
  10.5 0.0 collective-permute-done.refs_1_
  10.6 3.2 %collective-permute-start.1 = (bf16[384,256]{1,0:T(8,128)(2,1)S(1)}, bf16[384,256]{1,0:T(8,128)(2,1)S(1)}, u32[]{:S(2)}, u32[]{:S(2)}) collective-permute-start(bf16[384,256]{1,0:T(8,128)(2,1)S(1)} %get-tuple-element.82), channel_id=1, source_target_pairs={{0,8},{1,9},{2,10},{3,11},{4,12},{5,13},{6,14},{7,15},{8,0},{9,1},... | collective-permute-start | bytes 589832 | tf_op jit(solution)/shard_map/ppermute | solution.py:584
  13.7 1.6 %collective-permute-start.9 = (bf16[384,256]{1,0:T(8,128)(2,1)S(1)}, bf16[384,256]{1,0:T(8,128)(2,1)S(1)}, u32[]{:S(2)}, u32[]{:S(2)}) collective-permute-start(bf16[384,256]{1,0:T(8,128)(2,1)S(1)} %get-tuple-element.81.refs_6_.refs_2_.refs_0_), channel_id=1, source_target_pairs={{0,4},{1,5},{2,6},{3,7},{4,0},{5,1},{6,2},{7,3},{8,12},{9,13},{10,... | collective-permute-start | bytes 589832 | tf_op jit(solution)/shard_map/ppermute | solution.py:584
  15.3 2.9 %pair.3 = (bf16[8,64,128]{2,1,0:T(8,128)(2,1)S(1)}, bf16[128,128]{1,0:T(8,128)(2,1)S(1)}, f32[8,64,128]{2,1,0:T(8,128)S(1)}, f32[64,128]{1,0:T(8,128)S(1)}, f32[64,128]{1,0:T(8,128)S(1)}) custom-call(bf16[128,128,128]{2,1,0:T(8,128)(2,1)S(1)} %copy-done, bf16[128,512]{1,0:T(8,128)(2,1)S(1)} %get-tuple-element.77.refs_1_, ...), custom_call_target="tpu_custom_call" | custom-call | flops 7500000256 | tf_op jit(solution)/shard_map/pair/pallas_call | solution.py:58
  18.3 0.1 collective-permute-start.2
  18.3 0.0 collective-permute-done.3.refs_3_.refs_2_.refs_11_
  18.3 1.2 %collective-permute-done.2.refs_2_ = bf16[128,128]{1,0:T(8,128)(2,1)S(1)} collective-permute-done((bf16[128,128]{1,0:T(8,128)(2,1)S(1)}, bf16[128,128]{1,0:T(8,128)(2,1)S(1)}, u32[]{:S(2)}, u32[]{:S(2)}) %collective-permute-start.2) | collective-permute-done | bytes 32800 | tf_op jit(solution)/shard_map/ppermute | solution.py:584
  19.5 0.1 attach.2.refs_1_.refs_10_
  19.6 1.6 %collective-permute-start.5 = (bf16[10,64,128]{2,1,0:T(8,128)(2,1)S(1)}, bf16[10,64,128]{2,1,0:T(8,128)(2,1)S(1)}, u32[]{:S(2)}, u32[]{:S(2)}) collective-permute-start(bf16[10,64,128]{2,1,0:T(8,128)(2,1)S(1)} %attach.2.refs_1_.refs_10_), channel_id=1, source_target_pairs={{0,2},{1,3},{2,0},{3,1},{4,6},{5,7},{6,4},{7,5},{8,10},{9,11},{10,... | collective-permute-start | bytes 491528 | tf_op jit(solution)/shard_map/ppermute | solution.py:584
  21.2 1.2 %collective-permute-done.1.refs_0_.refs_3_.refs_2_ = bf16[384,256]{1,0:T(8,128)(2,1)S(1)} collective-permute-done((bf16[384,256]{1,0:T(8,128)(2,1)S(1)}, bf16[384,256]{1,0:T(8,128)(2,1)S(1)}, u32[]{:S(2)}, u32[]{:S(2)}) %collective-permute-start.1) | collective-permute-done | bytes 196640 | tf_op jit(solution)/shard_map/ppermute | solution.py:584
  22.5 0.1 collective-permute-start.4
  22.5 0.5 collective-permute-start.6
  23.0 0.6 %collective-permute-start.7 = (bf16[384,256]{1,0:T(8,128)(2,1)S(1)}, bf16[384,256]{1,0:T(8,128)(2,1)S(1)}, u32[]{:S(2)}, u32[]{:S(2)}) collective-permute-start(bf16[384,256]{1,0:T(8,128)(2,1)S(1)} %get-tuple-element.96), channel_id=1, source_target_pairs={{0,4},{1,5},{2,6},{3,7},{4,0},{5,1},{6,2},{7,3},{8,12},{9,13},{10,... | collective-permute-start | bytes 589832 | tf_op jit(solution)/shard_map/ppermute | solution.py:584
  23.7 0.0 collective-permute-done.9.refs_0_.refs_2_
  23.7 0.1 collective-permute-start.10
  23.8 0.1 collective-permute-done.4.refs_1_
  23.9 0.5 prepare.4
  24.4 0.0 collective-permute-done.6.refs_1_
  24.4 0.5 prepare.5
  24.9 1.1 %collective-permute-done.5.refs_3_.refs_12_ = bf16[10,64,128]{2,1,0:T(8,128)(2,1)S(1)} collective-permute-done((bf16[10,64,128]{2,1,0:T(8,128)(2,1)S(1)}, bf16[10,64,128]{2,1,0:T(8,128)(2,1)S(1)}, u32[]{:S(2)}, u32[]{:S(2)}) %collective-permute-start.5) | collective-permute-done | bytes 163872 | tf_op jit(solution)/shard_map/ppermute | solution.py:584
  25.9 0.6 %probs.1 = (bf16[8,128,256]{2,1,0:T(8,128)(2,1)S(1)}, f32[2,128,128]{2,1,0:T(8,128)S(1)}) custom-call(bf16[8,64,128]{2,1,0:T(8,128)(2,1)S(1)} %get-tuple-element.85.refs_0_.refs_9_.refs_1_, bf16[10,64,128]{2,1,0:T(8,128)(2,1)S(1)} %attach.2.refs_1_.refs_10_, bf16[8,64,128]{2,1,0:T(8,128)(2,1)S(1)} %collective-permute-done.3.refs_3_.refs_2_.refs_11_, ...), custom_call_target="tpu_custom_call" | custom-call | tf_op jit(solution)/shard_map/probs/pallas_call | solution.py:58
  26.5 1.0 %work.4 = (f32[1,256,256]{2,1,0:T(8,128)S(1)}, bf16[1,256,256]{2,1,0:T(8,128)(2,1)S(1)}, f32[1,256,256]{2,1,0:T(8,128)S(1)}) custom-call(bf16[8,256,128]{2,1,0:T(8,128)(2,1)S(1)} %get-tuple-element.97.refs_0_.refs_4_, bf16[8,128,128]{2,1,0:T(8,128)(2,1)S(1)} %get-tuple-element.94.refs_4_.refs_1_.refs_0_, f32[1,128,1024]{2,1,0:T(8,128)S(1)} %get-tuple-element.98.refs_2_, ...), custom_call_target="tpu_custom_call" | custom-call | tf_op jit(solution)/shard_map/work/pallas_call | solution.py:58
  27.5 0.1 collective-permute-start.8
  27.6 0.0 collective-permute-done.10.refs_1_
  27.6 0.5 prepare.6
  28.1 1.0 %work.5 = (f32[1,256,256]{2,1,0:T(8,128)S(1)}, bf16[1,256,256]{2,1,0:T(8,128)(2,1)S(1)}, f32[1,256,256]{2,1,0:T(8,128)S(1)}) custom-call(bf16[8,256,128]{2,1,0:T(8,128)(2,1)S(1)} %get-tuple-element.103.refs_0_.refs_6_, bf16[8,128,128]{2,1,0:T(8,128)(2,1)S(1)} %get-tuple-element.104.refs_1_.refs_2_, f32[1,128,1024]{2,1,0:T(8,128)S(1)} %get-tuple-element.105.refs_2_, ...), custom_call_target="tpu_custom_call" | custom-call | tf_op jit(solution)/shard_map/work/pallas_call | solution.py:58
  29.1 0.0 collective-permute-done.8.refs_1_
  29.1 2.7 %collective-permute-start.15 = (bf16[384,256]{1,0:T(8,128)(2,1)S(1)}, bf16[384,256]{1,0:T(8,128)(2,1)S(1)}, u32[]{:S(2)}, u32[]{:S(2)}) collective-permute-start(bf16[384,256]{1,0:T(8,128)(2,1)S(1)} %finish.4.refs_1_), channel_id=1, source_target_pairs={{0,8},{1,9},{2,10},{3,11},{4,12},{5,13},{6,14},{7,15},{8,0},{9,1},... | collective-permute-start | bytes 589832 | tf_op jit(solution)/shard_map/ppermute | solution.py:584
  31.9 0.1 collective-permute-start.13
  32.0 0.5 collective-permute-start.12
  32.5 1.0 %work.6 = (f32[1,256,256]{2,1,0:T(8,128)S(1)}, bf16[1,256,256]{2,1,0:T(8,128)(2,1)S(1)}, f32[1,256,256]{2,1,0:T(8,128)S(1)}) custom-call(bf16[8,256,128]{2,1,0:T(8,128)(2,1)S(1)} %get-tuple-element.90.refs_0_.refs_5_, bf16[8,128,128]{2,1,0:T(8,128)(2,1)S(1)} %get-tuple-element.91.refs_5_.refs_1_, f32[1,128,1024]{2,1,0:T(8,128)S(1)} %get-tuple-element.92.refs_2_, ...), custom_call_target="tpu_custom_call" | custom-call | tf_op jit(solution)/shard_map/work/pallas_call | solution.py:58
  33.5 0.1 collective-permute-start.11
  33.6 0.7 %prepare.7 = (bf16[8,256,128]{2,1,0:T(8,128)(2,1)S(1)}, bf16[8,128,128]{2,1,0:T(8,128)(2,1)S(1)}, f32[1,128,1024]{2,1,0:T(8,128)S(1)}, f32[1,128,1024]{2,1,0:T(8,128)S(1)}) custom-call(bf16[1,256,256]{2,1,0:T(8,128)(2,1)S(1)} %pick.7.refs_8_.refs_0_, bf16[1,256,256]{2,1,0:T(8,128)(2,1)S(1)} %collective-permute-done.13.refs_1_, ...), custom_call_target="tpu_custom_call" | custom-call | tf_op jit(solution)/shard_map/prepare/pallas_call | solution.py:58
  34.3 1.8 %scores.1 = (f32[8,128,128]{2,1,0:T(8,128)S(1)}, bf16[128,128]{1,0:T(8,128)(2,1)S(1)}, bf16[4,128,128]{2,1,0:T(8,128)(2,1)S(1)}, bf16[4,128,128]{2,1,0:T(8,128)(2,1)S(1)}) custom-call(bf16[8,128,128]{2,1,0:T(8,128)(2,1)S(1)} %get-tuple-element.94.refs_4_.refs_1_.refs_0_, bf16[8,128,128]{2,1,0:T(8,128)(2,1)S(1)} %get-tuple-element.91.refs_5_.refs_1_, ...), custom_call_target="tpu_custom_call" | custom-call | tf_op jit(solution)/shard_map/scores/pallas_call | solution.py:58
  36.0 0.5 collective-permute-start.18
  36.5 1.0 %work.7 = (f32[1,256,256]{2,1,0:T(8,128)S(1)}, bf16[1,256,256]{2,1,0:T(8,128)(2,1)S(1)}, f32[1,256,256]{2,1,0:T(8,128)S(1)}) custom-call(bf16[8,256,128]{2,1,0:T(8,128)(2,1)S(1)} %get-tuple-element.113.refs_0_.refs_7_, bf16[8,128,128]{2,1,0:T(8,128)(2,1)S(1)} %get-tuple-element.114.refs_1_.refs_3_, f32[1,128,1024]{2,1,0:T(8,128)S(1)} %get-tuple-element.115.refs_2_, ...), custom_call_target="tpu_custom_call" | custom-call | tf_op jit(solution)/shard_map/work/pallas_call | solution.py:58
  37.5 0.0 collective-permute-done.12.refs_1_
  37.5 0.1 finish.6
  37.6 0.4 collective-permute-start.14
  38.0 0.0 collective-permute-done.11.refs_1_
  38.0 1.5 %collective-permute-start.19 = (bf16[4,128,128]{2,1,0:T(8,128)(2,1)S(1)}, bf16[4,128,128]{2,1,0:T(8,128)(2,1)S(1)}, u32[]{:S(2)}, u32[]{:S(2)}) collective-permute-start(bf16[4,128,128]{2,1,0:T(8,128)(2,1)S(1)} %get-tuple-element.128), channel_id=1, source_target_pairs={{0,2},{1,3},{2,0},{3,1},{4,6},{5,7},{6,4},{7,5},{8,10},{9,11},{10,... | collective-permute-start | bytes 393224 | tf_op jit(solution)/shard_map/ppermute | solution.py:584
  39.5 0.1 finish.5.refs_0_
  39.6 0.0 collective-permute-done.18.refs_2_
  39.6 0.2 attach.3.refs_8_
  39.8 0.6 collective-permute-start.20
  40.3 1.2 %collective-permute-done.15.refs_1_.refs_2_ = bf16[384,256]{1,0:T(8,128)(2,1)S(1)} collective-permute-done((bf16[384,256]{1,0:T(8,128)(2,1)S(1)}, bf16[384,256]{1,0:T(8,128)(2,1)S(1)}, u32[]{:S(2)}, u32[]{:S(2)}) %collective-permute-start.15) | collective-permute-done | bytes 196640 | tf_op jit(solution)/shard_map/ppermute | solution.py:584
  41.6 0.1 finish.7
  41.7 2.6 %collective-permute-start.17 = (bf16[384,256]{1,0:T(8,128)(2,1)S(1)}, bf16[384,256]{1,0:T(8,128)(2,1)S(1)}, u32[]{:S(2)}, u32[]{:S(2)}) collective-permute-start(bf16[384,256]{1,0:T(8,128)(2,1)S(1)} %finish.7), channel_id=1, source_target_pairs={{0,12},{1,13},{2,14},{3,15},{4,8},{5,9},{6,10},{7,11},{8,4},{9,5},... | collective-permute-start | bytes 589832 | tf_op jit(solution)/shard_map/ppermute | solution.py:584
  44.2 0.0 collective-permute-done.19.refs_0_.refs_9_
  44.3 3.1 %collective-permute-done.20.refs_1_.refs_10_ = bf16[5,128,128]{2,1,0:T(8,128)(2,1)S(1)} collective-permute-done((bf16[5,128,128]{2,1,0:T(8,128)(2,1)S(1)}, bf16[5,128,128]{2,1,0:T(8,128)(2,1)S(1)}, u32[]{:S(2)}, u32[]{:S(2)}) %collective-permute-start.20) | collective-permute-done | bytes 163872 | tf_op jit(solution)/shard_map/ppermute | solution.py:584
  47.4 3.1 %pair_back.2 = (bf16[128,128,128]{2,1,0:T(8,128)(2,1)}, f32[8,128]{1,0:T(8,128)S(1)}) custom-call(bf16[128,128,128]{2,1,0:T(8,128)(2,1)S(1)} %copy-done, bf16[8,64,128]{2,1,0:T(8,128)(2,1)S(1)} %get-tuple-element.85.refs_0_.refs_9_.refs_1_, f32[8,64,128]{2,1,0:T(8,128)S(1)} %get-tuple-element.120.refs_2_, f32[64,128]{1,0:T(8,128)S(1)} %get-tuple-element.121.refs_3_, ...), custom_call_target="tpu_custom_call" | custom-call | tf_op jit(solution)/shard_map/pair_back/pallas_call | solution.py:58
  50.5 0.0 collective-permute-done.14.refs_1_
  50.5 0.0 collective-permute-done.17.refs_3_
  50.5 0.1 fold.1
  50.6 1.6 %collective-permute-start.21 = (bf16[256,256]{1,0:T(8,128)(2,1)S(1)}, bf16[256,256]{1,0:T(8,128)(2,1)S(1)}, u32[]{:S(2)}, u32[]{:S(2)}) collective-permute-start(bf16[256,256]{1,0:T(8,128)(2,1)S(1)} %get-tuple-element.131), channel_id=1, source_target_pairs={{0,2},{1,3},{2,0},{3,1},{4,6},{5,7},{6,4},{7,5},{8,10},{9,11},{10,... | collective-permute-start | bytes 393224 | tf_op jit(solution)/shard_map/ppermute | solution.py:584
  52.2 3.1 %pair_back.3 = (bf16[128,128,128]{2,1,0:T(8,128)(2,1)}, f32[8,128]{1,0:T(8,128)}) custom-call(bf16[128,128,128]{2,1,0:T(8,128)(2,1)S(1)} %copy-done, bf16[8,64,128]{2,1,0:T(8,128)(2,1)S(1)} %get-tuple-element.83.refs_0_.refs_1_, f32[8,64,128]{2,1,0:T(8,128)S(1)} %get-tuple-element.134.refs_2_, ...), custom_call_target="tpu_custom_call", output_to_operand_aliasing={{0}: (12, {})} | custom-call | tf_op jit(solution)/shard_map/pair_back/pallas_call | solution.py:58
  55.3 0.5 collective-permute-done.21.refs_5_
  55.8 1.1 %last.1 = (bf16[8,64,128]{2,1,0:T(8,128)(2,1)}, bf16[8,64,128]{2,1,0:T(8,128)(2,1)}) custom-call(f32[128,512]{1,0:T(8,128)S(1)} %get-tuple-element.71.refs_0_, f32[128,512]{1,0:T(8,128)S(1)} %get-tuple-element.72.refs_1_, f32[128,512]{1,0:T(8,128)S(1)} %get-tuple-element.73.refs_2_, f32[8,128]{1,0:T(8,128)S(1)} %get-tuple-element.74.refs_3_, ...), custom_call_target="tpu_custom_call" | custom-call | tf_op jit(solution)/shard_map/last/pallas_call | solution.py:58
  (13 shorter events, 0.2 us)
Async XLA Ops:
  2.2 8.3 %collective-permute-start = (bf16[256,256]{1,0:T(8,128)(2,1)S(1)}, bf16[256,256]{1,0:T(8,128)(2,1)S(1)}, u32[]{:S(2)}, u32[]{:S(2)}) collective-permute-start(bf16[256,256]{1,0:T(8,128)(2,1)S(1)} %get-tuple-element.76), channel_id=1, source_target_pairs={{0,2},{1,3},{2,0},{3,1},{4,6},{5,7},{6,4},{7,5},{8,10},{9,11},{10,... | collective-permute-start | bytes 393224 | tf_op jit(solution)/shard_map/ppermute | solution.py:584
  5.2 2.3 %copy-start = (bf16[128,128,128]{2,1,0:T(8,128)(2,1)S(1)}, bf16[128,128,128]{2,1,0:T(8,128)(2,1)}, u32[]{:S(2)}) copy-start(bf16[128,128,128]{2,1,0:T(8,128)(2,1)} %refs_0_.9) | copy-start | bytes 12582916
  10.4 7.9 %collective-permute-start.3 = (bf16[8,64,128]{2,1,0:T(8,128)(2,1)S(1)}, bf16[8,64,128]{2,1,0:T(8,128)(2,1)S(1)}, u32[]{:S(2)}, u32[]{:S(2)}) collective-permute-start(bf16[8,64,128]{2,1,0:T(8,128)(2,1)S(1)} %get-tuple-element.85.refs_0_.refs_9_.refs_1_), channel_id=1, source_target_pairs={{0,2},{1,3},{2,0},{3,1},{4,6},{5,7},{6,4},{7,5},{8,10},{9,11},{10,... | collective-permute-start | bytes 393224 | tf_op jit(solution)/shard_map/ppermute | solution.py:584
  10.6 11.8 %collective-permute-start.1 = (bf16[384,256]{1,0:T(8,128)(2,1)S(1)}, bf16[384,256]{1,0:T(8,128)(2,1)S(1)}, u32[]{:S(2)}, u32[]{:S(2)}) collective-permute-start(bf16[384,256]{1,0:T(8,128)(2,1)S(1)} %get-tuple-element.82), channel_id=1, source_target_pairs={{0,8},{1,9},{2,10},{3,11},{4,12},{5,13},{6,14},{7,15},{8,0},{9,1},... | collective-permute-start | bytes 589832 | tf_op jit(solution)/shard_map/ppermute | solution.py:584
  13.7 9.9 %collective-permute-start.9 = (bf16[384,256]{1,0:T(8,128)(2,1)S(1)}, bf16[384,256]{1,0:T(8,128)(2,1)S(1)}, u32[]{:S(2)}, u32[]{:S(2)}) collective-permute-start(bf16[384,256]{1,0:T(8,128)(2,1)S(1)} %get-tuple-element.81.refs_6_.refs_2_.refs_0_), channel_id=1, source_target_pairs={{0,4},{1,5},{2,6},{3,7},{4,0},{5,1},{6,2},{7,3},{8,12},{9,13},{10,... | collective-permute-start | bytes 589832 | tf_op jit(solution)/shard_map/ppermute | solution.py:584
  18.3 1.3 %collective-permute-start.2 = (bf16[128,128]{1,0:T(8,128)(2,1)S(1)}, bf16[128,128]{1,0:T(8,128)(2,1)S(1)}, u32[]{:S(2)}, u32[]{:S(2)}) collective-permute-start(bf16[128,128]{1,0:T(8,128)(2,1)S(1)} %get-tuple-element.84.refs_1_), channel_id=1, source_target_pairs={{0,1},{1,0},{2,3},{3,2},{4,5},{5,4},{6,7},{7,6},{8,9},{9,8},{10,11... | collective-permute-start | bytes 98312 | tf_op jit(solution)/shard_map/ppermute | solution.py:584
  19.6 6.3 %collective-permute-start.5 = (bf16[10,64,128]{2,1,0:T(8,128)(2,1)S(1)}, bf16[10,64,128]{2,1,0:T(8,128)(2,1)S(1)}, u32[]{:S(2)}, u32[]{:S(2)}) collective-permute-start(bf16[10,64,128]{2,1,0:T(8,128)(2,1)S(1)} %attach.2.refs_1_.refs_10_), channel_id=1, source_target_pairs={{0,2},{1,3},{2,0},{3,1},{4,6},{5,7},{6,4},{7,5},{8,10},{9,11},{10,... | collective-permute-start | bytes 491528 | tf_op jit(solution)/shard_map/ppermute | solution.py:584
  22.5 1.4 %collective-permute-start.4 = (bf16[1,256,256]{2,1,0:T(8,128)(2,1)S(1)}, bf16[1,256,256]{2,1,0:T(8,128)(2,1)S(1)}, u32[]{:S(2)}, u32[]{:S(2)}) collective-permute-start(bf16[1,256,256]{2,1,0:T(8,128)(2,1)S(1)} %pick.5.refs_0_), channel_id=1, source_target_pairs={{0,1},{1,0},{2,3},{3,2},{4,5},{5,4},{6,7},{7,6},{8,9},{9,8},{10,11... | collective-permute-start | bytes 393224 | tf_op jit(solution)/shard_map/ppermute | solution.py:584
  22.5 1.8 %collective-permute-start.6 = (bf16[1,256,256]{2,1,0:T(8,128)(2,1)S(1)}, bf16[1,256,256]{2,1,0:T(8,128)(2,1)S(1)}, u32[]{:S(2)}, u32[]{:S(2)}) collective-permute-start(bf16[1,256,256]{2,1,0:T(8,128)(2,1)S(1)} %get-tuple-element.86.refs_1_.refs_0_), channel_id=1, source_target_pairs={{0,1},{1,0},{2,3},{3,2},{4,5},{5,4},{6,7},{7,6},{8,9},{9,8},{10,11... | collective-permute-start | bytes 393224 | tf_op jit(solution)/shard_map/ppermute | solution.py:584
  23.0 8.8 %collective-permute-start.7 = (bf16[384,256]{1,0:T(8,128)(2,1)S(1)}, bf16[384,256]{1,0:T(8,128)(2,1)S(1)}, u32[]{:S(2)}, u32[]{:S(2)}) collective-permute-start(bf16[384,256]{1,0:T(8,128)(2,1)S(1)} %get-tuple-element.96), channel_id=1, source_target_pairs={{0,4},{1,5},{2,6},{3,7},{4,0},{5,1},{6,2},{7,3},{8,12},{9,13},{10,... | collective-permute-start | bytes 589832 | tf_op jit(solution)/shard_map/ppermute | solution.py:584
  23.7 3.9 %collective-permute-start.10 = (bf16[1,256,256]{2,1,0:T(8,128)(2,1)S(1)}, bf16[1,256,256]{2,1,0:T(8,128)(2,1)S(1)}, u32[]{:S(2)}, u32[]{:S(2)}) collective-permute-start(bf16[1,256,256]{2,1,0:T(8,128)(2,1)S(1)} %pick.6.refs_0_), channel_id=1, source_target_pairs={{0,1},{1,0},{2,3},{3,2},{4,5},{5,4},{6,7},{7,6},{8,9},{9,8},{10,11... | collective-permute-start | bytes 393224 | tf_op jit(solution)/shard_map/ppermute | solution.py:584
  27.5 1.6 %collective-permute-start.8 = (bf16[1,256,256]{2,1,0:T(8,128)(2,1)S(1)}, bf16[1,256,256]{2,1,0:T(8,128)(2,1)S(1)}, u32[]{:S(2)}, u32[]{:S(2)}) collective-permute-start(bf16[1,256,256]{2,1,0:T(8,128)(2,1)S(1)} %get-tuple-element.101), channel_id=1, source_target_pairs={{0,1},{1,0},{2,3},{3,2},{4,5},{5,4},{6,7},{7,6},{8,9},{9,8},{10,11... | collective-permute-start | bytes 393224 | tf_op jit(solution)/shard_map/ppermute | solution.py:584
  29.1 12.4 %collective-permute-start.15 = (bf16[384,256]{1,0:T(8,128)(2,1)S(1)}, bf16[384,256]{1,0:T(8,128)(2,1)S(1)}, u32[]{:S(2)}, u32[]{:S(2)}) collective-permute-start(bf16[384,256]{1,0:T(8,128)(2,1)S(1)} %finish.4.refs_1_), channel_id=1, source_target_pairs={{0,8},{1,9},{2,10},{3,11},{4,12},{5,13},{6,14},{7,15},{8,0},{9,1},... | collective-permute-start | bytes 589832 | tf_op jit(solution)/shard_map/ppermute | solution.py:584
  31.9 1.7 %collective-permute-start.13 = (bf16[1,256,256]{2,1,0:T(8,128)(2,1)S(1)}, bf16[1,256,256]{2,1,0:T(8,128)(2,1)S(1)}, u32[]{:S(2)}, u32[]{:S(2)}) collective-permute-start(bf16[1,256,256]{2,1,0:T(8,128)(2,1)S(1)} %pick.7.refs_8_.refs_0_), channel_id=1, source_target_pairs={{0,1},{1,0},{2,3},{3,2},{4,5},{5,4},{6,7},{7,6},{8,9},{9,8},{10,11... | collective-permute-start | bytes 393224 | tf_op jit(solution)/shard_map/ppermute | solution.py:584
  32.0 5.5 %collective-permute-start.12 = (bf16[1,256,256]{2,1,0:T(8,128)(2,1)S(1)}, bf16[1,256,256]{2,1,0:T(8,128)(2,1)S(1)}, u32[]{:S(2)}, u32[]{:S(2)}) collective-permute-start(bf16[1,256,256]{2,1,0:T(8,128)(2,1)S(1)} %get-tuple-element.112), channel_id=1, source_target_pairs={{0,1},{1,0},{2,3},{3,2},{4,5},{5,4},{6,7},{7,6},{8,9},{9,8},{10,11... | collective-permute-start | bytes 393224 | tf_op jit(solution)/shard_map/ppermute | solution.py:584
  33.5 4.5 %collective-permute-start.11 = (bf16[1,256,256]{2,1,0:T(8,128)(2,1)S(1)}, bf16[1,256,256]{2,1,0:T(8,128)(2,1)S(1)}, u32[]{:S(2)}, u32[]{:S(2)}) collective-permute-start(bf16[1,256,256]{2,1,0:T(8,128)(2,1)S(1)} %get-tuple-element.109), channel_id=1, source_target_pairs={{0,1},{1,0},{2,3},{3,2},{4,5},{5,4},{6,7},{7,6},{8,9},{9,8},{10,11... | collective-permute-start | bytes 393224 | tf_op jit(solution)/shard_map/ppermute | solution.py:584
  36.0 3.5 %collective-permute-start.18 = (bf16[128,128]{1,0:T(8,128)(2,1)S(1)}, bf16[128,128]{1,0:T(8,128)(2,1)S(1)}, u32[]{:S(2)}, u32[]{:S(2)}) collective-permute-start(bf16[128,128]{1,0:T(8,128)(2,1)S(1)} %get-tuple-element.127.refs_1_), channel_id=1, source_target_pairs={{0,1},{1,0},{2,3},{3,2},{4,5},{5,4},{6,7},{7,6},{8,9},{9,8},{10,11... | collective-permute-start | bytes 98312 | tf_op jit(solution)/shard_map/ppermute | solution.py:584
  37.6 12.9 %collective-permute-start.14 = (bf16[384,256]{1,0:T(8,128)(2,1)S(1)}, bf16[384,256]{1,0:T(8,128)(2,1)S(1)}, u32[]{:S(2)}, u32[]{:S(2)}) collective-permute-start(bf16[384,256]{1,0:T(8,128)(2,1)S(1)} %finish.6), channel_id=1, source_target_pairs={{0,4},{1,5},{2,6},{3,7},{4,0},{5,1},{6,2},{7,3},{8,12},{9,13},{10,... | collective-permute-start | bytes 589832 | tf_op jit(solution)/shard_map/ppermute | solution.py:584
  38.0 3.6 %collective-permute-start.16 = (bf16[1,256,256]{2,1,0:T(8,128)(2,1)S(1)}, bf16[1,256,256]{2,1,0:T(8,128)(2,1)S(1)}, u32[]{:S(2)}, u32[]{:S(2)}) collective-permute-start(bf16[1,256,256]{2,1,0:T(8,128)(2,1)S(1)} %get-tuple-element.119), channel_id=1, source_target_pairs={{0,1},{1,0},{2,3},{3,2},{4,5},{5,4},{6,7},{7,6},{8,9},{9,8},{10,11... | collective-permute-start | bytes 393224 | tf_op jit(solution)/shard_map/ppermute | solution.py:584
  38.0 6.3 %collective-permute-start.19 = (bf16[4,128,128]{2,1,0:T(8,128)(2,1)S(1)}, bf16[4,128,128]{2,1,0:T(8,128)(2,1)S(1)}, u32[]{:S(2)}, u32[]{:S(2)}) collective-permute-start(bf16[4,128,128]{2,1,0:T(8,128)(2,1)S(1)} %get-tuple-element.128), channel_id=1, source_target_pairs={{0,2},{1,3},{2,0},{3,1},{4,6},{5,7},{6,4},{7,5},{8,10},{9,11},{10,... | collective-permute-start | bytes 393224 | tf_op jit(solution)/shard_map/ppermute | solution.py:584
  39.8 7.6 %collective-permute-start.20 = (bf16[5,128,128]{2,1,0:T(8,128)(2,1)S(1)}, bf16[5,128,128]{2,1,0:T(8,128)(2,1)S(1)}, u32[]{:S(2)}, u32[]{:S(2)}) collective-permute-start(bf16[5,128,128]{2,1,0:T(8,128)(2,1)S(1)} %attach.3.refs_8_), channel_id=1, source_target_pairs={{0,2},{1,3},{2,0},{3,1},{4,6},{5,7},{6,4},{7,5},{8,10},{9,11},{10,... | collective-permute-start | bytes 491528 | tf_op jit(solution)/shard_map/ppermute | solution.py:584
  41.7 8.8 %collective-permute-start.17 = (bf16[384,256]{1,0:T(8,128)(2,1)S(1)}, bf16[384,256]{1,0:T(8,128)(2,1)S(1)}, u32[]{:S(2)}, u32[]{:S(2)}) collective-permute-start(bf16[384,256]{1,0:T(8,128)(2,1)S(1)} %finish.7), channel_id=1, source_target_pairs={{0,12},{1,13},{2,14},{3,15},{4,8},{5,9},{6,10},{7,11},{8,4},{9,5},... | collective-permute-start | bytes 589832 | tf_op jit(solution)/shard_map/ppermute | solution.py:584
  50.6 5.2 %collective-permute-start.21 = (bf16[256,256]{1,0:T(8,128)(2,1)S(1)}, bf16[256,256]{1,0:T(8,128)(2,1)S(1)}, u32[]{:S(2)}, u32[]{:S(2)}) collective-permute-start(bf16[256,256]{1,0:T(8,128)(2,1)S(1)} %get-tuple-element.131), channel_id=1, source_target_pairs={{0,2},{1,3},{2,0},{3,1},{4,6},{5,7},{6,4},{7,5},{8,10},{9,11},{10,... | collective-permute-start | bytes 393224 | tf_op jit(solution)/shard_map/ppermute | solution.py:584

commit v6 on v5

--- a/solution.py
+++ b/solution.py
@@ -15,6 +15,7 @@
 SLOTS = 32
 BACK_SLOTS = 16
 BACK_GROUP = 8
+TOTAL_LANES = 32
 COST = dict(first=1.5, pack=0.1, weights=1.3, pair=2.5, attach=0, pick=0, probs=0, prepare=0, work=0.0, scores=0.0, finish=0, pair_back=0, gather=5, settle=5, fold=0, last=0)
 VMEM = 20 * 1024 * 1024
 
@@ -421,13 +422,17 @@
             message[pl.ds(at, rows)] = (partial[a, pl.ds(at, rows)] + both[rows:]).astype(BF16)
 
 
+def first_heads(heads):
+    return heads * 5 // 8
+
+
 def scores_kernel(R, heads, count, *refs):
     mixed_grads, refs = refs[:count], refs[count:]
     values, refs = refs[:count], refs[count:]
     scales, *refs = refs
     exps, refs = refs[: 2 * R], refs[2 * R :]
     own_scores, total_ref, *messages = refs
-    half = heads // 2
+    half = first_heads(heads)
     rows, columns = total_ref.shape
     lane = iota((rows, columns), 1)
     sums = jnp.zeros((rows, columns), F32)
@@ -454,30 +459,41 @@
 
 
 def attach_total_kernel(heads, scores_ref, own_ref, other_ref, message):
-    count = scores_ref.shape[0]
-    message[0:count] = scores_ref[...]
+    count, rows, columns = scores_ref.shape
+    for h in range(count):
+        message[h * rows : (h + 1) * rows] = scores_ref[h]
     total = sum(joined_thirds(ref[...].astype(F32), heads) for ref in (own_ref, other_ref))
-    message[count] = thirds(total, heads).astype(BF16)
+    total = thirds(total, heads)
+    packed, size = 0.0, message.shape[0] - count * rows
+    for n in range(rows // size):
+        part = total[n * size : (n + 1) * size]
+        packed = packed + (pltpu.roll(part, n * TOTAL_LANES, 1) if n else part)
+    message[count * rows :] = packed.astype(BF16)
 
 
 def pair_back_kernel(R, heads, first, x_ref, e_ref, logit_ref, mean_ref, inverse_ref, scale_ref, own_ref, back_ref, *refs):
     own_total, received, refs = refs[0], refs[1 : 2 * R - 1], refs[2 * R - 1 :]
-    firsts, seconds, half = received[::2], received[1::2], heads // 2
+    firsts, seconds, half = received[::2], received[1::2], first_heads(heads)
     out_ref, done_ref, scratch, turned, rounded = refs
     count, columns, width = out_ref.shape
     here = pl.ds(pl.multiple_of(pl.program_id(0) * count, count), count)
     low = pl.multiple_of(first + pl.program_id(0) * count, count)
     at = pl.ds(low, count)
     done_ref[...] = jnp.zeros_like(done_ref)
-    total = sum(m[half, at].astype(F32) for m in (own_total, *seconds))
+    rows = own_ref.shape[1]
+    total = sum(m[(heads - half) * rows :].astype(F32) for m in (own_total, *seconds))
+    lanes = total.shape[1]
+    total = pltpu.roll(total, lax.rem(lanes - low // count * TOTAL_LANES, lanes), 1)
     total = joined_thirds(total, heads)
     scale = scale_ref[0, at]
     inverse = inverse_ref[here]
     cross = 0.0
     for h in range(heads):
         scores = own_ref[h, at]
-        for m in (firsts, seconds)[h // half]:
-            scores = scores + m[h % half, at].astype(F32)
+        for m in firsts if h < half else ():
+            scores = scores + m[h, at].astype(F32)
+        for m in () if h < half else seconds:
+            scores = scores + m[pl.ds(pl.multiple_of((h - half) * rows + low, count), count)].astype(F32)
         prob = e_ref[h, here].astype(F32) * scale[:, h : h + 1]
         grad = prob * (scores - total[:, h : h + 1])
         cross = cross + grad * logit_ref[h, here]
@@ -751,7 +767,11 @@
     own_scores, own_total, *scores = call(
         functools.partial(scores_kernel, R, heads, len(prepared)),
         [shape((heads, rows, columns), F32), shape((rows, columns), BF16)]
-        + [shape((heads // 2, rows, columns), BF16)] * (2 * R - 2),
+        + [
+            shape((count, rows, columns), BF16)
+            for _ in range(R - 1)
+            for count in (first_heads(heads), heads - first_heads(heads))
+        ],
         "scores",
         after=[],
         operands=(
@@ -764,7 +784,7 @@
         upper, lower = scores[2 * b - 2 : 2 * b]
         (lower,) = call(
             functools.partial(attach_total_kernel, heads),
-            [shape((heads // 2 + 1, rows, columns), BF16)],
+            [shape(((heads - first_heads(heads)) * rows + rows // 4, columns), BF16)],
             "attach",
             operands=(lower, own_total, other_total),
         )

time: 57.1 us -> 56.8 us (level)
  transfers between devices with their start and end apart: 22 -> 22, of which waited for: 7 -> 8; matrix products, arithmetic and copies ran while one was open for 0% -> 0% of each run, Pallas kernels for 39% -> 40%
where the time goes in v6:
time: 56.8 us; the launch traced here: 56.6 us
  Pallas kernels  25.6 us (45%)
  starting transfers between devices  21.3 us (38%)
  waiting for transfers between devices  7.98 us (14%)
  between operations  0.92 us (2%)
  local copies, waits for them, and re-layouts  0.83 us (1%)
    pallas_call x31, Pallas kernels, call(): pl.pallas_call(body, out_shape=out_shape, in_specs=[whole] * count + [pl....  25.6 us
    ppermute x22, starting transfers between devices, exchange(): lax.ppermute(value, everyone, [(at(z, x, c), at(z ^ dz, x ^ dx, c ^ dc))...  21.3 us
    ppermute x22, waiting for transfers between devices, exchange(): lax.ppermute(value, everyone, [(at(z, x, c), at(z ^ dz, x ^ dx, c ^ dc))...  7.98 us
  transfers between devices with their start and end apart: 22, of which 8 were waited for; matrix products, arithmetic and copies ran while one was open for 0% of the time, Pallas kernels for 40%

profile of v6, /device:TPU:0, one launch (start us, length us, event | category | flops | bytes accessed | tf_op | source)
XLA Modules:
  0.0 56.6 jit_solution(8265564709982688313)
XLA Ops:
  0.6 1.6 %first.1 = (f32[128,512]{1,0:T(8,128)S(1)}, f32[128,512]{1,0:T(8,128)S(1)}, f32[128,512]{1,0:T(8,128)S(1)}, f32[8,128]{1,0:T(8,128)S(1)}, bf16[256,256]{1,0:T(8,128)(2,1)S(1)}, /*index=5*/bf16[256,256]{1,0:T(8,128)(2,1)S(1)}) custom-call(s32[1,8]{1,0:T(1,128)} %bitcast.16, bf16[8,64,128]{2,1,0:T(8,128)(2,1)} %bitcast.10, bf16[8,64,128]{2,1,0:T(8,128)(2,1)} %bitcast.11, ...), custom_call_target="tpu_custom_call" | custom-call | flops 4499999744 | tf_op jit(solution)/shard_map/first/pallas_call | solution.py:59
  2.2 3.0 %collective-permute-start = (bf16[256,256]{1,0:T(8,128)(2,1)S(1)}, bf16[256,256]{1,0:T(8,128)(2,1)S(1)}, u32[]{:S(2)}, u32[]{:S(2)}) collective-permute-start(bf16[256,256]{1,0:T(8,128)(2,1)S(1)} %get-tuple-element.76), channel_id=1, source_target_pairs={{0,2},{1,3},{2,0},{3,1},{4,6},{5,7},{6,4},{7,5},{8,10},{9,11},{10,... | collective-permute-start | bytes 393224 | tf_op jit(solution)/shard_map/ppermute | solution.py:600
  5.3 1.4 %weights.1 = (bf16[256,1024]{1,0:T(8,128)(2,1)S(1)}, bf16[256,1024]{1,0:T(8,128)(2,1)S(1)}, bf16[256,1024]{1,0:T(8,128)(2,1)S(1)}, bf16[128,512]{1,0:T(8,128)(2,...) custom-call(bf16[64,256]{1,0:T(8,128)(2,1)} %refs_0_.5, ...), custom_call_target="tpu_custom_call" | custom-call | flops 3900000000 | tf_op jit(solution)/shard_map/weights/pallas_call | solution.py:59
  6.7 0.8 %copy-done = bf16[128,128,128]{2,1,0:T(8,128)(2,1)S(1)} copy-done((bf16[128,128,128]{2,1,0:T(8,128)(2,1)S(1)}, bf16[128,128,128]{2,1,0:T(8,128)(2,1)}, u32[]{:S(2)}) %copy-start) | copy-done | bytes 4194328
  7.5 2.9 %pair.2 = (bf16[8,64,128]{2,1,0:T(8,128)(2,1)S(1)}, bf16[64,128]{1,0:T(8,128)(2,1)S(1)}, f32[8,64,128]{2,1,0:T(8,128)S(1)}, f32[64,128]{1,0:T(8,128)S(1)}, f32[64,128]{1,0:T(8,128)S(1)}) custom-call(bf16[128,128,128]{2,1,0:T(8,128)(2,1)S(1)} %copy-done, bf16[128,512]{1,0:T(8,128)(2,1)S(1)} %get-tuple-element.77.refs_1_, ...), custom_call_target="tpu_custom_call" | custom-call | flops 7500000256 | tf_op jit(solution)/shard_map/pair/pallas_call | solution.py:59
  10.4 0.1 collective-permute-start.3
  10.5 0.0 collective-permute-done.refs_1_
  10.6 3.2 %collective-permute-start.1 = (bf16[384,256]{1,0:T(8,128)(2,1)S(1)}, bf16[384,256]{1,0:T(8,128)(2,1)S(1)}, u32[]{:S(2)}, u32[]{:S(2)}) collective-permute-start(bf16[384,256]{1,0:T(8,128)(2,1)S(1)} %get-tuple-element.82), channel_id=1, source_target_pairs={{0,8},{1,9},{2,10},{3,11},{4,12},{5,13},{6,14},{7,15},{8,0},{9,1},... | collective-permute-start | bytes 589832 | tf_op jit(solution)/shard_map/ppermute | solution.py:600
  13.7 1.6 %collective-permute-start.9 = (bf16[384,256]{1,0:T(8,128)(2,1)S(1)}, bf16[384,256]{1,0:T(8,128)(2,1)S(1)}, u32[]{:S(2)}, u32[]{:S(2)}) collective-permute-start(bf16[384,256]{1,0:T(8,128)(2,1)S(1)} %get-tuple-element.81.refs_6_.refs_2_.refs_0_), channel_id=1, source_target_pairs={{0,4},{1,5},{2,6},{3,7},{4,0},{5,1},{6,2},{7,3},{8,12},{9,13},{10,... | collective-permute-start | bytes 589832 | tf_op jit(solution)/shard_map/ppermute | solution.py:600
  15.3 2.9 %pair.3 = (bf16[8,64,128]{2,1,0:T(8,128)(2,1)S(1)}, bf16[128,128]{1,0:T(8,128)(2,1)S(1)}, f32[8,64,128]{2,1,0:T(8,128)S(1)}, f32[64,128]{1,0:T(8,128)S(1)}, f32[64,128]{1,0:T(8,128)S(1)}) custom-call(bf16[128,128,128]{2,1,0:T(8,128)(2,1)S(1)} %copy-done, bf16[128,512]{1,0:T(8,128)(2,1)S(1)} %get-tuple-element.77.refs_1_, ...), custom_call_target="tpu_custom_call" | custom-call | flops 7500000256 | tf_op jit(solution)/shard_map/pair/pallas_call | solution.py:59
  18.3 0.1 collective-permute-start.2
  18.3 0.0 collective-permute-done.3.refs_3_.refs_2_.refs_11_
  18.3 1.2 %collective-permute-done.2.refs_2_ = bf16[128,128]{1,0:T(8,128)(2,1)S(1)} collective-permute-done((bf16[128,128]{1,0:T(8,128)(2,1)S(1)}, bf16[128,128]{1,0:T(8,128)(2,1)S(1)}, u32[]{:S(2)}, u32[]{:S(2)}) %collective-permute-start.2) | collective-permute-done | bytes 32800 | tf_op jit(solution)/shard_map/ppermute | solution.py:600
  19.5 0.1 attach.2.refs_1_.refs_10_
  19.6 1.6 %collective-permute-start.5 = (bf16[10,64,128]{2,1,0:T(8,128)(2,1)S(1)}, bf16[10,64,128]{2,1,0:T(8,128)(2,1)S(1)}, u32[]{:S(2)}, u32[]{:S(2)}) collective-permute-start(bf16[10,64,128]{2,1,0:T(8,128)(2,1)S(1)} %attach.2.refs_1_.refs_10_), channel_id=1, source_target_pairs={{0,2},{1,3},{2,0},{3,1},{4,6},{5,7},{6,4},{7,5},{8,10},{9,11},{10,... | collective-permute-start | bytes 491528 | tf_op jit(solution)/shard_map/ppermute | solution.py:600
  21.2 1.2 %collective-permute-done.1.refs_0_.refs_3_.refs_2_ = bf16[384,256]{1,0:T(8,128)(2,1)S(1)} collective-permute-done((bf16[384,256]{1,0:T(8,128)(2,1)S(1)}, bf16[384,256]{1,0:T(8,128)(2,1)S(1)}, u32[]{:S(2)}, u32[]{:S(2)}) %collective-permute-start.1) | collective-permute-done | bytes 196640 | tf_op jit(solution)/shard_map/ppermute | solution.py:600
  22.5 0.1 collective-permute-start.4
  22.5 0.5 collective-permute-start.6
  23.0 0.6 %collective-permute-start.7 = (bf16[384,256]{1,0:T(8,128)(2,1)S(1)}, bf16[384,256]{1,0:T(8,128)(2,1)S(1)}, u32[]{:S(2)}, u32[]{:S(2)}) collective-permute-start(bf16[384,256]{1,0:T(8,128)(2,1)S(1)} %get-tuple-element.96), channel_id=1, source_target_pairs={{0,4},{1,5},{2,6},{3,7},{4,0},{5,1},{6,2},{7,3},{8,12},{9,13},{10,... | collective-permute-start | bytes 589832 | tf_op jit(solution)/shard_map/ppermute | solution.py:600
  23.7 0.0 collective-permute-done.9.refs_0_.refs_2_
  23.7 0.1 collective-permute-start.10
  23.8 0.1 collective-permute-done.4.refs_1_
  23.9 0.5 prepare.4
  24.4 0.0 collective-permute-done.6.refs_1_
  24.4 0.5 prepare.5
  24.9 1.1 %collective-permute-done.5.refs_3_.refs_12_ = bf16[10,64,128]{2,1,0:T(8,128)(2,1)S(1)} collective-permute-done((bf16[10,64,128]{2,1,0:T(8,128)(2,1)S(1)}, bf16[10,64,128]{2,1,0:T(8,128)(2,1)S(1)}, u32[]{:S(2)}, u32[]{:S(2)}) %collective-permute-start.5) | collective-permute-done | bytes 163872 | tf_op jit(solution)/shard_map/ppermute | solution.py:600
  25.9 0.6 %probs.1 = (bf16[8,128,256]{2,1,0:T(8,128)(2,1)S(1)}, f32[2,128,128]{2,1,0:T(8,128)S(1)}) custom-call(bf16[8,64,128]{2,1,0:T(8,128)(2,1)S(1)} %get-tuple-element.85.refs_0_.refs_9_.refs_1_, bf16[10,64,128]{2,1,0:T(8,128)(2,1)S(1)} %attach.2.refs_1_.refs_10_, bf16[8,64,128]{2,1,0:T(8,128)(2,1)S(1)} %collective-permute-done.3.refs_3_.refs_2_.refs_11_, ...), custom_call_target="tpu_custom_call" | custom-call | tf_op jit(solution)/shard_map/probs/pallas_call | solution.py:59
  26.5 1.0 %work.4 = (f32[1,256,256]{2,1,0:T(8,128)S(1)}, bf16[1,256,256]{2,1,0:T(8,128)(2,1)S(1)}, f32[1,256,256]{2,1,0:T(8,128)S(1)}) custom-call(bf16[8,256,128]{2,1,0:T(8,128)(2,1)S(1)} %get-tuple-element.97.refs_0_.refs_4_, bf16[8,128,128]{2,1,0:T(8,128)(2,1)S(1)} %get-tuple-element.94.refs_4_.refs_1_.refs_0_, f32[1,128,1024]{2,1,0:T(8,128)S(1)} %get-tuple-element.98.refs_2_, ...), custom_call_target="tpu_custom_call" | custom-call | tf_op jit(solution)/shard_map/work/pallas_call | solution.py:59
  27.5 0.1 collective-permute-start.8
  27.6 0.0 collective-permute-done.10.refs_1_
  27.6 0.5 prepare.6
  28.1 1.0 %work.5 = (f32[1,256,256]{2,1,0:T(8,128)S(1)}, bf16[1,256,256]{2,1,0:T(8,128)(2,1)S(1)}, f32[1,256,256]{2,1,0:T(8,128)S(1)}) custom-call(bf16[8,256,128]{2,1,0:T(8,128)(2,1)S(1)} %get-tuple-element.103.refs_0_.refs_6_, bf16[8,128,128]{2,1,0:T(8,128)(2,1)S(1)} %get-tuple-element.104.refs_1_.refs_2_, f32[1,128,1024]{2,1,0:T(8,128)S(1)} %get-tuple-element.105.refs_2_, ...), custom_call_target="tpu_custom_call" | custom-call | tf_op jit(solution)/shard_map/work/pallas_call | solution.py:59
  29.1 2.7 %collective-permute-start.15 = (bf16[384,256]{1,0:T(8,128)(2,1)S(1)}, bf16[384,256]{1,0:T(8,128)(2,1)S(1)}, u32[]{:S(2)}, u32[]{:S(2)}) collective-permute-start(bf16[384,256]{1,0:T(8,128)(2,1)S(1)} %finish.4.refs_1_), channel_id=1, source_target_pairs={{0,8},{1,9},{2,10},{3,11},{4,12},{5,13},{6,14},{7,15},{8,0},{9,1},... | collective-permute-start | bytes 589832 | tf_op jit(solution)/shard_map/ppermute | solution.py:600
  31.9 0.0 collective-permute-done.7.refs_0_.refs_2_
  31.9 0.1 collective-permute-start.13
  32.0 0.5 collective-permute-start.12
  32.5 1.0 %work.6 = (f32[1,256,256]{2,1,0:T(8,128)S(1)}, bf16[1,256,256]{2,1,0:T(8,128)(2,1)S(1)}, f32[1,256,256]{2,1,0:T(8,128)S(1)}) custom-call(bf16[8,256,128]{2,1,0:T(8,128)(2,1)S(1)} %get-tuple-element.90.refs_0_.refs_5_, bf16[8,128,128]{2,1,0:T(8,128)(2,1)S(1)} %get-tuple-element.91.refs_5_.refs_1_, f32[1,128,1024]{2,1,0:T(8,128)S(1)} %get-tuple-element.92.refs_2_, ...), custom_call_target="tpu_custom_call" | custom-call | tf_op jit(solution)/shard_map/work/pallas_call | solution.py:59
  33.4 0.1 collective-permute-start.11
  33.6 0.0 collective-permute-done.13.refs_1_
  33.6 0.7 %prepare.7 = (bf16[8,256,128]{2,1,0:T(8,128)(2,1)S(1)}, bf16[8,128,128]{2,1,0:T(8,128)(2,1)S(1)}, f32[1,128,1024]{2,1,0:T(8,128)S(1)}, f32[1,128,1024]{2,1,0:T(8,128)S(1)}) custom-call(bf16[1,256,256]{2,1,0:T(8,128)(2,1)S(1)} %pick.7.refs_8_.refs_0_, bf16[1,256,256]{2,1,0:T(8,128)(2,1)S(1)} %collective-permute-done.13.refs_1_, ...), custom_call_target="tpu_custom_call" | custom-call | tf_op jit(solution)/shard_map/prepare/pallas_call | solution.py:59
  34.2 1.8 %scores.1 = (f32[8,128,128]{2,1,0:T(8,128)S(1)}, bf16[128,128]{1,0:T(8,128)(2,1)S(1)}, bf16[5,128,128]{2,1,0:T(8,128)(2,1)S(1)}, bf16[3,128,128]{2,1,0:T(8,128)(2,1)S(1)}) custom-call(bf16[8,128,128]{2,1,0:T(8,128)(2,1)S(1)} %get-tuple-element.94.refs_4_.refs_1_.refs_0_, bf16[8,128,128]{2,1,0:T(8,128)(2,1)S(1)} %get-tuple-element.91.refs_5_.refs_1_, ...), custom_call_target="tpu_custom_call" | custom-call | tf_op jit(solution)/shard_map/scores/pallas_call | solution.py:59
  36.0 0.5 collective-permute-start.18
  36.5 1.0 %work.7 = (f32[1,256,256]{2,1,0:T(8,128)S(1)}, bf16[1,256,256]{2,1,0:T(8,128)(2,1)S(1)}, f32[1,256,256]{2,1,0:T(8,128)S(1)}) custom-call(bf16[8,256,128]{2,1,0:T(8,128)(2,1)S(1)} %get-tuple-element.113.refs_0_.refs_7_, bf16[8,128,128]{2,1,0:T(8,128)(2,1)S(1)} %get-tuple-element.114.refs_1_.refs_3_, f32[1,128,1024]{2,1,0:T(8,128)S(1)} %get-tuple-element.115.refs_2_, ...), custom_call_target="tpu_custom_call" | custom-call | tf_op jit(solution)/shard_map/work/pallas_call | solution.py:59
  37.5 0.1 finish.6
  37.6 0.4 collective-permute-start.14
  38.0 0.0 collective-permute-start.16
  38.0 0.0 collective-permute-done.11.refs_1_
  38.0 1.5 %collective-permute-start.19 = (bf16[5,128,128]{2,1,0:T(8,128)(2,1)S(1)}, bf16[5,128,128]{2,1,0:T(8,128)(2,1)S(1)}, u32[]{:S(2)}, u32[]{:S(2)}) collective-permute-start(bf16[5,128,128]{2,1,0:T(8,128)(2,1)S(1)} %get-tuple-element.128), channel_id=1, source_target_pairs={{0,2},{1,3},{2,0},{3,1},{4,6},{5,7},{6,4},{7,5},{8,10},{9,11},{10,... | collective-permute-start | bytes 491528 | tf_op jit(solution)/shard_map/ppermute | solution.py:600
  39.5 0.1 finish.5.refs_0_
  39.5 0.3 attach.3.refs_8_
  39.8 0.6 %collective-permute-start.20 = (bf16[416,128]{1,0:T(8,128)(2,1)S(1)}, bf16[416,128]{1,0:T(8,128)(2,1)S(1)}, u32[]{:S(2)}, u32[]{:S(2)}) collective-permute-start(bf16[416,128]{1,0:T(8,128)(2,1)S(1)} %attach.3.refs_8_), channel_id=1, source_target_pairs={{0,2},{1,3},{2,0},{3,1},{4,6},{5,7},{6,4},{7,5},{8,10},{9,11},{10,... | collective-permute-start | bytes 319496 | tf_op jit(solution)/shard_map/ppermute | solution.py:600
  40.4 1.2 %collective-permute-done.15.refs_1_.refs_2_ = bf16[384,256]{1,0:T(8,128)(2,1)S(1)} collective-permute-done((bf16[384,256]{1,0:T(8,128)(2,1)S(1)}, bf16[384,256]{1,0:T(8,128)(2,1)S(1)}, u32[]{:S(2)}, u32[]{:S(2)}) %collective-permute-start.15) | collective-permute-done | bytes 196640 | tf_op jit(solution)/shard_map/ppermute | solution.py:600
  41.6 0.1 finish.7
  41.7 2.5 %collective-permute-start.17 = (bf16[384,256]{1,0:T(8,128)(2,1)S(1)}, bf16[384,256]{1,0:T(8,128)(2,1)S(1)}, u32[]{:S(2)}, u32[]{:S(2)}) collective-permute-start(bf16[384,256]{1,0:T(8,128)(2,1)S(1)} %finish.7), channel_id=1, source_target_pairs={{0,12},{1,13},{2,14},{3,15},{4,8},{5,9},{6,10},{7,11},{8,4},{9,5},... | collective-permute-start | bytes 589832 | tf_op jit(solution)/shard_map/ppermute | solution.py:600
  44.2 2.7 %collective-permute-done.20.refs_1_.refs_10_ = bf16[416,128]{1,0:T(8,128)(2,1)S(1)} collective-permute-done((bf16[416,128]{1,0:T(8,128)(2,1)S(1)}, bf16[416,128]{1,0:T(8,128)(2,1)S(1)}, u32[]{:S(2)}, u32[]{:S(2)}) %collective-permute-start.20) | collective-permute-done | bytes 106528 | tf_op jit(solution)/shard_map/ppermute | solution.py:600
  46.9 0.0 collective-permute-done.19.refs_0_.refs_9_
  46.9 3.3 %pair_back.2 = (bf16[128,128,128]{2,1,0:T(8,128)(2,1)}, f32[8,128]{1,0:T(8,128)S(1)}) custom-call(bf16[128,128,128]{2,1,0:T(8,128)(2,1)S(1)} %copy-done, bf16[8,64,128]{2,1,0:T(8,128)(2,1)S(1)} %get-tuple-element.85.refs_0_.refs_9_.refs_1_, f32[8,64,128]{2,1,0:T(8,128)S(1)} %get-tuple-element.120.refs_2_, f32[64,128]{1,0:T(8,128)S(1)} %get-tuple-element.121.refs_3_, ...), custom_call_target="tpu_custom_call" | custom-call | tf_op jit(solution)/shard_map/pair_back/pallas_call | solution.py:59
  50.1 0.0 collective-permute-done.14.refs_1_
  50.1 0.2 collective-permute-done.17.refs_3_
  50.4 0.1 fold.1
  50.5 1.6 %collective-permute-start.21 = (bf16[256,256]{1,0:T(8,128)(2,1)S(1)}, bf16[256,256]{1,0:T(8,128)(2,1)S(1)}, u32[]{:S(2)}, u32[]{:S(2)}) collective-permute-start(bf16[256,256]{1,0:T(8,128)(2,1)S(1)} %get-tuple-element.131), channel_id=1, source_target_pairs={{0,2},{1,3},{2,0},{3,1},{4,6},{5,7},{6,4},{7,5},{8,10},{9,11},{10,... | collective-permute-start | bytes 393224 | tf_op jit(solution)/shard_map/ppermute | solution.py:600
  52.0 3.3 %pair_back.3 = (bf16[128,128,128]{2,1,0:T(8,128)(2,1)}, f32[8,128]{1,0:T(8,128)}) custom-call(bf16[128,128,128]{2,1,0:T(8,128)(2,1)S(1)} %copy-done, bf16[8,64,128]{2,1,0:T(8,128)(2,1)S(1)} %get-tuple-element.83.refs_0_.refs_1_, f32[8,64,128]{2,1,0:T(8,128)S(1)} %get-tuple-element.134.refs_2_, ...), custom_call_target="tpu_custom_call", output_to_operand_aliasing={{0}: (12, {})} | custom-call | tf_op jit(solution)/shard_map/pair_back/pallas_call | solution.py:59
  55.3 0.2 collective-permute-done.21.refs_5_
  55.5 1.1 %last.1 = (bf16[8,64,128]{2,1,0:T(8,128)(2,1)}, bf16[8,64,128]{2,1,0:T(8,128)(2,1)}) custom-call(f32[128,512]{1,0:T(8,128)S(1)} %get-tuple-element.71.refs_0_, f32[128,512]{1,0:T(8,128)S(1)} %get-tuple-element.72.refs_1_, f32[128,512]{1,0:T(8,128)S(1)} %get-tuple-element.73.refs_2_, f32[8,128]{1,0:T(8,128)S(1)} %get-tuple-element.74.refs_3_, ...), custom_call_target="tpu_custom_call" | custom-call | tf_op jit(solution)/shard_map/last/pallas_call | solution.py:59
  (13 shorter events, 0.2 us)
Async XLA Ops:
  2.2 8.3 %collective-permute-start = (bf16[256,256]{1,0:T(8,128)(2,1)S(1)}, bf16[256,256]{1,0:T(8,128)(2,1)S(1)}, u32[]{:S(2)}, u32[]{:S(2)}) collective-permute-start(bf16[256,256]{1,0:T(8,128)(2,1)S(1)} %get-tuple-element.76), channel_id=1, source_target_pairs={{0,2},{1,3},{2,0},{3,1},{4,6},{5,7},{6,4},{7,5},{8,10},{9,11},{10,... | collective-permute-start | bytes 393224 | tf_op jit(solution)/shard_map/ppermute | solution.py:600
  5.2 2.3 %copy-start = (bf16[128,128,128]{2,1,0:T(8,128)(2,1)S(1)}, bf16[128,128,128]{2,1,0:T(8,128)(2,1)}, u32[]{:S(2)}) copy-start(bf16[128,128,128]{2,1,0:T(8,128)(2,1)} %refs_0_.9) | copy-start | bytes 12582916
  10.4 7.9 %collective-permute-start.3 = (bf16[8,64,128]{2,1,0:T(8,128)(2,1)S(1)}, bf16[8,64,128]{2,1,0:T(8,128)(2,1)S(1)}, u32[]{:S(2)}, u32[]{:S(2)}) collective-permute-start(bf16[8,64,128]{2,1,0:T(8,128)(2,1)S(1)} %get-tuple-element.85.refs_0_.refs_9_.refs_1_), channel_id=1, source_target_pairs={{0,2},{1,3},{2,0},{3,1},{4,6},{5,7},{6,4},{7,5},{8,10},{9,11},{10,... | collective-permute-start | bytes 393224 | tf_op jit(solution)/shard_map/ppermute | solution.py:600
  10.6 11.8 %collective-permute-start.1 = (bf16[384,256]{1,0:T(8,128)(2,1)S(1)}, bf16[384,256]{1,0:T(8,128)(2,1)S(1)}, u32[]{:S(2)}, u32[]{:S(2)}) collective-permute-start(bf16[384,256]{1,0:T(8,128)(2,1)S(1)} %get-tuple-element.82), channel_id=1, source_target_pairs={{0,8},{1,9},{2,10},{3,11},{4,12},{5,13},{6,14},{7,15},{8,0},{9,1},... | collective-permute-start | bytes 589832 | tf_op jit(solution)/shard_map/ppermute | solution.py:600
  13.7 9.9 %collective-permute-start.9 = (bf16[384,256]{1,0:T(8,128)(2,1)S(1)}, bf16[384,256]{1,0:T(8,128)(2,1)S(1)}, u32[]{:S(2)}, u32[]{:S(2)}) collective-permute-start(bf16[384,256]{1,0:T(8,128)(2,1)S(1)} %get-tuple-element.81.refs_6_.refs_2_.refs_0_), channel_id=1, source_target_pairs={{0,4},{1,5},{2,6},{3,7},{4,0},{5,1},{6,2},{7,3},{8,12},{9,13},{10,... | collective-permute-start | bytes 589832 | tf_op jit(solution)/shard_map/ppermute | solution.py:600
  18.3 1.3 %collective-permute-start.2 = (bf16[128,128]{1,0:T(8,128)(2,1)S(1)}, bf16[128,128]{1,0:T(8,128)(2,1)S(1)}, u32[]{:S(2)}, u32[]{:S(2)}) collective-permute-start(bf16[128,128]{1,0:T(8,128)(2,1)S(1)} %get-tuple-element.84.refs_1_), channel_id=1, source_target_pairs={{0,1},{1,0},{2,3},{3,2},{4,5},{5,4},{6,7},{7,6},{8,9},{9,8},{10,11... | collective-permute-start | bytes 98312 | tf_op jit(solution)/shard_map/ppermute | solution.py:600
  19.6 6.3 %collective-permute-start.5 = (bf16[10,64,128]{2,1,0:T(8,128)(2,1)S(1)}, bf16[10,64,128]{2,1,0:T(8,128)(2,1)S(1)}, u32[]{:S(2)}, u32[]{:S(2)}) collective-permute-start(bf16[10,64,128]{2,1,0:T(8,128)(2,1)S(1)} %attach.2.refs_1_.refs_10_), channel_id=1, source_target_pairs={{0,2},{1,3},{2,0},{3,1},{4,6},{5,7},{6,4},{7,5},{8,10},{9,11},{10,... | collective-permute-start | bytes 491528 | tf_op jit(solution)/shard_map/ppermute | solution.py:600
  22.5 1.4 %collective-permute-start.4 = (bf16[1,256,256]{2,1,0:T(8,128)(2,1)S(1)}, bf16[1,256,256]{2,1,0:T(8,128)(2,1)S(1)}, u32[]{:S(2)}, u32[]{:S(2)}) collective-permute-start(bf16[1,256,256]{2,1,0:T(8,128)(2,1)S(1)} %pick.5.refs_0_), channel_id=1, source_target_pairs={{0,1},{1,0},{2,3},{3,2},{4,5},{5,4},{6,7},{7,6},{8,9},{9,8},{10,11... | collective-permute-start | bytes 393224 | tf_op jit(solution)/shard_map/ppermute | solution.py:600
  22.5 1.8 %collective-permute-start.6 = (bf16[1,256,256]{2,1,0:T(8,128)(2,1)S(1)}, bf16[1,256,256]{2,1,0:T(8,128)(2,1)S(1)}, u32[]{:S(2)}, u32[]{:S(2)}) collective-permute-start(bf16[1,256,256]{2,1,0:T(8,128)(2,1)S(1)} %get-tuple-element.86.refs_1_.refs_0_), channel_id=1, source_target_pairs={{0,1},{1,0},{2,3},{3,2},{4,5},{5,4},{6,7},{7,6},{8,9},{9,8},{10,11... | collective-permute-start | bytes 393224 | tf_op jit(solution)/shard_map/ppermute | solution.py:600
  23.0 8.8 %collective-permute-start.7 = (bf16[384,256]{1,0:T(8,128)(2,1)S(1)}, bf16[384,256]{1,0:T(8,128)(2,1)S(1)}, u32[]{:S(2)}, u32[]{:S(2)}) collective-permute-start(bf16[384,256]{1,0:T(8,128)(2,1)S(1)} %get-tuple-element.96), channel_id=1, source_target_pairs={{0,4},{1,5},{2,6},{3,7},{4,0},{5,1},{6,2},{7,3},{8,12},{9,13},{10,... | collective-permute-start | bytes 589832 | tf_op jit(solution)/shard_map/ppermute | solution.py:600
  23.7 3.9 %collective-permute-start.10 = (bf16[1,256,256]{2,1,0:T(8,128)(2,1)S(1)}, bf16[1,256,256]{2,1,0:T(8,128)(2,1)S(1)}, u32[]{:S(2)}, u32[]{:S(2)}) collective-permute-start(bf16[1,256,256]{2,1,0:T(8,128)(2,1)S(1)} %pick.6.refs_0_), channel_id=1, source_target_pairs={{0,1},{1,0},{2,3},{3,2},{4,5},{5,4},{6,7},{7,6},{8,9},{9,8},{10,11... | collective-permute-start | bytes 393224 | tf_op jit(solution)/shard_map/ppermute | solution.py:600
  27.5 1.6 %collective-permute-start.8 = (bf16[1,256,256]{2,1,0:T(8,128)(2,1)S(1)}, bf16[1,256,256]{2,1,0:T(8,128)(2,1)S(1)}, u32[]{:S(2)}, u32[]{:S(2)}) collective-permute-start(bf16[1,256,256]{2,1,0:T(8,128)(2,1)S(1)} %get-tuple-element.101), channel_id=1, source_target_pairs={{0,1},{1,0},{2,3},{3,2},{4,5},{5,4},{6,7},{7,6},{8,9},{9,8},{10,11... | collective-permute-start | bytes 393224 | tf_op jit(solution)/shard_map/ppermute | solution.py:600
  29.1 12.4 %collective-permute-start.15 = (bf16[384,256]{1,0:T(8,128)(2,1)S(1)}, bf16[384,256]{1,0:T(8,128)(2,1)S(1)}, u32[]{:S(2)}, u32[]{:S(2)}) collective-permute-start(bf16[384,256]{1,0:T(8,128)(2,1)S(1)} %finish.4.refs_1_), channel_id=1, source_target_pairs={{0,8},{1,9},{2,10},{3,11},{4,12},{5,13},{6,14},{7,15},{8,0},{9,1},... | collective-permute-start | bytes 589832 | tf_op jit(solution)/shard_map/ppermute | solution.py:600
  31.9 1.7 %collective-permute-start.13 = (bf16[1,256,256]{2,1,0:T(8,128)(2,1)S(1)}, bf16[1,256,256]{2,1,0:T(8,128)(2,1)S(1)}, u32[]{:S(2)}, u32[]{:S(2)}) collective-permute-start(bf16[1,256,256]{2,1,0:T(8,128)(2,1)S(1)} %pick.7.refs_8_.refs_0_), channel_id=1, source_target_pairs={{0,1},{1,0},{2,3},{3,2},{4,5},{5,4},{6,7},{7,6},{8,9},{9,8},{10,11... | collective-permute-start | bytes 393224 | tf_op jit(solution)/shard_map/ppermute | solution.py:600
  32.0 5.5 %collective-permute-start.12 = (bf16[1,256,256]{2,1,0:T(8,128)(2,1)S(1)}, bf16[1,256,256]{2,1,0:T(8,128)(2,1)S(1)}, u32[]{:S(2)}, u32[]{:S(2)}) collective-permute-start(bf16[1,256,256]{2,1,0:T(8,128)(2,1)S(1)} %get-tuple-element.112), channel_id=1, source_target_pairs={{0,1},{1,0},{2,3},{3,2},{4,5},{5,4},{6,7},{7,6},{8,9},{9,8},{10,11... | collective-permute-start | bytes 393224 | tf_op jit(solution)/shard_map/ppermute | solution.py:600
  33.4 4.5 %collective-permute-start.11 = (bf16[1,256,256]{2,1,0:T(8,128)(2,1)S(1)}, bf16[1,256,256]{2,1,0:T(8,128)(2,1)S(1)}, u32[]{:S(2)}, u32[]{:S(2)}) collective-permute-start(bf16[1,256,256]{2,1,0:T(8,128)(2,1)S(1)} %get-tuple-element.109), channel_id=1, source_target_pairs={{0,1},{1,0},{2,3},{3,2},{4,5},{5,4},{6,7},{7,6},{8,9},{9,8},{10,11... | collective-permute-start | bytes 393224 | tf_op jit(solution)/shard_map/ppermute | solution.py:600
  36.0 3.5 %collective-permute-start.18 = (bf16[128,128]{1,0:T(8,128)(2,1)S(1)}, bf16[128,128]{1,0:T(8,128)(2,1)S(1)}, u32[]{:S(2)}, u32[]{:S(2)}) collective-permute-start(bf16[128,128]{1,0:T(8,128)(2,1)S(1)} %get-tuple-element.127.refs_1_), channel_id=1, source_target_pairs={{0,1},{1,0},{2,3},{3,2},{4,5},{5,4},{6,7},{7,6},{8,9},{9,8},{10,11... | collective-permute-start | bytes 98312 | tf_op jit(solution)/shard_map/ppermute | solution.py:600
  37.6 12.6 %collective-permute-start.14 = (bf16[384,256]{1,0:T(8,128)(2,1)S(1)}, bf16[384,256]{1,0:T(8,128)(2,1)S(1)}, u32[]{:S(2)}, u32[]{:S(2)}) collective-permute-start(bf16[384,256]{1,0:T(8,128)(2,1)S(1)} %finish.6), channel_id=1, source_target_pairs={{0,4},{1,5},{2,6},{3,7},{4,0},{5,1},{6,2},{7,3},{8,12},{9,13},{10,... | collective-permute-start | bytes 589832 | tf_op jit(solution)/shard_map/ppermute | solution.py:600
  38.0 3.6 %collective-permute-start.16 = (bf16[1,256,256]{2,1,0:T(8,128)(2,1)S(1)}, bf16[1,256,256]{2,1,0:T(8,128)(2,1)S(1)}, u32[]{:S(2)}, u32[]{:S(2)}) collective-permute-start(bf16[1,256,256]{2,1,0:T(8,128)(2,1)S(1)} %get-tuple-element.119), channel_id=1, source_target_pairs={{0,1},{1,0},{2,3},{3,2},{4,5},{5,4},{6,7},{7,6},{8,9},{9,8},{10,11... | collective-permute-start | bytes 393224 | tf_op jit(solution)/shard_map/ppermute | solution.py:600
  38.0 8.9 %collective-permute-start.19 = (bf16[5,128,128]{2,1,0:T(8,128)(2,1)S(1)}, bf16[5,128,128]{2,1,0:T(8,128)(2,1)S(1)}, u32[]{:S(2)}, u32[]{:S(2)}) collective-permute-start(bf16[5,128,128]{2,1,0:T(8,128)(2,1)S(1)} %get-tuple-element.128), channel_id=1, source_target_pairs={{0,2},{1,3},{2,0},{3,1},{4,6},{5,7},{6,4},{7,5},{8,10},{9,11},{10,... | collective-permute-start | bytes 491528 | tf_op jit(solution)/shard_map/ppermute | solution.py:600
  39.8 7.1 %collective-permute-start.20 = (bf16[416,128]{1,0:T(8,128)(2,1)S(1)}, bf16[416,128]{1,0:T(8,128)(2,1)S(1)}, u32[]{:S(2)}, u32[]{:S(2)}) collective-permute-start(bf16[416,128]{1,0:T(8,128)(2,1)S(1)} %attach.3.refs_8_), channel_id=1, source_target_pairs={{0,2},{1,3},{2,0},{3,1},{4,6},{5,7},{6,4},{7,5},{8,10},{9,11},{10,... | collective-permute-start | bytes 319496 | tf_op jit(solution)/shard_map/ppermute | solution.py:600
  41.7 8.7 %collective-permute-start.17 = (bf16[384,256]{1,0:T(8,128)(2,1)S(1)}, bf16[384,256]{1,0:T(8,128)(2,1)S(1)}, u32[]{:S(2)}, u32[]{:S(2)}) collective-permute-start(bf16[384,256]{1,0:T(8,128)(2,1)S(1)} %finish.7), channel_id=1, source_target_pairs={{0,12},{1,13},{2,14},{3,15},{4,8},{5,9},{6,10},{7,11},{8,4},{9,5},... | collective-permute-start | bytes 589832 | tf_op jit(solution)/shard_map/ppermute | solution.py:600
  50.5 5.0 %collective-permute-start.21 = (bf16[256,256]{1,0:T(8,128)(2,1)S(1)}, bf16[256,256]{1,0:T(8,128)(2,1)S(1)}, u32[]{:S(2)}, u32[]{:S(2)}) collective-permute-start(bf16[256,256]{1,0:T(8,128)(2,1)S(1)} %get-tuple-element.131), channel_id=1, source_target_pairs={{0,2},{1,3},{2,0},{3,1},{4,6},{5,7},{6,4},{7,5},{8,10},{9,11},{10,... | collective-permute-start | bytes 393224 | tf_op jit(solution)/shard_map/ppermute | solution.py:600

commit v7 on v6

--- a/solution.py
+++ b/solution.py
@@ -423,7 +423,7 @@
 
 
 def first_heads(heads):
-    return heads * 5 // 8
+    return heads * 6 // 8
 
 
 def scores_kernel(R, heads, count, *refs):

time: 56.8 us -> 56.8 us (level)
  no operation moved by 1% of the time
where the time goes in v7:
time: 56.8 us; the launch traced here: 56.6 us
  Pallas kernels  25.6 us (45%)
  starting transfers between devices  21.3 us (38%)
  waiting for transfers between devices  7.97 us (14%)
  between operations  0.92 us (2%)
  local copies, waits for them, and re-layouts  0.83 us (1%)
    pallas_call x31, Pallas kernels, call(): pl.pallas_call(body, out_shape=out_shape, in_specs=[whole] * count + [pl....  25.6 us
    ppermute x22, starting transfers between devices, exchange(): lax.ppermute(value, everyone, [(at(z, x, c), at(z ^ dz, x ^ dx, c ^ dc))...  21.3 us
    ppermute x22, waiting for transfers between devices, exchange(): lax.ppermute(value, everyone, [(at(z, x, c), at(z ^ dz, x ^ dx, c ^ dc))...  7.97 us
  transfers between devices with their start and end apart: 22, of which 8 were waited for; matrix products, arithmetic and copies ran while one was open for 0% of the time, Pallas kernels for 40%

profile of v7, /device:TPU:0, one launch (start us, length us, event | category | flops | bytes accessed | tf_op | source)
XLA Modules:
  0.0 56.6 jit_solution(1479149371121852507)
XLA Ops:
  0.6 1.6 %first.1 = (f32[128,512]{1,0:T(8,128)S(1)}, f32[128,512]{1,0:T(8,128)S(1)}, f32[128,512]{1,0:T(8,128)S(1)}, f32[8,128]{1,0:T(8,128)S(1)}, bf16[256,256]{1,0:T(8,128)(2,1)S(1)}, /*index=5*/bf16[256,256]{1,0:T(8,128)(2,1)S(1)}) custom-call(s32[1,8]{1,0:T(1,128)} %bitcast.16, bf16[8,64,128]{2,1,0:T(8,128)(2,1)} %bitcast.10, bf16[8,64,128]{2,1,0:T(8,128)(2,1)} %bitcast.11, ...), custom_call_target="tpu_custom_call" | custom-call | flops 4499999744 | tf_op jit(solution)/shard_map/first/pallas_call | solution.py:59
  2.2 3.0 %collective-permute-start = (bf16[256,256]{1,0:T(8,128)(2,1)S(1)}, bf16[256,256]{1,0:T(8,128)(2,1)S(1)}, u32[]{:S(2)}, u32[]{:S(2)}) collective-permute-start(bf16[256,256]{1,0:T(8,128)(2,1)S(1)} %get-tuple-element.76), channel_id=1, source_target_pairs={{0,2},{1,3},{2,0},{3,1},{4,6},{5,7},{6,4},{7,5},{8,10},{9,11},{10,... | collective-permute-start | bytes 393224 | tf_op jit(solution)/shard_map/ppermute | solution.py:600
  5.3 1.4 %weights.1 = (bf16[256,1024]{1,0:T(8,128)(2,1)S(1)}, bf16[256,1024]{1,0:T(8,128)(2,1)S(1)}, bf16[256,1024]{1,0:T(8,128)(2,1)S(1)}, bf16[128,512]{1,0:T(8,128)(2,...) custom-call(bf16[64,256]{1,0:T(8,128)(2,1)} %refs_0_.5, ...), custom_call_target="tpu_custom_call" | custom-call | flops 3900000000 | tf_op jit(solution)/shard_map/weights/pallas_call | solution.py:59
  6.7 0.8 %copy-done = bf16[128,128,128]{2,1,0:T(8,128)(2,1)S(1)} copy-done((bf16[128,128,128]{2,1,0:T(8,128)(2,1)S(1)}, bf16[128,128,128]{2,1,0:T(8,128)(2,1)}, u32[]{:S(2)}) %copy-start) | copy-done | bytes 4194328
  7.5 2.9 %pair.2 = (bf16[8,64,128]{2,1,0:T(8,128)(2,1)S(1)}, bf16[64,128]{1,0:T(8,128)(2,1)S(1)}, f32[8,64,128]{2,1,0:T(8,128)S(1)}, f32[64,128]{1,0:T(8,128)S(1)}, f32[64,128]{1,0:T(8,128)S(1)}) custom-call(bf16[128,128,128]{2,1,0:T(8,128)(2,1)S(1)} %copy-done, bf16[128,512]{1,0:T(8,128)(2,1)S(1)} %get-tuple-element.77.refs_1_, ...), custom_call_target="tpu_custom_call" | custom-call | flops 7500000256 | tf_op jit(solution)/shard_map/pair/pallas_call | solution.py:59
  10.4 0.1 collective-permute-start.3
  10.5 0.0 collective-permute-done.refs_1_
  10.6 3.2 %collective-permute-start.1 = (bf16[384,256]{1,0:T(8,128)(2,1)S(1)}, bf16[384,256]{1,0:T(8,128)(2,1)S(1)}, u32[]{:S(2)}, u32[]{:S(2)}) collective-permute-start(bf16[384,256]{1,0:T(8,128)(2,1)S(1)} %get-tuple-element.82), channel_id=1, source_target_pairs={{0,8},{1,9},{2,10},{3,11},{4,12},{5,13},{6,14},{7,15},{8,0},{9,1},... | collective-permute-start | bytes 589832 | tf_op jit(solution)/shard_map/ppermute | solution.py:600
  13.7 1.6 %collective-permute-start.9 = (bf16[384,256]{1,0:T(8,128)(2,1)S(1)}, bf16[384,256]{1,0:T(8,128)(2,1)S(1)}, u32[]{:S(2)}, u32[]{:S(2)}) collective-permute-start(bf16[384,256]{1,0:T(8,128)(2,1)S(1)} %get-tuple-element.81.refs_6_.refs_2_.refs_0_), channel_id=1, source_target_pairs={{0,4},{1,5},{2,6},{3,7},{4,0},{5,1},{6,2},{7,3},{8,12},{9,13},{10,... | collective-permute-start | bytes 589832 | tf_op jit(solution)/shard_map/ppermute | solution.py:600
  15.3 2.9 %pair.3 = (bf16[8,64,128]{2,1,0:T(8,128)(2,1)S(1)}, bf16[128,128]{1,0:T(8,128)(2,1)S(1)}, f32[8,64,128]{2,1,0:T(8,128)S(1)}, f32[64,128]{1,0:T(8,128)S(1)}, f32[64,128]{1,0:T(8,128)S(1)}) custom-call(bf16[128,128,128]{2,1,0:T(8,128)(2,1)S(1)} %copy-done, bf16[128,512]{1,0:T(8,128)(2,1)S(1)} %get-tuple-element.77.refs_1_, ...), custom_call_target="tpu_custom_call" | custom-call | flops 7500000256 | tf_op jit(solution)/shard_map/pair/pallas_call | solution.py:59
  18.3 0.1 collective-permute-start.2
  18.3 0.0 collective-permute-done.3.refs_3_.refs_2_.refs_11_
  18.3 1.2 %collective-permute-done.2.refs_2_ = bf16[128,128]{1,0:T(8,128)(2,1)S(1)} collective-permute-done((bf16[128,128]{1,0:T(8,128)(2,1)S(1)}, bf16[128,128]{1,0:T(8,128)(2,1)S(1)}, u32[]{:S(2)}, u32[]{:S(2)}) %collective-permute-start.2) | collective-permute-done | bytes 32800 | tf_op jit(solution)/shard_map/ppermute | solution.py:600
  19.5 0.1 attach.2.refs_1_.refs_10_
  19.6 1.6 %collective-permute-start.5 = (bf16[10,64,128]{2,1,0:T(8,128)(2,1)S(1)}, bf16[10,64,128]{2,1,0:T(8,128)(2,1)S(1)}, u32[]{:S(2)}, u32[]{:S(2)}) collective-permute-start(bf16[10,64,128]{2,1,0:T(8,128)(2,1)S(1)} %attach.2.refs_1_.refs_10_), channel_id=1, source_target_pairs={{0,2},{1,3},{2,0},{3,1},{4,6},{5,7},{6,4},{7,5},{8,10},{9,11},{10,... | collective-permute-start | bytes 491528 | tf_op jit(solution)/shard_map/ppermute | solution.py:600
  21.2 1.2 %collective-permute-done.1.refs_0_.refs_3_.refs_2_ = bf16[384,256]{1,0:T(8,128)(2,1)S(1)} collective-permute-done((bf16[384,256]{1,0:T(8,128)(2,1)S(1)}, bf16[384,256]{1,0:T(8,128)(2,1)S(1)}, u32[]{:S(2)}, u32[]{:S(2)}) %collective-permute-start.1) | collective-permute-done | bytes 196640 | tf_op jit(solution)/shard_map/ppermute | solution.py:600
  22.5 0.1 collective-permute-start.4
  22.5 0.5 collective-permute-start.6
  23.0 0.6 %collective-permute-start.7 = (bf16[384,256]{1,0:T(8,128)(2,1)S(1)}, bf16[384,256]{1,0:T(8,128)(2,1)S(1)}, u32[]{:S(2)}, u32[]{:S(2)}) collective-permute-start(bf16[384,256]{1,0:T(8,128)(2,1)S(1)} %get-tuple-element.96), channel_id=1, source_target_pairs={{0,4},{1,5},{2,6},{3,7},{4,0},{5,1},{6,2},{7,3},{8,12},{9,13},{10,... | collective-permute-start | bytes 589832 | tf_op jit(solution)/shard_map/ppermute | solution.py:600
  23.7 0.0 collective-permute-done.9.refs_0_.refs_2_
  23.7 0.1 collective-permute-start.10
  23.8 0.1 collective-permute-done.4.refs_1_
  23.9 0.5 prepare.4
  24.4 0.0 collective-permute-done.6.refs_1_
  24.4 0.5 prepare.5
  24.9 1.1 %collective-permute-done.5.refs_3_.refs_12_ = bf16[10,64,128]{2,1,0:T(8,128)(2,1)S(1)} collective-permute-done((bf16[10,64,128]{2,1,0:T(8,128)(2,1)S(1)}, bf16[10,64,128]{2,1,0:T(8,128)(2,1)S(1)}, u32[]{:S(2)}, u32[]{:S(2)}) %collective-permute-start.5) | collective-permute-done | bytes 163872 | tf_op jit(solution)/shard_map/ppermute | solution.py:600
  25.9 0.6 %probs.1 = (bf16[8,128,256]{2,1,0:T(8,128)(2,1)S(1)}, f32[2,128,128]{2,1,0:T(8,128)S(1)}) custom-call(bf16[8,64,128]{2,1,0:T(8,128)(2,1)S(1)} %get-tuple-element.85.refs_0_.refs_9_.refs_1_, bf16[10,64,128]{2,1,0:T(8,128)(2,1)S(1)} %attach.2.refs_1_.refs_10_, bf16[8,64,128]{2,1,0:T(8,128)(2,1)S(1)} %collective-permute-done.3.refs_3_.refs_2_.refs_11_, ...), custom_call_target="tpu_custom_call" | custom-call | tf_op jit(solution)/shard_map/probs/pallas_call | solution.py:59
  26.5 1.0 %work.4 = (f32[1,256,256]{2,1,0:T(8,128)S(1)}, bf16[1,256,256]{2,1,0:T(8,128)(2,1)S(1)}, f32[1,256,256]{2,1,0:T(8,128)S(1)}) custom-call(bf16[8,256,128]{2,1,0:T(8,128)(2,1)S(1)} %get-tuple-element.97.refs_0_.refs_4_, bf16[8,128,128]{2,1,0:T(8,128)(2,1)S(1)} %get-tuple-element.94.refs_4_.refs_1_.refs_0_, f32[1,128,1024]{2,1,0:T(8,128)S(1)} %get-tuple-element.98.refs_2_, ...), custom_call_target="tpu_custom_call" | custom-call | tf_op jit(solution)/shard_map/work/pallas_call | solution.py:59
  27.5 0.1 collective-permute-start.8
  27.6 0.0 collective-permute-done.10.refs_1_
  27.6 0.5 prepare.6
  28.1 1.0 %work.5 = (f32[1,256,256]{2,1,0:T(8,128)S(1)}, bf16[1,256,256]{2,1,0:T(8,128)(2,1)S(1)}, f32[1,256,256]{2,1,0:T(8,128)S(1)}) custom-call(bf16[8,256,128]{2,1,0:T(8,128)(2,1)S(1)} %get-tuple-element.103.refs_0_.refs_6_, bf16[8,128,128]{2,1,0:T(8,128)(2,1)S(1)} %get-tuple-element.104.refs_1_.refs_2_, f32[1,128,1024]{2,1,0:T(8,128)S(1)} %get-tuple-element.105.refs_2_, ...), custom_call_target="tpu_custom_call" | custom-call | tf_op jit(solution)/shard_map/work/pallas_call | solution.py:59
  29.1 0.0 collective-permute-done.8.refs_1_
  29.1 2.7 %collective-permute-start.15 = (bf16[384,256]{1,0:T(8,128)(2,1)S(1)}, bf16[384,256]{1,0:T(8,128)(2,1)S(1)}, u32[]{:S(2)}, u32[]{:S(2)}) collective-permute-start(bf16[384,256]{1,0:T(8,128)(2,1)S(1)} %finish.4.refs_1_), channel_id=1, source_target_pairs={{0,8},{1,9},{2,10},{3,11},{4,12},{5,13},{6,14},{7,15},{8,0},{9,1},... | collective-permute-start | bytes 589832 | tf_op jit(solution)/shard_map/ppermute | solution.py:600
  31.9 0.0 collective-permute-done.7.refs_0_.refs_2_
  31.9 0.1 collective-permute-start.13
  32.0 0.5 collective-permute-start.12
  32.5 1.0 %work.6 = (f32[1,256,256]{2,1,0:T(8,128)S(1)}, bf16[1,256,256]{2,1,0:T(8,128)(2,1)S(1)}, f32[1,256,256]{2,1,0:T(8,128)S(1)}) custom-call(bf16[8,256,128]{2,1,0:T(8,128)(2,1)S(1)} %get-tuple-element.90.refs_0_.refs_5_, bf16[8,128,128]{2,1,0:T(8,128)(2,1)S(1)} %get-tuple-element.91.refs_5_.refs_1_, f32[1,128,1024]{2,1,0:T(8,128)S(1)} %get-tuple-element.92.refs_2_, ...), custom_call_target="tpu_custom_call" | custom-call | tf_op jit(solution)/shard_map/work/pallas_call | solution.py:59
  33.4 0.1 collective-permute-start.11
  33.6 0.0 collective-permute-done.13.refs_1_
  33.6 0.7 %prepare.7 = (bf16[8,256,128]{2,1,0:T(8,128)(2,1)S(1)}, bf16[8,128,128]{2,1,0:T(8,128)(2,1)S(1)}, f32[1,128,1024]{2,1,0:T(8,128)S(1)}, f32[1,128,1024]{2,1,0:T(8,128)S(1)}) custom-call(bf16[1,256,256]{2,1,0:T(8,128)(2,1)S(1)} %pick.7.refs_8_.refs_0_, bf16[1,256,256]{2,1,0:T(8,128)(2,1)S(1)} %collective-permute-done.13.refs_1_, ...), custom_call_target="tpu_custom_call" | custom-call | tf_op jit(solution)/shard_map/prepare/pallas_call | solution.py:59
  34.2 1.8 %scores.1 = (f32[8,128,128]{2,1,0:T(8,128)S(1)}, bf16[128,128]{1,0:T(8,128)(2,1)S(1)}, bf16[6,128,128]{2,1,0:T(8,128)(2,1)S(1)}, bf16[2,128,128]{2,1,0:T(8,128)(2,1)S(1)}) custom-call(bf16[8,128,128]{2,1,0:T(8,128)(2,1)S(1)} %get-tuple-element.94.refs_4_.refs_1_.refs_0_, bf16[8,128,128]{2,1,0:T(8,128)(2,1)S(1)} %get-tuple-element.91.refs_5_.refs_1_, ...), custom_call_target="tpu_custom_call" | custom-call | tf_op jit(solution)/shard_map/scores/pallas_call | solution.py:59
  36.0 0.5 collective-permute-start.18
  36.5 1.0 %work.7 = (f32[1,256,256]{2,1,0:T(8,128)S(1)}, bf16[1,256,256]{2,1,0:T(8,128)(2,1)S(1)}, f32[1,256,256]{2,1,0:T(8,128)S(1)}) custom-call(bf16[8,256,128]{2,1,0:T(8,128)(2,1)S(1)} %get-tuple-element.113.refs_0_.refs_7_, bf16[8,128,128]{2,1,0:T(8,128)(2,1)S(1)} %get-tuple-element.114.refs_1_.refs_3_, f32[1,128,1024]{2,1,0:T(8,128)S(1)} %get-tuple-element.115.refs_2_, ...), custom_call_target="tpu_custom_call" | custom-call | tf_op jit(solution)/shard_map/work/pallas_call | solution.py:59
  37.5 0.0 collective-permute-done.12.refs_1_
  37.5 0.1 finish.6
  37.6 0.4 collective-permute-start.14
  38.0 1.5 %collective-permute-start.19 = (bf16[6,128,128]{2,1,0:T(8,128)(2,1)S(1)}, bf16[6,128,128]{2,1,0:T(8,128)(2,1)S(1)}, u32[]{:S(2)}, u32[]{:S(2)}) collective-permute-start(bf16[6,128,128]{2,1,0:T(8,128)(2,1)S(1)} %get-tuple-element.128), channel_id=1, source_target_pairs={{0,2},{1,3},{2,0},{3,1},{4,6},{5,7},{6,4},{7,5},{8,10},{9,11},{10,... | collective-permute-start | bytes 589832 | tf_op jit(solution)/shard_map/ppermute | solution.py:600
  39.5 0.1 finish.5.refs_0_
  39.5 0.0 collective-permute-done.18.refs_2_
  39.5 0.3 attach.3.refs_8_
  39.8 0.6 %collective-permute-start.20 = (bf16[288,128]{1,0:T(8,128)(2,1)S(1)}, bf16[288,128]{1,0:T(8,128)(2,1)S(1)}, u32[]{:S(2)}, u32[]{:S(2)}) collective-permute-start(bf16[288,128]{1,0:T(8,128)(2,1)S(1)} %attach.3.refs_8_), channel_id=1, source_target_pairs={{0,2},{1,3},{2,0},{3,1},{4,6},{5,7},{6,4},{7,5},{8,10},{9,11},{10,... | collective-permute-start | bytes 221192 | tf_op jit(solution)/shard_map/ppermute | solution.py:600
  40.4 1.2 %collective-permute-done.15.refs_1_.refs_2_ = bf16[384,256]{1,0:T(8,128)(2,1)S(1)} collective-permute-done((bf16[384,256]{1,0:T(8,128)(2,1)S(1)}, bf16[384,256]{1,0:T(8,128)(2,1)S(1)}, u32[]{:S(2)}, u32[]{:S(2)}) %collective-permute-start.15) | collective-permute-done | bytes 196640 | tf_op jit(solution)/shard_map/ppermute | solution.py:600
  41.6 0.1 finish.7
  41.7 2.5 %collective-permute-start.17 = (bf16[384,256]{1,0:T(8,128)(2,1)S(1)}, bf16[384,256]{1,0:T(8,128)(2,1)S(1)}, u32[]{:S(2)}, u32[]{:S(2)}) collective-permute-start(bf16[384,256]{1,0:T(8,128)(2,1)S(1)} %finish.7), channel_id=1, source_target_pairs={{0,12},{1,13},{2,14},{3,15},{4,8},{5,9},{6,10},{7,11},{8,4},{9,5},... | collective-permute-start | bytes 589832 | tf_op jit(solution)/shard_map/ppermute | solution.py:600
  44.2 2.7 %collective-permute-done.20.refs_1_.refs_10_ = bf16[288,128]{1,0:T(8,128)(2,1)S(1)} collective-permute-done((bf16[288,128]{1,0:T(8,128)(2,1)S(1)}, bf16[288,128]{1,0:T(8,128)(2,1)S(1)}, u32[]{:S(2)}, u32[]{:S(2)}) %collective-permute-start.20) | collective-permute-done | bytes 73760 | tf_op jit(solution)/shard_map/ppermute | solution.py:600
  46.9 3.3 %pair_back.2 = (bf16[128,128,128]{2,1,0:T(8,128)(2,1)}, f32[8,128]{1,0:T(8,128)S(1)}) custom-call(bf16[128,128,128]{2,1,0:T(8,128)(2,1)S(1)} %copy-done, bf16[8,64,128]{2,1,0:T(8,128)(2,1)S(1)} %get-tuple-element.85.refs_0_.refs_9_.refs_1_, f32[8,64,128]{2,1,0:T(8,128)S(1)} %get-tuple-element.120.refs_2_, f32[64,128]{1,0:T(8,128)S(1)} %get-tuple-element.121.refs_3_, ...), custom_call_target="tpu_custom_call" | custom-call | tf_op jit(solution)/shard_map/pair_back/pallas_call | solution.py:59
  50.1 0.0 collective-permute-done.14.refs_1_
  50.1 0.2 collective-permute-done.17.refs_3_
  50.4 0.1 fold.1
  50.5 1.6 %collective-permute-start.21 = (bf16[256,256]{1,0:T(8,128)(2,1)S(1)}, bf16[256,256]{1,0:T(8,128)(2,1)S(1)}, u32[]{:S(2)}, u32[]{:S(2)}) collective-permute-start(bf16[256,256]{1,0:T(8,128)(2,1)S(1)} %get-tuple-element.131), channel_id=1, source_target_pairs={{0,2},{1,3},{2,0},{3,1},{4,6},{5,7},{6,4},{7,5},{8,10},{9,11},{10,... | collective-permute-start | bytes 393224 | tf_op jit(solution)/shard_map/ppermute | solution.py:600
  52.0 3.3 %pair_back.3 = (bf16[128,128,128]{2,1,0:T(8,128)(2,1)}, f32[8,128]{1,0:T(8,128)}) custom-call(bf16[128,128,128]{2,1,0:T(8,128)(2,1)S(1)} %copy-done, bf16[8,64,128]{2,1,0:T(8,128)(2,1)S(1)} %get-tuple-element.83.refs_0_.refs_1_, f32[8,64,128]{2,1,0:T(8,128)S(1)} %get-tuple-element.134.refs_2_, ...), custom_call_target="tpu_custom_call", output_to_operand_aliasing={{0}: (12, {})} | custom-call | tf_op jit(solution)/shard_map/pair_back/pallas_call | solution.py:59
  55.3 0.2 collective-permute-done.21.refs_5_
  55.5 1.1 %last.1 = (bf16[8,64,128]{2,1,0:T(8,128)(2,1)}, bf16[8,64,128]{2,1,0:T(8,128)(2,1)}) custom-call(f32[128,512]{1,0:T(8,128)S(1)} %get-tuple-element.71.refs_0_, f32[128,512]{1,0:T(8,128)S(1)} %get-tuple-element.72.refs_1_, f32[128,512]{1,0:T(8,128)S(1)} %get-tuple-element.73.refs_2_, f32[8,128]{1,0:T(8,128)S(1)} %get-tuple-element.74.refs_3_, ...), custom_call_target="tpu_custom_call" | custom-call | tf_op jit(solution)/shard_map/last/pallas_call | solution.py:59
  (13 shorter events, 0.2 us)
Async XLA Ops:
  2.2 8.3 %collective-permute-start = (bf16[256,256]{1,0:T(8,128)(2,1)S(1)}, bf16[256,256]{1,0:T(8,128)(2,1)S(1)}, u32[]{:S(2)}, u32[]{:S(2)}) collective-permute-start(bf16[256,256]{1,0:T(8,128)(2,1)S(1)} %get-tuple-element.76), channel_id=1, source_target_pairs={{0,2},{1,3},{2,0},{3,1},{4,6},{5,7},{6,4},{7,5},{8,10},{9,11},{10,... | collective-permute-start | bytes 393224 | tf_op jit(solution)/shard_map/ppermute | solution.py:600
  5.2 2.3 %copy-start = (bf16[128,128,128]{2,1,0:T(8,128)(2,1)S(1)}, bf16[128,128,128]{2,1,0:T(8,128)(2,1)}, u32[]{:S(2)}) copy-start(bf16[128,128,128]{2,1,0:T(8,128)(2,1)} %refs_0_.9) | copy-start | bytes 12582916
  10.4 7.9 %collective-permute-start.3 = (bf16[8,64,128]{2,1,0:T(8,128)(2,1)S(1)}, bf16[8,64,128]{2,1,0:T(8,128)(2,1)S(1)}, u32[]{:S(2)}, u32[]{:S(2)}) collective-permute-start(bf16[8,64,128]{2,1,0:T(8,128)(2,1)S(1)} %get-tuple-element.85.refs_0_.refs_9_.refs_1_), channel_id=1, source_target_pairs={{0,2},{1,3},{2,0},{3,1},{4,6},{5,7},{6,4},{7,5},{8,10},{9,11},{10,... | collective-permute-start | bytes 393224 | tf_op jit(solution)/shard_map/ppermute | solution.py:600
  10.6 11.8 %collective-permute-start.1 = (bf16[384,256]{1,0:T(8,128)(2,1)S(1)}, bf16[384,256]{1,0:T(8,128)(2,1)S(1)}, u32[]{:S(2)}, u32[]{:S(2)}) collective-permute-start(bf16[384,256]{1,0:T(8,128)(2,1)S(1)} %get-tuple-element.82), channel_id=1, source_target_pairs={{0,8},{1,9},{2,10},{3,11},{4,12},{5,13},{6,14},{7,15},{8,0},{9,1},... | collective-permute-start | bytes 589832 | tf_op jit(solution)/shard_map/ppermute | solution.py:600
  13.7 9.9 %collective-permute-start.9 = (bf16[384,256]{1,0:T(8,128)(2,1)S(1)}, bf16[384,256]{1,0:T(8,128)(2,1)S(1)}, u32[]{:S(2)}, u32[]{:S(2)}) collective-permute-start(bf16[384,256]{1,0:T(8,128)(2,1)S(1)} %get-tuple-element.81.refs_6_.refs_2_.refs_0_), channel_id=1, source_target_pairs={{0,4},{1,5},{2,6},{3,7},{4,0},{5,1},{6,2},{7,3},{8,12},{9,13},{10,... | collective-permute-start | bytes 589832 | tf_op jit(solution)/shard_map/ppermute | solution.py:600
  18.3 1.3 %collective-permute-start.2 = (bf16[128,128]{1,0:T(8,128)(2,1)S(1)}, bf16[128,128]{1,0:T(8,128)(2,1)S(1)}, u32[]{:S(2)}, u32[]{:S(2)}) collective-permute-start(bf16[128,128]{1,0:T(8,128)(2,1)S(1)} %get-tuple-element.84.refs_1_), channel_id=1, source_target_pairs={{0,1},{1,0},{2,3},{3,2},{4,5},{5,4},{6,7},{7,6},{8,9},{9,8},{10,11... | collective-permute-start | bytes 98312 | tf_op jit(solution)/shard_map/ppermute | solution.py:600
  19.6 6.3 %collective-permute-start.5 = (bf16[10,64,128]{2,1,0:T(8,128)(2,1)S(1)}, bf16[10,64,128]{2,1,0:T(8,128)(2,1)S(1)}, u32[]{:S(2)}, u32[]{:S(2)}) collective-permute-start(bf16[10,64,128]{2,1,0:T(8,128)(2,1)S(1)} %attach.2.refs_1_.refs_10_), channel_id=1, source_target_pairs={{0,2},{1,3},{2,0},{3,1},{4,6},{5,7},{6,4},{7,5},{8,10},{9,11},{10,... | collective-permute-start | bytes 491528 | tf_op jit(solution)/shard_map/ppermute | solution.py:600
  22.5 1.4 %collective-permute-start.4 = (bf16[1,256,256]{2,1,0:T(8,128)(2,1)S(1)}, bf16[1,256,256]{2,1,0:T(8,128)(2,1)S(1)}, u32[]{:S(2)}, u32[]{:S(2)}) collective-permute-start(bf16[1,256,256]{2,1,0:T(8,128)(2,1)S(1)} %pick.5.refs_0_), channel_id=1, source_target_pairs={{0,1},{1,0},{2,3},{3,2},{4,5},{5,4},{6,7},{7,6},{8,9},{9,8},{10,11... | collective-permute-start | bytes 393224 | tf_op jit(solution)/shard_map/ppermute | solution.py:600
  22.5 1.8 %collective-permute-start.6 = (bf16[1,256,256]{2,1,0:T(8,128)(2,1)S(1)}, bf16[1,256,256]{2,1,0:T(8,128)(2,1)S(1)}, u32[]{:S(2)}, u32[]{:S(2)}) collective-permute-start(bf16[1,256,256]{2,1,0:T(8,128)(2,1)S(1)} %get-tuple-element.86.refs_1_.refs_0_), channel_id=1, source_target_pairs={{0,1},{1,0},{2,3},{3,2},{4,5},{5,4},{6,7},{7,6},{8,9},{9,8},{10,11... | collective-permute-start | bytes 393224 | tf_op jit(solution)/shard_map/ppermute | solution.py:600
  23.0 8.8 %collective-permute-start.7 = (bf16[384,256]{1,0:T(8,128)(2,1)S(1)}, bf16[384,256]{1,0:T(8,128)(2,1)S(1)}, u32[]{:S(2)}, u32[]{:S(2)}) collective-permute-start(bf16[384,256]{1,0:T(8,128)(2,1)S(1)} %get-tuple-element.96), channel_id=1, source_target_pairs={{0,4},{1,5},{2,6},{3,7},{4,0},{5,1},{6,2},{7,3},{8,12},{9,13},{10,... | collective-permute-start | bytes 589832 | tf_op jit(solution)/shard_map/ppermute | solution.py:600
  23.7 3.9 %collective-permute-start.10 = (bf16[1,256,256]{2,1,0:T(8,128)(2,1)S(1)}, bf16[1,256,256]{2,1,0:T(8,128)(2,1)S(1)}, u32[]{:S(2)}, u32[]{:S(2)}) collective-permute-start(bf16[1,256,256]{2,1,0:T(8,128)(2,1)S(1)} %pick.6.refs_0_), channel_id=1, source_target_pairs={{0,1},{1,0},{2,3},{3,2},{4,5},{5,4},{6,7},{7,6},{8,9},{9,8},{10,11... | collective-permute-start | bytes 393224 | tf_op jit(solution)/shard_map/ppermute | solution.py:600
  27.5 1.6 %collective-permute-start.8 = (bf16[1,256,256]{2,1,0:T(8,128)(2,1)S(1)}, bf16[1,256,256]{2,1,0:T(8,128)(2,1)S(1)}, u32[]{:S(2)}, u32[]{:S(2)}) collective-permute-start(bf16[1,256,256]{2,1,0:T(8,128)(2,1)S(1)} %get-tuple-element.101), channel_id=1, source_target_pairs={{0,1},{1,0},{2,3},{3,2},{4,5},{5,4},{6,7},{7,6},{8,9},{9,8},{10,11... | collective-permute-start | bytes 393224 | tf_op jit(solution)/shard_map/ppermute | solution.py:600
  29.1 12.4 %collective-permute-start.15 = (bf16[384,256]{1,0:T(8,128)(2,1)S(1)}, bf16[384,256]{1,0:T(8,128)(2,1)S(1)}, u32[]{:S(2)}, u32[]{:S(2)}) collective-permute-start(bf16[384,256]{1,0:T(8,128)(2,1)S(1)} %finish.4.refs_1_), channel_id=1, source_target_pairs={{0,8},{1,9},{2,10},{3,11},{4,12},{5,13},{6,14},{7,15},{8,0},{9,1},... | collective-permute-start | bytes 589832 | tf_op jit(solution)/shard_map/ppermute | solution.py:600
  31.9 1.7 %collective-permute-start.13 = (bf16[1,256,256]{2,1,0:T(8,128)(2,1)S(1)}, bf16[1,256,256]{2,1,0:T(8,128)(2,1)S(1)}, u32[]{:S(2)}, u32[]{:S(2)}) collective-permute-start(bf16[1,256,256]{2,1,0:T(8,128)(2,1)S(1)} %pick.7.refs_8_.refs_0_), channel_id=1, source_target_pairs={{0,1},{1,0},{2,3},{3,2},{4,5},{5,4},{6,7},{7,6},{8,9},{9,8},{10,11... | collective-permute-start | bytes 393224 | tf_op jit(solution)/shard_map/ppermute | solution.py:600
  32.0 5.5 %collective-permute-start.12 = (bf16[1,256,256]{2,1,0:T(8,128)(2,1)S(1)}, bf16[1,256,256]{2,1,0:T(8,128)(2,1)S(1)}, u32[]{:S(2)}, u32[]{:S(2)}) collective-permute-start(bf16[1,256,256]{2,1,0:T(8,128)(2,1)S(1)} %get-tuple-element.112), channel_id=1, source_target_pairs={{0,1},{1,0},{2,3},{3,2},{4,5},{5,4},{6,7},{7,6},{8,9},{9,8},{10,11... | collective-permute-start | bytes 393224 | tf_op jit(solution)/shard_map/ppermute | solution.py:600
  33.4 4.5 %collective-permute-start.11 = (bf16[1,256,256]{2,1,0:T(8,128)(2,1)S(1)}, bf16[1,256,256]{2,1,0:T(8,128)(2,1)S(1)}, u32[]{:S(2)}, u32[]{:S(2)}) collective-permute-start(bf16[1,256,256]{2,1,0:T(8,128)(2,1)S(1)} %get-tuple-element.109), channel_id=1, source_target_pairs={{0,1},{1,0},{2,3},{3,2},{4,5},{5,4},{6,7},{7,6},{8,9},{9,8},{10,11... | collective-permute-start | bytes 393224 | tf_op jit(solution)/shard_map/ppermute | solution.py:600
  36.0 3.5 %collective-permute-start.18 = (bf16[128,128]{1,0:T(8,128)(2,1)S(1)}, bf16[128,128]{1,0:T(8,128)(2,1)S(1)}, u32[]{:S(2)}, u32[]{:S(2)}) collective-permute-start(bf16[128,128]{1,0:T(8,128)(2,1)S(1)} %get-tuple-element.127.refs_1_), channel_id=1, source_target_pairs={{0,1},{1,0},{2,3},{3,2},{4,5},{5,4},{6,7},{7,6},{8,9},{9,8},{10,11... | collective-permute-start | bytes 98312 | tf_op jit(solution)/shard_map/ppermute | solution.py:600
  37.6 12.6 %collective-permute-start.14 = (bf16[384,256]{1,0:T(8,128)(2,1)S(1)}, bf16[384,256]{1,0:T(8,128)(2,1)S(1)}, u32[]{:S(2)}, u32[]{:S(2)}) collective-permute-start(bf16[384,256]{1,0:T(8,128)(2,1)S(1)} %finish.6), channel_id=1, source_target_pairs={{0,4},{1,5},{2,6},{3,7},{4,0},{5,1},{6,2},{7,3},{8,12},{9,13},{10,... | collective-permute-start | bytes 589832 | tf_op jit(solution)/shard_map/ppermute | solution.py:600
  38.0 3.6 %collective-permute-start.16 = (bf16[1,256,256]{2,1,0:T(8,128)(2,1)S(1)}, bf16[1,256,256]{2,1,0:T(8,128)(2,1)S(1)}, u32[]{:S(2)}, u32[]{:S(2)}) collective-permute-start(bf16[1,256,256]{2,1,0:T(8,128)(2,1)S(1)} %get-tuple-element.119), channel_id=1, source_target_pairs={{0,1},{1,0},{2,3},{3,2},{4,5},{5,4},{6,7},{7,6},{8,9},{9,8},{10,11... | collective-permute-start | bytes 393224 | tf_op jit(solution)/shard_map/ppermute | solution.py:600
  38.0 8.9 %collective-permute-start.19 = (bf16[6,128,128]{2,1,0:T(8,128)(2,1)S(1)}, bf16[6,128,128]{2,1,0:T(8,128)(2,1)S(1)}, u32[]{:S(2)}, u32[]{:S(2)}) collective-permute-start(bf16[6,128,128]{2,1,0:T(8,128)(2,1)S(1)} %get-tuple-element.128), channel_id=1, source_target_pairs={{0,2},{1,3},{2,0},{3,1},{4,6},{5,7},{6,4},{7,5},{8,10},{9,11},{10,... | collective-permute-start | bytes 589832 | tf_op jit(solution)/shard_map/ppermute | solution.py:600
  39.8 7.1 %collective-permute-start.20 = (bf16[288,128]{1,0:T(8,128)(2,1)S(1)}, bf16[288,128]{1,0:T(8,128)(2,1)S(1)}, u32[]{:S(2)}, u32[]{:S(2)}) collective-permute-start(bf16[288,128]{1,0:T(8,128)(2,1)S(1)} %attach.3.refs_8_), channel_id=1, source_target_pairs={{0,2},{1,3},{2,0},{3,1},{4,6},{5,7},{6,4},{7,5},{8,10},{9,11},{10,... | collective-permute-start | bytes 221192 | tf_op jit(solution)/shard_map/ppermute | solution.py:600
  41.7 8.7 %collective-permute-start.17 = (bf16[384,256]{1,0:T(8,128)(2,1)S(1)}, bf16[384,256]{1,0:T(8,128)(2,1)S(1)}, u32[]{:S(2)}, u32[]{:S(2)}) collective-permute-start(bf16[384,256]{1,0:T(8,128)(2,1)S(1)} %finish.7), channel_id=1, source_target_pairs={{0,12},{1,13},{2,14},{3,15},{4,8},{5,9},{6,10},{7,11},{8,4},{9,5},... | collective-permute-start | bytes 589832 | tf_op jit(solution)/shard_map/ppermute | solution.py:600
  50.5 5.0 %collective-permute-start.21 = (bf16[256,256]{1,0:T(8,128)(2,1)S(1)}, bf16[256,256]{1,0:T(8,128)(2,1)S(1)}, u32[]{:S(2)}, u32[]{:S(2)}) collective-permute-start(bf16[256,256]{1,0:T(8,128)(2,1)S(1)} %get-tuple-element.131), channel_id=1, source_target_pairs={{0,2},{1,3},{2,0},{3,1},{4,6},{5,7},{6,4},{7,5},{8,10},{9,11},{10,... | collective-permute-start | bytes 393224 | tf_op jit(solution)/shard_map/ppermute | solution.py:600
